TPU v7x, 32 devices: a whole 2x2x4 slice. The times are simulated.
32 devices in a mesh: dp: 2 (over core), blk: 8 (over z, y), tensor: 2 (over x).
Axes of the slice: x: 2, y: 2, z: 4, core: 2. Of those that a mesh axis runs over, the one named last changes fastest.
Arguments:
- tokens: bfloat16 [14, 2048, 1024], P('dp', 'blk'), may hold values from -6 to 6
- ln_gain: float32 [1024], replicated, may hold values from 0.5 to 1.5
- ln_bias: float32 [1024], replicated, may hold values from -2 to 2
- w_qkv: bfloat16 [1024, 3, 1024], P(('dp', 'blk'), None, 'tensor'), may hold values from -0.1875 to 0.1875
- b_qkv: float32 [3, 1024], P(None, 'tensor'), may hold values from -3 to 3
- w_out: bfloat16 [1024, 1024], P('tensor', ('dp', 'blk')), may hold values from -1.5 to 1.5
- w_fc: bfloat16 [1024, 4096], P(('dp', 'blk'), 'tensor'), may hold values from -0.1875 to 0.1875
- b_fc: float32 [4096], P('tensor'), may hold values from -3 to 3
- w_proj: bfloat16 [4096, 1024], P('tensor', ('dp', 'blk')), may hold values from -0.09375 to 0.09375
- b_out: float32 [1024], replicated, may hold values from -2 to 2
- bounds: int32 [14, 5], P('dp'), may hold values from 0 to 2047, as said below
- cotangent: bfloat16 [14, 2048, 1024], P('dp', 'blk'), may hold values from -6 to 6
Outputs:
- result: bfloat16 [14, 2048, 1024], P('dp', 'blk')
- grad_tokens: bfloat16 [14, 2048, 1024], P('dp', 'blk')
- grad_ln_gain: float32 [1024], replicated
- grad_ln_bias: float32 [1024], replicated
- grad_w_qkv: float32 [1024, 3, 1024], P(('dp', 'blk'), None, 'tensor')
- grad_b_qkv: float32 [3, 1024], P(None, 'tensor')
- grad_w_out: float32 [1024, 1024], P('tensor', ('dp', 'blk'))
- grad_w_fc: float32 [1024, 4096], P(('dp', 'blk'), 'tensor')
- grad_b_fc: float32 [4096], P('tensor')
- grad_w_proj: float32 [4096, 1024], P('tensor', ('dp', 'blk'))
- grad_b_out: float32 [1024], replicated
Inputs may be any that keep to these rules, and one draw needn't show every extreme that they name: `bounds`: each row lists the first positions of its 5 packed documents, strictly increasing, the first 0; a document runs to the next start or to the row's end at 2048.
All inputs are finite; a program needn't handle non-finite values.
Results may differ from a plain program's by a relative error of at most 0.015.
Values may be sent and summed in bfloat16 or wider, within the bound.
A program may use at most 256 MiB of HBM per device.

v0:
```python
import jax
import jax.numpy as jnp
from jax import lax
from jax.sharding import PartitionSpec as P

HEAD_DIM = 64
ROT_DIM = 16


epsilon = 1e-05


def layer_norm(values, gain, shift):
    center = values - jnp.mean(values, -1, keepdims=True)
    spread = jnp.mean(center * center, -1, keepdims=True)
    return center * lax.rsqrt(spread + epsilon) * gain + shift


def rotary(values, cosine, sine):
    half = ROT_DIM // 2
    rot_part = values[..., :ROT_DIM]
    turned = jnp.concatenate([-rot_part[..., half:], rot_part[..., :half]], -1)
    return jnp.concatenate([rot_part * cosine + turned * sine, values[..., ROT_DIM:]], -1)


def angles(positions):
    freqs = 10000.0 ** (-jnp.arange(0, ROT_DIM, 2, dtype=jnp.float32) / ROT_DIM)
    phase = positions[..., None] * freqs
    phase = jnp.concatenate([phase, phase], -1)[..., None, :]
    return (jnp.cos(phase), jnp.sin(phase))


def doc_starts(bounds, token_index):
    return jnp.max(
        jnp.where(bounds[:, None, :] <= token_index[None, :, None], bounds[:, None, :], 0), -1
    )


def exact_gelu(values):
    return jax.nn.gelu(values, approximate=False)


def pair_mask(query_index, query_start, key_index):
    allowed = (key_index[None, None, :] <= query_index[None, :, None]) & (
        key_index[None, None, :] >= query_start[:, :, None]
    )
    return allowed[:, None]


def local(
    tokens, ln_gain, ln_bias, w_qkv, b_qkv, w_out, w_fc, b_fc, w_proj, b_out, bounds, cotangent
):
    row_count, group_len, model_width = tokens.shape
    local_width = b_qkv.shape[1]
    head_count = local_width // HEAD_DIM
    scale = HEAD_DIM ** (-0.5)
    token_index = lax.axis_index("blk") * group_len + jnp.arange(group_len, dtype=jnp.int32)
    doc_first = doc_starts(bounds, token_index)
    cosine, sine = angles((token_index[None, :] - doc_first).astype(jnp.float32))

    def visible(key_first, key_count):
        return pair_mask(token_index, doc_first, key_first + jnp.arange(key_count, dtype=jnp.int32))

    full_qkv, full_out, full_fc, full_proj = (
        lax.all_gather(w_qkv, ("dp", "blk"), axis=0, tiled=True),
        lax.all_gather(w_out, ("dp", "blk"), axis=1, tiled=True),
        lax.all_gather(w_fc, ("dp", "blk"), axis=0, tiled=True),
        lax.all_gather(w_proj, ("dp", "blk"), axis=1, tiled=True),
    )
    inputs = tokens.astype(jnp.float32)
    hidden_f, norm_back = jax.vjp(layer_norm, inputs, ln_gain, ln_bias)
    hidden = hidden_f.astype(jnp.bfloat16)
    packed = (
        jnp.einsum("rcd,dkf->rckf", hidden, full_qkv, preferred_element_type=jnp.float32) + b_qkv
    )

    def turn(query_part, key_part):
        return (rotary(query_part, cosine, sine), rotary(key_part, cosine, sine))

    head_shape = (row_count, group_len, head_count, HEAD_DIM)
    (turned_q, turned_k), turn_back = jax.vjp(
        turn, packed[:, :, 0].reshape(head_shape), packed[:, :, 1].reshape(head_shape)
    )
    queries = turned_q.astype(jnp.bfloat16)
    keys = turned_k.reshape(row_count, group_len, local_width).astype(jnp.bfloat16)
    values = packed[:, :, 2].astype(jnp.bfloat16)

    def attend_piece(state, key_piece, value_piece, key_first):
        running_max, running_sum, running_acc = state
        key_count = key_piece.shape[1]
        key_heads = key_piece.reshape(row_count, key_count, head_count, HEAD_DIM)
        value_heads = value_piece.reshape(row_count, key_count, head_count, HEAD_DIM)
        scores = (
            jnp.einsum("rqhd,rkhd->rhqk", queries, key_heads, preferred_element_type=jnp.float32)
            * scale
        )
        allowed = visible(key_first, key_count)
        new_max = jnp.maximum(running_max, jnp.max(jnp.where(allowed, scores, -1e30), -1))
        decay = jnp.exp(running_max - new_max)
        weights = jnp.where(allowed, jnp.exp(scores - new_max[..., None]), 0.0)
        new_sum = running_sum * decay + jnp.sum(weights, -1)
        new_acc = running_acc * decay[..., None] + jnp.einsum(
            "rhqk,rkhd->rhqd",
            weights.astype(jnp.bfloat16),
            value_heads,
            preferred_element_type=jnp.float32,
        )
        return (new_max, new_sum, new_acc)

    stat_shape = (row_count, head_count, group_len)
    initial = (
        jnp.full(stat_shape, -1e30, jnp.float32),
        jnp.zeros(stat_shape, jnp.float32),
        jnp.zeros(stat_shape + (HEAD_DIM,), jnp.float32),
    )
    key_all = lax.all_gather(keys, "blk", axis=1, tiled=True)
    value_all = lax.all_gather(values, "blk", axis=1, tiled=True)
    piece_total = key_all.shape[1] // group_len

    def one_block(block_index, state):
        offset = block_index * group_len
        key_piece = lax.dynamic_slice_in_dim(key_all, offset, group_len, 1)
        value_piece = lax.dynamic_slice_in_dim(value_all, offset, group_len, 1)
        return attend_piece(state, key_piece, value_piece, offset)

    state = lax.fori_loop(0, piece_total, one_block, initial)
    row_max, row_sum, row_acc = state
    attended = row_acc / row_sum[..., None]
    log_total = row_max + jnp.log(row_sum)
    attended_rows = attended.transpose(0, 2, 1, 3)
    mixed = attended_rows.reshape(row_count, group_len, local_width).astype(jnp.bfloat16)
    inner = jnp.einsum("rcd,df->rcf", hidden, full_fc, preferred_element_type=jnp.float32) + b_fc
    activated_f, gelu_back = jax.vjp(exact_gelu, inner)
    activated = activated_f.astype(jnp.bfloat16)
    partial_sum = jnp.einsum(
        "rcf,fd->rcd", mixed, full_out, preferred_element_type=jnp.float32
    ) + jnp.einsum("rcf,fd->rcd", activated, full_proj, preferred_element_type=jnp.float32)
    branches = lax.psum(partial_sum.astype(jnp.bfloat16), "tensor").astype(jnp.float32)
    result = (inputs + branches + b_out).astype(jnp.bfloat16)
    full_qkv, full_out, full_fc, full_proj = (
        lax.all_gather(w_qkv, ("dp", "blk"), axis=0, tiled=True),
        lax.all_gather(w_out, ("dp", "blk"), axis=1, tiled=True),
        lax.all_gather(w_fc, ("dp", "blk"), axis=0, tiled=True),
        lax.all_gather(w_proj, ("dp", "blk"), axis=1, tiled=True),
    )
    grad_out = cotangent.astype(jnp.float32)
    grad_proj = jnp.einsum("rcf,rcd->fd", activated, cotangent, preferred_element_type=jnp.float32)
    grad_wout = jnp.einsum("rcf,rcd->fd", mixed, cotangent, preferred_element_type=jnp.float32)
    grad_act = jnp.einsum("rcd,fd->rcf", cotangent, full_proj, preferred_element_type=jnp.float32)
    grad_inner = gelu_back(grad_act)[0].astype(jnp.bfloat16)
    grad_bfc = jnp.sum(grad_inner.astype(jnp.float32), (0, 1))
    grad_wfc = jnp.einsum("rcd,rcf->df", hidden, grad_inner, preferred_element_type=jnp.float32)
    grad_mixed = jnp.einsum(
        "rcd,fd->rcf", cotangent, full_out, preferred_element_type=jnp.float32
    ).astype(jnp.bfloat16)
    grad_heads = grad_mixed.reshape(head_shape)
    delta = jnp.einsum("rqhd,rqhd->rhq", grad_heads.astype(jnp.float32), attended_rows)
    key_whole, value_whole = (
        lax.all_gather(keys, "blk", axis=1, tiled=True),
        lax.all_gather(values, "blk", axis=1, tiled=True),
    )

    def pair_grads(query_part, grad_part, total_part, delta_part, key_heads, value_heads, allowed):
        scores = (
            jnp.einsum("rqhd,rkhd->rhqk", query_part, key_heads, preferred_element_type=jnp.float32)
            * scale
        )
        probs = jnp.where(allowed, jnp.exp(scores - total_part[..., None]), 0.0)
        grad_probs = jnp.einsum(
            "rqhd,rkhd->rhqk", grad_part, value_heads, preferred_element_type=jnp.float32
        )
        grad_scores = (probs * (grad_probs - delta_part[..., None])).astype(jnp.bfloat16)
        return (probs, grad_scores)

    block_total = key_whole.shape[1] // group_len

    def key_step(grad_query, block_index):
        offset = block_index * group_len
        key_heads = lax.dynamic_slice_in_dim(key_whole, offset, group_len, 1).reshape(head_shape)
        value_heads = lax.dynamic_slice_in_dim(value_whole, offset, group_len, 1).reshape(
            head_shape
        )
        probs, grad_scores = pair_grads(
            queries,
            grad_heads,
            log_total,
            delta,
            key_heads,
            value_heads,
            visible(offset, group_len),
        )
        grad_value = jnp.einsum(
            "rhqk,rqhd->rkhd",
            probs.astype(jnp.bfloat16),
            grad_heads,
            preferred_element_type=jnp.float32,
        )
        grad_query = (
            grad_query
            + jnp.einsum(
                "rhqk,rkhd->rqhd", grad_scores, key_heads, preferred_element_type=jnp.float32
            )
            * scale
        )
        grad_key = (
            jnp.einsum("rhqk,rqhd->rkhd", grad_scores, queries, preferred_element_type=jnp.float32)
            * scale
        )
        term = jnp.concatenate(
            [
                grad_key.reshape(row_count, group_len, local_width),
                grad_value.reshape(row_count, group_len, local_width),
            ],
            -1,
        )
        return (grad_query, term)

    grad_query, key_terms = lax.scan(
        key_step, jnp.zeros(head_shape, jnp.float32), jnp.arange(block_total, dtype=jnp.int32)
    )
    key_grads = lax.psum_scatter(
        key_terms.astype(jnp.bfloat16), "blk", scatter_dimension=0, tiled=True
    ).astype(jnp.float32)[0]
    grad_pre_q, grad_pre_k = turn_back(
        (grad_query, key_grads[:, :, :local_width].reshape(head_shape))
    )
    grad_packed = jnp.stack(
        [
            grad_pre_q.reshape(row_count, group_len, local_width),
            grad_pre_k.reshape(row_count, group_len, local_width),
            key_grads[:, :, local_width:],
        ],
        2,
    ).astype(jnp.bfloat16)
    grad_bqkv = jnp.sum(grad_packed.astype(jnp.float32), (0, 1))
    grad_wqkv = jnp.einsum("rcd,rckf->dkf", hidden, grad_packed, preferred_element_type=jnp.float32)
    grad_hidden_part = jnp.einsum(
        "rckf,dkf->rcd", grad_packed, full_qkv, preferred_element_type=jnp.float32
    ) + jnp.einsum("rcf,df->rcd", grad_inner, full_fc, preferred_element_type=jnp.float32)
    grad_hidden = lax.psum(grad_hidden_part.astype(jnp.bfloat16), "tensor").astype(jnp.float32)
    grad_inputs, grad_gain, grad_shift = norm_back(grad_hidden)
    grad_tokens = (grad_out + grad_inputs).astype(jnp.bfloat16)
    grad_bout = jnp.sum(grad_out, (0, 1))
    sharded = (
        lax.psum_scatter(
            grad_wqkv.astype(jnp.bfloat16), ("dp", "blk"), scatter_dimension=0, tiled=True
        ).astype(jnp.float32),
        lax.psum_scatter(
            grad_wout.astype(jnp.bfloat16), ("dp", "blk"), scatter_dimension=1, tiled=True
        ).astype(jnp.float32),
        lax.psum_scatter(
            grad_wfc.astype(jnp.bfloat16), ("dp", "blk"), scatter_dimension=0, tiled=True
        ).astype(jnp.float32),
        lax.psum_scatter(
            grad_proj.astype(jnp.bfloat16), ("dp", "blk"), scatter_dimension=1, tiled=True
        ).astype(jnp.float32),
    )
    summed = lax.psum((grad_gain, grad_shift, grad_bqkv, grad_bfc, grad_bout), ("dp", "blk"))
    return (
        result,
        grad_tokens,
        summed[0],
        summed[1],
        sharded[0],
        summed[2],
        sharded[1],
        sharded[2],
        summed[3],
        sharded[3],
        summed[4],
    )


def solution(mesh):
    in_specs = (
        P("dp", "blk", None),
        P(),
        P(),
        P(("dp", "blk"), None, "tensor"),
        P(None, "tensor"),
        P("tensor", ("dp", "blk")),
        P(("dp", "blk"), "tensor"),
        P("tensor"),
        P("tensor", ("dp", "blk")),
        P(),
        P("dp", None),
        P("dp", "blk", None),
    )
    out_specs = (
        P("dp", "blk", None),
        P("dp", "blk", None),
        P(),
        P(),
        P(("dp", "blk"), None, "tensor"),
        P(None, "tensor"),
        P("tensor", ("dp", "blk")),
        P(("dp", "blk"), "tensor"),
        P("tensor"),
        P("tensor", ("dp", "blk")),
        P(),
    )
    return jax.shard_map(local, mesh=mesh, in_specs=in_specs, out_specs=out_specs, check_vma=False)
```

profile of v0, /device:TPU:28, one launch (start us, length us, event | category | flops | bytes accessed | tf_op | source)
XLA Modules:
  0.0 2225.7 jit_solution(7576682364921086609)
XLA Ops:
  15.1 39.2 %all-gather.8.cloned.1.call-done = bf16[1024,3,512]{2,0,1:T(8,128)(2,1)} async-done(((bf16[64,3,512]{2,0,1:T(8,128)(2,1)}), bf16[1024,3,512]{2,0,1:T(8,128)(2,1)}) %all-gather.8.cloned.1.call-update) | async-done | bytes 3145744 | tf_op jit(solution)/shard_map/all_gather | solution.py:65
  54.3 9.5 broadcast_add_fusion
  105.5 190.1 %all-gather.18.cloned.1.call-done = bf16[7,2048,1,512]{3,1,2,0:T(8,128)(2,1)} async-done(((bf16[7,256,1,512]{3,1,2,0:T(8,128)(2,1)}), bf16[7,2048,1,512]{3,1,2,0:T(8,128)(2,1)}) %all-gather.18.cloned.1.call-update) | async-done | bytes 14680080 | tf_op jit(solution)/shard_map/all_gather | solution.py:117
  295.7 19.4 copy.78
  315.1 183.0 %all-gather.10.cloned.1.call-done = bf16[7,2048,512]{1,2,0:T(8,128)(2,1)} async-done(((bf16[7,256,512]{1,2,0:T(8,128)(2,1)}), bf16[7,2048,512]{1,2,0:T(8,128)(2,1)}) %all-gather.10.cloned.1.call-update) | async-done | bytes 14680080 | tf_op jit(solution)/shard_map/all_gather | solution.py:116
  498.1 233.3 %while.31 = (s32[]{:T(128)}, f32[7,8,256]{2,1,0:T(8,128)S(1)}, f32[7,8,256]{2,1,0:T(8,128)S(1)}, f32[7,8,256,64]{2,3,1,0:T(8,128)}, s32[7,256]{1,0:T(8,128)S(1)}...) while((s32[]{:T(128)}, f32[7,8,256]{2,1,0:T(8,128)S(1)}, ...), condition=%wide.region_6.7_spmd.clone, body=%wide.region_3.6_spmd.clone.sunk | while | flops 983702016 | bytes 96481528 | solution.py:126
  538.4 9.1 fusion.142
  597.4 9.1 fusion.142
  736.2 484.0 %while.32 = (s32[]{:T(128)}, f32[7,256,8,64]{1,3,2,0:T(8,128)}, bf16[8,7,256,1024]{3,2,1,0:T(8,128)(2,1)}, s32[8]{0:T(128)S(1)}, bf16[7,2048,512]{1,2,0:T(8,128)...) while((s32[]{:T(128)}, f32[7,256,8,64]{1,3,2,0:T(8,128)}, ...), condition=%wide.region_9.10_spmd.clone, body=%wide.region_8.9_spmd.clone.sunk | while | flops 2398421504 | bytes 157668128 | solution.py:218
  765.5 9.7 fusion.157
  825.0 9.7 fusion.157
  885.5 9.7 fusion.157
  946.2 9.7 fusion.157
  1006.9 9.7 fusion.157
  1067.4 9.7 fusion.157
  1128.0 9.7 fusion.157
  1188.7 9.7 fusion.157
  1221.0 15.8 fusion.66
  1241.9 34.6 %multiply_convert_fusion = (bf16[7,256,2048]{2,1,0:T(8,128)(2,1)}, f32[7,256,2048]{2,1,0:T(8,128)}) fusion(f32[7,256,2048]{2,1,0:T(8,128)S(1)} %get-tuple-element.467, f32[2048]{0:T(1024)S(1)} %copy-done.25, u8[256,2048]{1,0:T(8,128)(4,1)S(1)} %get-tuple-element.374, u8[256,2048]{1,0:T(8,128)(4,1)S(1)} %get-tuple-element.373), kind=kLoop, calls=%fused_computation.58 | loop fusion | flops 260571136 | bytes 37756928 | tf_op jit(solution)/shard_map/convert_element_type | solution.py:134
  1276.5 24.6 %convert_reduce_fusion = (f32[2048]{0:T(1024)S(1)}, bf16[7,256,2048]{2,1,0:T(8,128)(2,1)}) fusion(f32[7,256,2048]{2,1,0:T(8,128)} %get-tuple-element.431, bf16[7,256,1024]{2,1,0:T(8,128)(2,1)} %param.27, bf16[2048,1024]{0,1:T(8,128)(2,1)} %all-gather.16.cloned.1.call-done, f32[7,256,2048]{2,1,0:T(8,128)} %copy-done.3, f32[2048]{0:T(1024)S(1)} %copy-done.25), kind=kOutput, calls=%fused_computation.56 | convolution fusion | flops 7578580992 | bytes 44580864 | tf_op jit(solution)/shard_map/rcd,fd->rcf/dot_general | solution.py:149
  1301.1 13.9 bitcast_convert_fusion.1
  1315.1 13.3 bitcast_convert_fusion
  1336.2 347.3 %reduce-scatter.6.cloned.1.call-done = bf16[1,7,256,1024]{3,2,1,0:T(8,128)(2,1)} async-done(((bf16[8,7,256,1024]{3,2,1,0:T(8,128)(2,1)}), bf16[1,7,256,1024]{3,2,1,0:T(8,128)(2,1)}) %reduce-scatter.6.cloned.1.call-update) | async-done | bytes 3670032 | tf_op jit(solution)/shard_map/reduce_scatter | solution.py:221
  1714.0 11.6 bitcast_convert_fusion.2
  1725.7 13.5 fusion.56
  1739.2 10.3 fusion.54
  1753.6 9.5 fusion.51
  1764.9 69.9 %reduce-scatter.14.cloned.1.call-done = bf16[2048,64]{0,1:T(8,128)(2,1)} async-done(((bf16[2048,1024]{0,1:T(8,128)(2,1)}), bf16[2048,64]{0,1:T(8,128)(2,1)}) %reduce-scatter.14.cloned.1.call-update) | async-done | bytes 262160 | tf_op jit(solution)/shard_map/reduce_scatter | solution.py:254
  1836.6 58.4 %reduce-scatter.10.cloned.1.call-done = bf16[512,64]{0,1:T(8,128)(2,1)} async-done(((bf16[512,1024]{0,1:T(8,128)(2,1)}), bf16[512,64]{0,1:T(8,128)(2,1)}) %reduce-scatter.10.cloned.1.call-update) | async-done | bytes 65552 | tf_op jit(solution)/shard_map/reduce_scatter | solution.py:248
  1899.4 65.0 %reduce-scatter.8.cloned.1.call-done = bf16[64,3,512]{2,0,1:T(8,128)(2,1)} async-done(((bf16[1024,3,512]{2,0,1:T(8,128)(2,1)}), bf16[64,3,512]{2,0,1:T(8,128)(2,1)}) %reduce-scatter.8.cloned.1.call-update) | async-done | bytes 196624 | tf_op jit(solution)/shard_map/reduce_scatter | solution.py:245
  1966.1 178.5 %all-reduce.12.cloned.1.call-done = (bf16[7,256,1024]{2,1,0:T(8,128)(2,1)}, bf16[7,256,1024]{2,1,0:T(8,128)(2,1)}) async-done(((bf16[7,256,1024]{2,1,0:T(8,128)(2,1)}, bf16[7,256,1024]{2,1,0:T(8,128)(2,1)}), (bf16[7,256,1024]{2,1,0:T(8,128)(2,1)}, bf16[7,256,1024]{2,1,0:T(8,128)(2,1)})) %all-reduce.12.cloned.1.call-update) | async-done | bytes 7340048 | tf_op jit(solution)/shard_map/psum | solution.py:138
  2160.4 58.3 %all-reduce.8 = (f32[1024]{0:T(1024)}, f32[1024]{0:T(1024)}, f32[3,512]{1,0:T(4,128)}, f32[2048]{0:T(1024)}, f32[1024]{0:T(1024)}) all-reduce(f32[1024]{0:T(1024)S(1)} %get-tuple-element.375, f32[1024]{0:T(1024)S(1)} %get-tuple-element.377, ...), channel_id=1, replica_groups=mesh['dp'=2,'blk'=8,'tensor'=2] {'dp','blk'}, use_global_device_ids=true, to_apply=%region_15.16 | all-reduce | flops 6656 | bytes 53248 | tf_op jit(solution)/shard_map/psum | solution.py:258
  (381 shorter events, 742.6 us)
Async XLA Ops:
  7.2 47.2 %copy-start.23 = (f32[1024]{0:T(1024)S(1)}, f32[1024]{0:T(1024)}, u32[]{:S(2)}) copy-start(f32[1024]{0:T(1024)} %param.17) | copy-start | bytes 12292
  7.2 47.2 %copy-start.32 = (f32[1024]{0:T(1024)S(1)}, f32[1024]{0:T(1024)}, u32[]{:S(2)}) copy-start(f32[1024]{0:T(1024)} %param.18) | copy-start | bytes 12292
  7.2 47.1 %copy-start.31 = (f32[3,512]{1,0:T(4,128)S(1)}, f32[3,512]{1,0:T(4,128)}, u32[]{:S(2)}) copy-start(f32[3,512]{1,0:T(4,128)} %param.20) | copy-start | bytes 18436
  7.2 47.1 %all-gather.8.cloned.1.call-start = ((), (), s32[]{:S(2)}) async-start(), calls=%async_computation.5 | async-start | bytes 3342336 | tf_op jit(solution)/shard_map/all_gather | solution.py:65
  7.9 87.4 %all-gather.12.cloned.1.call-start = ((), (), s32[]{:S(2)}) async-start(), calls=%async_computation.7 | async-start | bytes 1114112 | tf_op jit(solution)/shard_map/all_gather | solution.py:66
  8.7 287.0 %all-gather.18.cloned.1.call-start = ((), (), s32[]{:S(2)}) async-start(), calls=%async_computation.15 | async-start | bytes 16515072 | tf_op jit(solution)/shard_map/all_gather | solution.py:117
  11.3 52.5 %copy-start.17 = (f32[7,256]{1,0:T(8,128)}, f32[7,256]{1,0:T(8,128)S(1)}, u32[]{:S(2)}) copy-start(f32[7,256]{1,0:T(8,128)S(1)} %broadcast_multiply_fusion.1) | copy-start | bytes 21508
  15.1 48.7 %copy-start.21 = (f32[7,256]{1,0:T(8,128)}, f32[7,256]{1,0:T(8,128)S(1)}, u32[]{:S(2)}) copy-start(f32[7,256]{1,0:T(8,128)S(1)} %fusion.84) | copy-start | bytes 21508
  15.1 54.5 %copy-start.26 = (s32[7,5]{1,0:T(8,128)S(1)}, s32[7,5]{1,0:T(8,128)}, u32[]{:S(2)}) copy-start(s32[7,5]{1,0:T(8,128)} %param.26) | copy-start | bytes 424
  69.6 428.5 %all-gather.10.cloned.1.call-start = ((), (), s32[]{:S(2)}) async-start(), calls=%async_computation.6 | async-start | bytes 16515072 | tf_op jit(solution)/shard_map/all_gather | solution.py:116
  70.3 20.0 copy-start.13
  70.3 20.0 copy-start.15
  93.9 1126.4 %all-gather.14.cloned.1.call-start = ((), (), s32[]{:S(2)}) async-start(), calls=%async_computation.8 | async-start | bytes 4456448 | tf_op jit(solution)/shard_map/all_gather | solution.py:67
  94.5 1182.0 %all-gather.16.cloned.1.call-start = ((), (), s32[]{:S(2)}) async-start(), calls=%async_computation.9 | async-start | bytes 4456448 | tf_op jit(solution)/shard_map/all_gather | solution.py:68
  95.1 1588.5 %reduce-scatter.6.cloned.1.call-start = ((), (), s32[]{:S(2)}) async-start(), calls=%async_computation.10 | async-start | bytes 33030144 | tf_op jit(solution)/shard_map/reduce_scatter | solution.py:221
  509.1 9.1 copy-start.8
  538.4 9.2 copy-start.8
  567.7 9.0 copy-start.8
  597.3 9.1 copy-start.8
  1220.3 542.9 %reduce-scatter.12.cloned.1.call-start = ((), (), s32[]{:S(2)}) async-start(), calls=%async_computation.13 | async-start | bytes 4456448 | tf_op jit(solution)/shard_map/reduce_scatter | solution.py:251
  1315.0 519.9 %reduce-scatter.14.cloned.1.call-start = ((), (), s32[]{:S(2)}) async-start(), calls=%async_computation.14 | async-start | bytes 4456448 | tf_op jit(solution)/shard_map/reduce_scatter | solution.py:254
  1328.4 566.7 %reduce-scatter.10.cloned.1.call-start = ((), (), s32[]{:S(2)}) async-start(), calls=%async_computation.12 | async-start | bytes 1114112 | tf_op jit(solution)/shard_map/reduce_scatter | solution.py:248
  1336.2 628.2 %reduce-scatter.8.cloned.1.call-start = ((), (), s32[]{:S(2)}) async-start(), calls=%async_computation.11 | async-start | bytes 3342336 | tf_op jit(solution)/shard_map/reduce_scatter | solution.py:245
  1683.6 10.2 copy-start.16
  1725.6 419.0 %all-reduce.12.cloned.1.call-start = ((), (), s32[]{:S(2)}) async-start(), calls=%async_computation.16 | async-start | bytes 14680064 | tf_op jit(solution)/shard_map/psum | solution.py:138
  1725.7 13.5 copy-start.28
  1739.2 10.3 copy-start.12
  1739.2 10.3 copy-start.30
  1764.9 384.7 %copy-start.20 = (f32[7,256]{1,0:T(8,128)S(1)}, f32[7,256]{1,0:T(8,128)}, u32[]{:S(2)}) copy-start(f32[7,256]{1,0:T(8,128)} %copy-done.19) | copy-start | bytes 21508
  2144.7 9.9 copy-start.10
  2144.7 9.9 copy-start.11
  2144.7 9.9 copy-start.27
  (42 other events, 188.6 us)
Sparse Core Ops, SparseCore 0:
  10.3 44.0 all-gather.7
  56.5 36.8 all-gather.11
  95.7 199.9 all-gather.17
  297.6 200.4 all-gather.9
  500.1 49.1 all-gather.13
  551.4 49.0 all-gather.15
  1220.4 463.1 reduce-scatter.5
  1687.4 71.2 reduce-scatter.11
  1763.0 71.7 reduce-scatter.13
  1838.3 56.6 reduce-scatter.9
  1899.3 65.0 reduce-scatter.7
  1967.5 177.1 all-reduce.11
where the time goes:
time: 2240 us; the launch traced here: 2230 us
  waiting for transfers between devices  1130 us (50%)
  matrix products  569 us (25%)
  local copies, waits for them, and re-layouts  236 us (11%)
  other arithmetic  206 us (9%)
  blocking collectives  58.3 us (3%)
    reduce_scatter x1, waiting for transfers between devices, local(): lax.psum_scatter(key_terms.astype(jnp.bfloat16), 'blk', scatter_dimension...  347 us
    all_gather x1, waiting for transfers between devices, local(): value_all = lax.all_gather(values, 'blk', axis=1, tiled=True)  190 us
    all_gather x1, waiting for transfers between devices, local(): key_all = lax.all_gather(keys, 'blk', axis=1, tiled=True)  183 us
    psum x1, waiting for transfers between devices, local(): lax.psum(partial_sum.astype(jnp.bfloat16), 'tensor').astype(jnp.float32)  179 us
    dynamic_update_slice x16, local copies, waits for them, and re-layouts, local(): lax.scan(key_step, jnp.zeros(head_shape, jnp.float32), jnp.arange(block_t...  83.4 us
    dot_general x8, matrix products, key_step(): jnp.einsum('rhqk,rqhd->rkhd', probs.astype(jnp.bfloat16), grad_heads, pre...  77.9 us
    reduce_sum x8, other arithmetic, attend_piece(): new_sum = running_sum * decay + jnp.sum(weights, -1)  71.9 us
    dot_general x8, matrix products, pair_grads(): jnp.einsum('rqhd,rkhd->rhqk', query_part, key_heads, preferred_element_ty...  71.2 us
  transfers between devices with their start and end apart: 12, of which 8 were waited for; matrix products, arithmetic and copies ran while one was open for 42% of the time, Pallas kernels for 0%

commit v1 on v0

v1 whole, which is shorter than its diff:
```python
import functools
import jax
import jax.numpy as jnp
from jax import lax
from jax.experimental import pallas as pl
from jax.experimental.pallas import tpu as pltpu
from jax.sharding import PartitionSpec as P

HEAD_DIM = 64
ROT_DIM = 16
LANES = 128
BF = jnp.bfloat16
F32 = jnp.float32


def nt(a, b):
    return lax.dot_general(a, b, (((1,), (1,)), ((), ())), preferred_element_type=F32)


def nn(a, b):
    return lax.dot_general(a, b, (((1,), (0,)), ((), ())), preferred_element_type=F32)


def attn_kernel(bq, bk, q_ref, k_ref, v_ref, do_ref, c_ref, sa_ref, sb_ref, st_ref,
                o_ref, g_ref, q2, qt, ks, vx, s_buf, p_buf, dkt, dvt):
    length = q_ref.shape[0]
    nq = length // bq
    lane = lax.broadcasted_iota(jnp.int32, (1, LANES), 1)
    first = lane < HEAD_DIM
    half = ROT_DIM // 2
    c2 = HEAD_DIM ** (-0.5) * 1.4426950408889634

    def rot(u, rows):
        return (u * c_ref[rows, :] + pltpu.roll(u, LANES - half, 1) * sa_ref[rows, :]
                + pltpu.roll(u, half, 1) * sb_ref[rows, :])

    def rot_back(u, rows):
        return (u * c_ref[rows, :] + pltpu.roll(u * sb_ref[rows, :], LANES - half, 1)
                + pltpu.roll(u * sa_ref[rows, :], half, 1))

    def prep(i, _):
        rows = pl.ds(i * bq, bq)
        q = rot(q_ref[rows, :].astype(F32), rows)
        qs = (q * c2).astype(BF)
        zero = jnp.zeros_like(qs)
        q2[0, rows, :] = jnp.where(first, qs, zero)
        q2[1, rows, :] = jnp.where(first, zero, qs)
        qt[:, rows] = q.T.astype(BF)
        ks[rows, :] = rot(k_ref[rows, :].astype(F32), rows).astype(BF)
        vx[rows, :LANES] = v_ref[rows, :].astype(BF)
        vx[rows, LANES:] = jnp.ones((bq, LANES), BF)
        dkt[:, rows] = jnp.zeros((LANES, bq), F32)
        dvt[:, rows] = jnp.zeros((LANES, bq), F32)
        return 0

    lax.fori_loop(0, nq, prep, 0)

    def q_block(i, _):
        rows = pl.ds(i * bq, bq)
        nj = (i * bq) // bk + 1
        start = st_ref[rows, :]
        qidx = i * bq + lax.broadcasted_iota(jnp.int32, (bq, 1), 0)
        q_h = (q2[0, rows, :], q2[1, rows, :])

        def pass1(j, mx):
            cols = pl.ds(j * bk, bk)
            k = ks[cols, :]
            kidx = j * bk + lax.broadcasted_iota(jnp.int32, (1, bk), 1)
            ok = (kidx >= start) & (kidx <= qidx)
            out = []
            for h in range(2):
                s = jnp.where(ok, nt(q_h[h], k), -1e30)
                s_buf[h, :, cols] = s
                m = mx[h]
                for t in range(bk // LANES):
                    m = jnp.maximum(m, s[:, t * LANES:(t + 1) * LANES])
                out.append(m)
            return tuple(out)

        neg = jnp.full((bq, LANES), -1e30, F32)
        mx = lax.fori_loop(0, nj, pass1, (neg, neg))
        mx = [jnp.max(m, -1, keepdims=True) for m in mx]

        def pass2(j, acc):
            cols = pl.ds(j * bk, bk)
            v = vx[cols, :]
            out = []
            for h in range(2):
                p = jnp.exp2(s_buf[h, :, cols] - mx[h]).astype(BF)
                p_buf[h, :, cols] = p
                out.append(acc[h] + nn(p, v))
            return tuple(out)

        zero = jnp.zeros((bq, 2 * LANES), F32)
        acc = lax.fori_loop(0, nj, pass2, (zero, zero))
        inv = [1.0 / a[:, LANES:] for a in acc]
        outs = [a[:, :LANES] * r for a, r in zip(acc, inv)]
        o = jnp.where(first, outs[0], outs[1])
        o_ref[rows, :] = o.astype(BF)
        do = do_ref[rows, :].astype(F32)
        dos, dots, deltas = [], [], []
        for h in range(2):
            mine = first if h == 0 else jnp.logical_not(first)
            d = jnp.where(mine, do * inv[h], 0.0)
            db = d.astype(BF)
            dos.append(db)
            df = db.astype(F32)
            deltas.append(jnp.sum(df * o, -1, keepdims=True))
            dots.append(df.T[h * HEAD_DIM:(h + 1) * HEAD_DIM].astype(BF))
        q_t = qt[:, rows]

        def pass3(j, acc):
            cols = pl.ds(j * bk, bk)
            v = vx[cols, :LANES]
            k = ks[cols, :]
            out = []
            for h in range(2):
                part = slice(h * HEAD_DIM, (h + 1) * HEAD_DIM)
                p = p_buf[h, :, cols]
                dp = nt(dos[h], v)
                ds = (p.astype(F32) * (dp - deltas[h])).astype(BF)
                dvt[part, cols] += nn(dots[h], p)
                dkt[part, cols] += nn(q_t[part], ds)
                out.append(acc[h] + nn(ds, k))
            return tuple(out)

        zero = jnp.zeros((bq, LANES), F32)
        dq = lax.fori_loop(0, nj, pass3, (zero, zero))
        dq = jnp.where(first, dq[0], dq[1]) * HEAD_DIM ** (-0.5)
        g_ref[0, rows, :] = rot_back(dq, rows).astype(BF)
        return 0

    lax.fori_loop(0, nq, q_block, 0)

    def finish(i, _):
        rows = pl.ds(i * bq, bq)
        g_ref[1, rows, :] = rot_back(dkt[:, rows].T * HEAD_DIM ** (-0.5), rows).astype(BF)
        g_ref[2, rows, :] = dvt[:, rows].T.astype(BF)
        return 0

    lax.fori_loop(0, nq, finish, 0)


def attention(packed, do, cos, sa, sb, start, bq=512, bk=512):
    length, width = do.shape
    bq = min(bq, 2 ** 20 // length)
    bk = max(bq, min(bk, length))
    n = width // LANES
    blk = lambda off: pl.BlockSpec((length, LANES), lambda g: (0, off + g))
    full = lambda w: pl.BlockSpec((length, w), lambda g: (0, 0))
    out = jax.ShapeDtypeStruct((length, width), BF)
    return pl.pallas_call(
        functools.partial(attn_kernel, bq, bk),
        grid=(n,),
        out_shape=[out, jax.ShapeDtypeStruct((3, length, width), BF)],
        in_specs=[blk(0), blk(n), blk(2 * n), blk(0), full(LANES), full(LANES), full(LANES), full(1)],
        out_specs=[blk(0), pl.BlockSpec((3, length, LANES), lambda g: (0, 0, g))],
        scratch_shapes=[
            pltpu.VMEM((2, length, LANES), BF),
            pltpu.VMEM((LANES, length), BF),
            pltpu.VMEM((length, LANES), BF),
            pltpu.VMEM((length, 2 * LANES), BF),
            pltpu.VMEM((2, bq, length), F32),
            pltpu.VMEM((2, bq, length), BF),
            pltpu.VMEM((LANES, length), F32),
            pltpu.VMEM((LANES, length), F32),
        ],
        compiler_params=pltpu.CompilerParams(vmem_limit_bytes=50 * 1024 * 1024),
        cost_estimate=pl.CostEstimate(flops=12 * length * length * width // 2 * 4, bytes_accessed=length * width * 22, transcendentals=length * length * n),
    )(packed, packed, packed, do, cos, sa, sb, start)


EPSILON = 1e-05


def normalize(values):
    center = values - jnp.mean(values, -1, keepdims=True)
    spread = jnp.mean(center * center, -1, keepdims=True)
    scale = lax.rsqrt(spread + EPSILON)
    return center * scale, scale


def exact_gelu(values):
    return jax.nn.gelu(values, approximate=False)


def rotary_tables(position):
    half = ROT_DIM // 2
    freqs = 10000.0 ** (-jnp.arange(0, ROT_DIM, 2, dtype=F32) / ROT_DIM)
    phase = position[:, None].astype(F32) * freqs
    cosine, sine = jnp.cos(phase), jnp.sin(phase)
    length = position.shape[0]
    rest = HEAD_DIM - ROT_DIM
    zero, one = jnp.zeros((length, half), F32), jnp.ones((length, rest), F32)
    keep = jnp.concatenate([cosine, cosine, one] * 2, 1)
    ahead = jnp.concatenate([-sine, zero, 0 * one] * 2, 1)
    behind = jnp.concatenate([zero, sine, 0 * one] * 2, 1)
    return keep, ahead, behind


def swap(value):
    return lax.ppermute(value, "tensor", [(0, 1), (1, 0)])


def split_tensor(value, axis):
    shape = value.shape
    parts = lax.axis_size("tensor")
    return value.reshape(shape[:axis] + (parts, shape[axis] // parts) + shape[axis + 1:])


def own_part(value, axis):
    return lax.dynamic_index_in_dim(
        split_tensor(value, axis), lax.axis_index("tensor"), axis, keepdims=False
    )


def sum_parts(value, axis):
    parts = lax.axis_size("tensor")
    mine = lax.axis_index("tensor")
    pieces = split_tensor(value, axis)
    if parts == 2:
        other = lax.dynamic_index_in_dim(pieces, 1 - mine, axis, keepdims=False).astype(BF)
        own = lax.dynamic_index_in_dim(pieces, mine, axis, keepdims=False)
        return own.astype(F32) + swap(other).astype(F32)
    return lax.psum_scatter(
        value.astype(BF), "tensor", scatter_dimension=axis, tiled=True
    ).astype(F32)


def join_parts(value, axis):
    parts = lax.axis_size("tensor")
    if parts != 2:
        return lax.all_gather(value, "tensor", axis=axis, tiled=True)
    other = swap(value)
    first = lax.axis_index("tensor") == 0
    low, high = jnp.where(first, value, other), jnp.where(first, other, value)
    return jnp.concatenate([low, high], axis)


def to_rows(value):
    blocks = lax.axis_size("blk")
    pad = jnp.zeros((blocks - value.shape[0],) + value.shape[1:], value.dtype)
    return lax.all_to_all(jnp.concatenate([value, pad], 0), "blk", 0, 0, tiled=True)


def to_blocks(value, rows):
    return lax.all_to_all(value, "blk", 0, 0, tiled=True)[:rows]


def local(
    tokens, ln_gain, ln_bias, w_qkv, b_qkv, w_out, w_fc, b_fc, w_proj, b_out, bounds, cotangent
):
    rows, group, model = tokens.shape
    width = b_qkv.shape[1]
    blocks = lax.axis_size("blk")
    length = blocks * group

    full_out = lax.all_gather(w_out, ("dp", "blk"), axis=1, tiled=True)
    full_qkv = lax.all_gather(w_qkv, ("dp", "blk"), axis=0, tiled=True)
    full_fc = lax.all_gather(w_fc, ("dp", "blk"), axis=0, tiled=True)
    full_proj = lax.all_gather(w_proj, ("dp", "blk"), axis=1, tiled=True)

    hidden = (normalize(tokens.astype(F32))[0] * ln_gain + ln_bias).astype(BF)

    row_hidden = join_parts(to_rows(own_part(hidden, 1)), 1).reshape(length, model)
    row_bounds = lax.dynamic_index_in_dim(
        bounds, jnp.minimum(lax.axis_index("blk"), rows - 1), 0, keepdims=False
    )
    index = jnp.arange(length, dtype=jnp.int32)
    start = jnp.max(jnp.where(row_bounds[None] <= index[:, None], row_bounds[None], 0), -1)
    tables = rotary_tables(index - start)
    packed = (
        jnp.dot(row_hidden, full_qkv.reshape(model, 3 * width), preferred_element_type=F32)
        + b_qkv.reshape(-1)
    )
    grad_mixed = jnp.einsum("rcd,fd->rcf", cotangent, full_out, preferred_element_type=F32).astype(BF)
    row_grad = to_rows(grad_mixed).reshape(length, width)
    attended, grad_packed = attention(packed, row_grad, *tables, start[:, None])
    mixed = to_blocks(attended.reshape(blocks, group, width), rows)
    grad_bqkv = jnp.sum(grad_packed.astype(F32), 1)
    grad_wqkv = jnp.einsum("ld,clf->dcf", row_hidden, grad_packed, preferred_element_type=F32)
    row_back = jnp.einsum("clf,dcf->ld", grad_packed, full_qkv, preferred_element_type=F32)
    back = sum_parts(row_back.reshape(blocks, group, model), 1).astype(BF)
    back = to_blocks(back, rows).astype(F32)

    inner = jnp.einsum("rcd,df->rcf", hidden, full_fc, preferred_element_type=F32) + b_fc
    activated_f, gelu_back = jax.vjp(exact_gelu, inner)
    activated = activated_f.astype(BF)
    partial = jnp.einsum("rcf,fd->rcd", mixed, full_out, preferred_element_type=F32) + jnp.einsum(
        "rcf,fd->rcd", activated, full_proj, preferred_element_type=F32
    )
    own_tokens = own_part(tokens, 1).astype(F32)
    result = join_parts((sum_parts(partial, 1) + own_tokens + b_out).astype(BF), 1)

    grad_proj = jnp.einsum("rcf,rcd->fd", activated, cotangent, preferred_element_type=F32)
    grad_wout = jnp.einsum("rcf,rcd->fd", mixed, cotangent, preferred_element_type=F32)
    grad_act = jnp.einsum("rcd,fd->rcf", cotangent, full_proj, preferred_element_type=F32)
    grad_inner = gelu_back(grad_act)[0].astype(BF)
    grad_bfc = jnp.sum(grad_inner.astype(F32), (0, 1))
    grad_wfc = jnp.einsum("rcd,rcf->df", hidden, grad_inner, preferred_element_type=F32)
    mlp_back = jnp.einsum("rcf,df->rcd", grad_inner, full_fc, preferred_element_type=F32)
    grad_hidden = sum_parts(mlp_back, 1) + back

    normal, scale = normalize(own_tokens)
    own_cot = own_part(cotangent, 1).astype(F32)
    grad_gain = jnp.sum(grad_hidden * normal, (0, 1))
    grad_shift = jnp.sum(grad_hidden, (0, 1))
    grad_normal = grad_hidden * ln_gain
    grad_inputs = scale * (
        grad_normal
        - jnp.mean(grad_normal, -1, keepdims=True)
        - normal * jnp.mean(grad_normal * normal, -1, keepdims=True)
    )
    grad_tokens = join_parts((own_cot + grad_inputs).astype(BF), 1)
    grad_bout = jnp.sum(own_cot, (0, 1))

    def scatter(value, axis):
        return lax.psum_scatter(
            value.astype(BF), ("dp", "blk"), scatter_dimension=axis, tiled=True
        ).astype(F32)

    out_wqkv, out_wout = scatter(grad_wqkv, 0), scatter(grad_wout, 1)
    out_wfc, out_proj = scatter(grad_wfc, 0), scatter(grad_proj, 1)
    grad_gain, grad_shift, grad_bout = lax.psum(
        (grad_gain, grad_shift, grad_bout), ("dp", "blk", "tensor")
    )
    grad_bqkv, grad_bfc = lax.psum((grad_bqkv, grad_bfc), ("dp", "blk"))
    return (
        result,
        grad_tokens,
        grad_gain,
        grad_shift,
        out_wqkv,
        grad_bqkv,
        out_wout,
        out_wfc,
        grad_bfc,
        out_proj,
        grad_bout,
    )


def solution(mesh):
    in_specs = (
        P("dp", "blk", None),
        P(),
        P(),
        P(("dp", "blk"), None, "tensor"),
        P(None, "tensor"),
        P("tensor", ("dp", "blk")),
        P(("dp", "blk"), "tensor"),
        P("tensor"),
        P("tensor", ("dp", "blk")),
        P(),
        P("dp", None),
        P("dp", "blk", None),
    )
    out_specs = (
        P("dp", "blk", None),
        P("dp", "blk", None),
        P(),
        P(),
        P(("dp", "blk"), None, "tensor"),
        P(None, "tensor"),
        P("tensor", ("dp", "blk")),
        P(("dp", "blk"), "tensor"),
        P("tensor"),
        P("tensor", ("dp", "blk")),
        P(),
    )
    return jax.shard_map(local, mesh=mesh, in_specs=in_specs, out_specs=out_specs, check_vma=False)
```

time: 2240 us -> 700 us (0.31)
  waiting for transfers between devices: 1130 us -> 77.4 us
  matrix products: 569 us -> 134 us
  local copies, waits for them, and re-layouts: 236 us -> 55.8 us
  Pallas kernels: 0 us -> 133 us
  other arithmetic: 206 us -> 82.4 us
  blocking collectives: 58.3 us -> 168 us
  starting transfers between devices: 0.65 us -> 26.3 us
    reduce_scatter x5 -> x4, waiting for transfers between devices: 541 us -> 0.01 us  [scatter(): lax.psum_scatter(value.astype(BF), ('dp', 'blk'), scatter_dimension=axis,...]
    dot_general x68 -> x12, matrix products: 569 us -> 134 us  [the longest x1 24.3 us: local(): jnp.einsum('rcd,fd->rcf', cotangent, full_proj, preferred_element_type=F32)]
    all_gather x6 -> x4, waiting for transfers between devices: 412 us -> 0.04 us  [the longest x1 0.02 us: local(): full_out = lax.all_gather(w_out, ('dp', 'blk'), axis=1, tiled=True)]
    psum x1 -> x0, waiting for transfers between devices: 179 us -> none  [local(): lax.psum(partial_sum.astype(jnp.bfloat16), 'tensor').astype(jnp.float32)]
    pallas_call x0 -> x1, Pallas kernels: none -> 133 us  [attention(): pl.pallas_call(functools.partial(attn_kernel, bq, bk), grid=(n,), out_sha...]
    dynamic_update_slice x16 -> x0, local copies, waits for them, and re-layouts: 83.4 us -> none  [local(): lax.scan(key_step, jnp.zeros(head_shape, jnp.float32), jnp.arange(block_t...]
    reduce_sum x14 -> x7, other arithmetic: 95.7 us -> 13.3 us  [the longest x1 5.26 us: local(): grad_gain = jnp.sum(grad_hidden * normal, (0, 1))]
    all_to_all x0 -> x1, blocking collectives: none -> 62.3 us  [to_rows(): lax.all_to_all(jnp.concatenate([value, pad], 0), 'blk', 0, 0, tiled=True)]
  transfers between devices with their start and end apart: 12 -> 17, of which waited for: 8 -> 5; matrix products, arithmetic and copies ran while one was open for 42% -> 38% of each run, Pallas kernels for 0% -> 19%
where the time goes in v1:
time: 700 us; the launch traced here: 692 us
  blocking collectives  168 us (24%)
  matrix products  134 us (19%)
  Pallas kernels  133 us (19%)
  other arithmetic  82.4 us (12%)
  waiting for transfers between devices  77.4 us (11%)
  local copies, waits for them, and re-layouts  55.8 us (8%)
  starting transfers between devices  26.3 us (4%)
  between operations  15.1 us (2%)
    pallas_call x1, Pallas kernels, attention(): pl.pallas_call(functools.partial(attn_kernel, bq, bk), grid=(n,), out_sha...  133 us
    all_to_all x1, blocking collectives, to_rows(): lax.all_to_all(jnp.concatenate([value, pad], 0), 'blk', 0, 0, tiled=True)  62.3 us
    psum x1, blocking collectives, local(): grad_bqkv, grad_bfc = lax.psum((grad_bqkv, grad_bfc), ('dp', 'blk'))  59.1 us
    ppermute x6, waiting for transfers between devices, swap(): return lax.ppermute(value, 'tensor', [(0, 1), (1, 0)])  48.6 us
    psum x1, blocking collectives, local(): lax.psum((grad_gain, grad_shift, grad_bout), ('dp', 'blk', 'tensor'))  47 us
    convert_element_type x1, other arithmetic, local(): activated = activated_f.astype(BF)  34.7 us
    all_to_all x2, waiting for transfers between devices, to_blocks(): return lax.all_to_all(value, 'blk', 0, 0, tiled=True)[:rows]  26.6 us
    dot_general x1, matrix products, local(): jnp.einsum('rcd,fd->rcf', cotangent, full_proj, preferred_element_type=F32)  24.3 us
  transfers between devices with their start and end apart: 17, of which 5 were waited for; matrix products, arithmetic and copies ran while one was open for 38% of the time, Pallas kernels for 19%

profile of v1, /device:TPU:28, one launch (start us, length us, event | category | flops | bytes accessed | tf_op | source)
XLA Modules:
  0.0 692.5 jit_solution(13385400684181831665)
XLA Ops:
  23.3 62.3 %all_to_all.20 = bf16[8,128,1024]{1,2,0:T(8,128)(2,1)} all-to-all(bf16[8,128,1024]{1,2,0:T(8,128)(2,1)S(1)} %concatenate.24), channel_id=1, replica_groups=mesh['dp'=2,'blk'=8,'tensor'=2] {'blk'}, dimensions={0} | all-to-all | bytes 4194304 | tf_op jit(solution)/shard_map/all_to_all | solution.py:243
  87.3 4.4 convolution_convert_fusion.1
  93.3 7.0 %all-to-all-start.1 = ((bf16[8,256,512]{2,1,0:T(8,128)(2,1)}), bf16[8,256,512]{2,1,0:T(8,128)(2,1)}, u32[]{:S(2)}, u32[]{:S(2)}) async-start(bf16[8,256,512]{2,1,0:T(8,128)(2,1)} %concatenate.26), calls=%async_computation.1 | async-start | bytes 4194304 | tf_op jit(solution)/shard_map/all_to_all | solution.py:243
  101.8 5.7 multiply_sine_fusion
  116.9 5.2 concatenate.27.c_ref
  122.0 10.9 %collective-permute-done = bf16[8,128,1024]{1,2,0:T(8,128)(2,1)} collective-permute-done((bf16[8,128,1024]{1,2,0:T(8,128)(2,1)}, bf16[8,128,1024]{1,2,0:T(8,128)(2,1)}, u32[]{:S(2)}, u32[]{:S(2)}) %collective-permute-start) | collective-permute-done | bytes 2097184 | tf_op jit(solution)/shard_map/ppermute | solution.py:202
  137.7 4.4 copy.63
  142.1 7.4 %reshape.119 = bf16[2048,1024,1]{0,1,2:T(8,128)(2,1)} reshape(bf16[8,256,1024]{1,0,2:T(8,128)(2,1)} %copy.63) | data formatting | bytes 8388608 | tf_op jit(solution)/shard_map/reshape | solution.py:265
  149.5 4.7 copy.82
  154.2 4.6 copy.64
  158.8 12.6 %convolution_add_fusion.q_ref.k_ref.v_ref = f32[2048,1536]{1,0:T(8,128)} fusion(bf16[2048,1024]{0,1:T(8,128)(2,1)} %bitcast.147, bf16[1024,1536]{0,1:T(8,128)(2,1)} %bitcast.152, f32[1536]{0:T(1024)S(1)} %add.125), kind=kOutput, calls=%fused_computation.27 | convolution fusion | flops 6445596672 | bytes 19929088 | tf_op jit(solution)/shard_map/dot_general | solution.py:273
  171.4 133.2 %shard_map.203 = (bf16[2048,512]{1,0:T(8,128)(2,1)}, bf16[3,2048,512]{2,1,0:T(8,128)(2,1)}) custom-call(f32[2048,1536]{1,0:T(8,128)} %convolution_add_fusion.q_ref.k_ref.v_ref, f32[2048,1536]{1,0:T(8,128)} %convolution_add_fusion.q_ref.k_ref.v_ref, f32[2048,1536]{1,0:T(8,128)} %convolution_add_fusion.q_ref.k_ref.v_ref, bf16[2048,512]{1,0:T(8,128)(2,1)} %bitcast.4.do_ref, ...), custom_call_target="tpu_custom_call" | custom-call | flops 51539607552 | bytes 23068672 | tf_op jit(solution)/shard_map/pallas_call | solution.py:152
  304.6 6.0 all-to-all-start.2
  310.6 11.1 %convolution_convert_fusion = bf16[1024,3,512]{2,0,1:T(8,128)(2,1)} fusion(bf16[2048,1024,1]{0,1,2:T(8,128)(2,1)} %reshape.119, bf16[3,2048,512]{2,1,0:T(8,128)(2,1)} %get-tuple-element.14), kind=kOutput, calls=%fused_computation.76 | convolution fusion | flops 6444023808 | bytes 13631488 | tf_op jit(solution)/shard_map/ld,clf->dcf/dot_general | solution.py:281
  321.8 16.2 %fusion.38 = (u8[256,2048]{1,0:T(8,128)(4,1)S(1)}, u8[256,2048]{1,0:T(8,128)(4,1)S(1)}, f32[7,256,2048]{2,1,0:T(8,128)S(1)}) fusion(f32[2048]{0:T(1024)S(1)} %copy-done.15, bf16[7,256,1024]{2,1,0:T(8,128)(2,1)} %copy-done.9, bf16[1024,2048]{1,0:T(8,128)(2,1)} %all-gather.9.cloned.1.call-done), kind=kOutput, calls=%fused_computation.73 | convolution fusion | flops 7566524416 | bytes 23601152 | tf_op jit(solution)/shard_map/rcd,df->rcf/dot_general | solution.py:286
  338.0 5.3 copy-done.8
  343.3 34.7 %multiply_convert_fusion = (bf16[7,256,2048]{2,1,0:T(8,128)(2,1)}, f32[7,256,2048]{2,1,0:T(8,128)}) fusion(f32[7,256,2048]{2,1,0:T(8,128)S(1)} %get-tuple-element.42, f32[2048]{0:T(1024)S(1)} %copy-done.15, u8[256,2048]{1,0:T(8,128)(4,1)S(1)} %get-tuple-element.16, u8[256,2048]{1,0:T(8,128)(4,1)S(1)} %get-tuple-element.15), kind=kLoop, calls=%fused_computation.9 | loop fusion | flops 260571136 | bytes 37756928 | tf_op jit(solution)/shard_map/convert_element_type | solution.py:288
  378.0 24.3 %convert_reduce_fusion = (f32[2048]{0:T(1024)S(1)}, bf16[7,256,2048]{2,1,0:T(8,128)(2,1)}) fusion(f32[7,256,2048]{2,1,0:T(8,128)} %get-tuple-element.28, bf16[7,256,1024]{2,1,0:T(8,128)(2,1)} %param.23, bf16[2048,1024]{0,1:T(8,128)(2,1)} %all-gather.11.cloned.1.call-done, f32[7,256,2048]{2,1,0:T(8,128)} %copy-done.8, f32[2048]{0:T(1024)S(1)} %copy-done.15), kind=kOutput, calls=%fused_computation.7 | convolution fusion | flops 7578580992 | bytes 44580864 | tf_op jit(solution)/shard_map/rcd,fd->rcf/dot_general | solution.py:297
  402.4 5.1 bitcast_convert_fusion.5
  407.5 12.8 %bitcast_convert_fusion.1 = bf16[1024,2048]{1,0:T(8,128)(2,1)} fusion(bf16[7,256,1024]{2,1,0:T(8,128)(2,1)} %copy-done.9, bf16[7,256,2048]{2,1,0:T(8,128)(2,1)} %get-tuple-element.44), kind=kOutput, calls=%fused_computation.29 | convolution fusion | flops 7518289920 | bytes 15204352 | tf_op jit(solution)/shard_map/rcd,rcf->df/dot_general | solution.py:300
  420.4 10.0 %fusion.49 = f32[2048,1024,1]{1,0,2:T(8,128)S(1)} fusion(bf16[3,2048,512]{2,1,0:T(8,128)(2,1)} %get-tuple-element.14, bf16[1024,3,512]{2,0,1:T(8,128)(2,1)} %all-gather.5.cloned.1.call-done), kind=kOutput, calls=%fused_computation.107 | convolution fusion | flops 6442450944 | bytes 17825792 | tf_op jit(solution)/shard_map/clf,dcf->ld/dot_general | solution.py:282
  432.3 10.1 %fusion.23 = f32[7,256,1024]{2,1,0:T(8,128)S(1)} fusion(bf16[7,256,2048]{2,1,0:T(8,128)(2,1)} %get-tuple-element.44, bf16[1024,2048]{1,0:T(8,128)(2,1)S(1)} %copy-done.19), kind=kOutput, calls=%fused_computation.52 | convolution fusion | flops 7516192768 | bytes 18874368 | tf_op jit(solution)/shard_map/rcf,df->rcd/dot_general | solution.py:301
  447.4 32.0 %collective-permute-done.4 = bf16[8,128,1024]{2,1,0:T(8,128)(2,1)S(1)} collective-permute-done((bf16[8,128,1024]{2,1,0:T(8,128)(2,1)S(1)}, bf16[8,128,1024]{2,1,0:T(8,128)(2,1)S(1)}, u32[]{:S(2)}, u32[]{:S(2)}) %collective-permute-start.4) | collective-permute-done | bytes 2097184 | tf_op jit(solution)/shard_map/ppermute | solution.py:202
  481.6 6.0 all-to-all-start.3
  487.6 13.6 %bitcast_convert_fusion = bf16[2048,1024]{0,1:T(8,128)(2,1)} fusion(bf16[7,256,2048]{2,1,0:T(8,128)(2,1)} %get-tuple-element.27, bf16[7,256,1024]{2,1,0:T(8,128)(2,1)} %param.23), kind=kOutput, calls=%fused_computation.28 | convolution fusion | flops 7518289920 | bytes 15204352 | tf_op jit(solution)/shard_map/rcf,rcd->fd/dot_general | solution.py:295
  501.2 11.4 %fusion.21 = f32[7,256,1024]{2,1,0:T(8,128)S(1)} fusion(bf16[7,256,2048]{2,1,0:T(8,128)(2,1)} %get-tuple-element.27, bf16[2048,1024]{0,1:T(8,128)(2,1)} %all-gather.11.cloned.1.call-done), kind=kOutput, calls=%fused_computation.50 | convolution fusion | flops 7516192768 | bytes 18874368 | tf_op jit(solution)/shard_map/rcf,fd->rcd/dot_general | solution.py:289
  518.8 26.6 %all-to-all-done.3 = bf16[8,128,1024]{2,1,0:T(8,128)(2,1)} async-done(((bf16[8,128,1024]{2,1,0:T(8,128)(2,1)}), bf16[8,128,1024]{2,1,0:T(8,128)(2,1)}, u32[]{:S(2)}, u32[]{:S(2)}) %all-to-all-start.3) | async-done | bytes 2097184 | tf_op jit(solution)/shard_map/all_to_all | solution.py:247
  545.4 5.3 fusion.32
  550.7 4.8 collective-permute-done.1
  555.6 4.9 fusion.31
  563.7 59.1 %all-reduce.3 = (f32[3,512]{1,0:T(4,128)}, f32[2048]{0:T(1024)}) all-reduce(f32[3,512]{1,0:T(4,128)S(1)} %convert_reduce_fusion.1, f32[2048]{0:T(1024)S(1)} %get-tuple-element.43), channel_id=1, replica_groups=mesh['dp'=2,'blk'=8,'tensor'=2] {'dp','blk'}, use_global_device_ids=true, to_apply=%region_13.14 | all-reduce | flops 3584 | bytes 28672 | tf_op jit(solution)/shard_map/psum | solution.py:327
  626.1 47.0 %all-reduce.2 = (f32[1024]{0:T(1024)}, f32[1024]{0:T(1024)}, f32[1024]{0:T(1024)}) all-reduce(f32[1024]{0:T(1024)S(1)} %get-tuple-element.17, f32[1024]{0:T(1024)S(1)} %get-tuple-element.20, f32[1024]{0:T(1024)S(1)} %convert_reduce_fusion.3), channel_id=1, replica_groups=mesh['dp'=2,'blk'=8,'tensor'=2] {'dp','blk','tensor'}, use_global_device_ids=true, to_apply=%region_8.9 | all-reduce | flops 3072 | bytes 24576 | tf_op jit(solution)/shard_map/psum | solution.py:324
  (121 shorter events, 68.8 us)
Async XLA Ops:
  7.2 79.9 %copy-start = (s32[7,5]{1,0:T(8,128)S(1)}, s32[7,5]{1,0:T(8,128)}, u32[]{:S(2)}) copy-start(s32[7,5]{1,0:T(8,128)} %param.22) | copy-start | bytes 424
  7.2 8.2 %copy-start.13 = (f32[1024]{0:T(1024)S(1)}, f32[1024]{0:T(1024)}, u32[]{:S(2)}) copy-start(f32[1024]{0:T(1024)} %param.13) | copy-start | bytes 12292
  7.2 8.2 %copy-start.17 = (f32[1024]{0:T(1024)S(1)}, f32[1024]{0:T(1024)}, u32[]{:S(2)}) copy-start(f32[1024]{0:T(1024)} %param.14) | copy-start | bytes 12292
  7.2 80.0 %all-gather.7.cloned.1.call-start = ((), (), s32[]{:S(2)}) async-start(), calls=%async_computation.9 | async-start | bytes 1114112 | tf_op jit(solution)/shard_map/all_gather | solution.py:258
  8.0 146.3 %all-gather.5.cloned.1.call-start = ((), (), s32[]{:S(2)}) async-start(), calls=%async_computation.8 | async-start | bytes 3342336 | tf_op jit(solution)/shard_map/all_gather | solution.py:259
  8.7 313.1 %all-gather.9.cloned.1.call-start = ((), (), s32[]{:S(2)}) async-start(), calls=%async_computation.10 | async-start | bytes 4456448 | tf_op jit(solution)/shard_map/all_gather | solution.py:260
  9.4 368.6 %all-gather.11.cloned.1.call-start = ((), (), s32[]{:S(2)}) async-start(), calls=%async_computation.11 | async-start | bytes 4456448 | tf_op jit(solution)/shard_map/all_gather | solution.py:261
  85.6 47.3 %collective-permute-start = (bf16[8,128,1024]{1,2,0:T(8,128)(2,1)}, bf16[8,128,1024]{1,2,0:T(8,128)(2,1)}, u32[]{:S(2)}, u32[]{:S(2)}) collective-permute-start(bf16[8,128,1024]{1,2,0:T(8,128)(2,1)} %all_to_all.20), channel_id=1, source_target_pairs={{0,1},{1,0},{2,3},{3,2},{4,5},{5,4},{6,7},{7,6},{8,9},{9,8},{10,11... | collective-permute-start | bytes 6291464 | tf_op jit(solution)/shard_map/ppermute | solution.py:202
  91.7 8.6 %copy-start.16 = (f32[3,512]{1,0:T(4,128)S(1)}, f32[3,512]{1,0:T(4,128)}, u32[]{:S(2)}) copy-start(f32[3,512]{1,0:T(4,128)} %param.16) | copy-start | bytes 18436
  93.3 78.1 %all-to-all-start.1 = ((bf16[8,256,512]{2,1,0:T(8,128)(2,1)}), bf16[8,256,512]{2,1,0:T(8,128)(2,1)}, u32[]{:S(2)}, u32[]{:S(2)}) async-start(bf16[8,256,512]{2,1,0:T(8,128)(2,1)} %concatenate.26), calls=%async_computation.1 | async-start | bytes 4194304 | tf_op jit(solution)/shard_map/all_to_all | solution.py:243
  304.6 97.8 %all-to-all-start.2 = ((bf16[8,256,512]{2,1,0:T(8,128)(2,1)}), bf16[8,256,512]{2,1,0:T(8,128)(2,1)S(1)}, u32[]{:S(2)}, u32[]{:S(2)}) async-start(bf16[8,256,512]{2,1,0:T(8,128)(2,1)} %bitcast.153), calls=%async_computation.2 | async-start | bytes 4194304 | tf_op jit(solution)/shard_map/all_to_all | solution.py:247
  310.6 312.3 %reduce-scatter.5.cloned.1.call-start = ((), (), s32[]{:S(2)}) async-start(), calls=%async_computation.12 | async-start | bytes 3342336 | tf_op jit(solution)/shard_map/reduce_scatter | solution.py:318
  310.6 11.2 %copy-start.15 = (f32[2048]{0:T(1024)S(1)}, f32[2048]{0:T(1024)}, u32[]{:S(2)}) copy-start(f32[2048]{0:T(1024)} %param.19) | copy-start | bytes 24580
  321.7 302.8 %reduce-scatter.7.cloned.1.call-start = ((), (), s32[]{:S(2)}) async-start(), calls=%async_computation.13 | async-start | bytes 1114112 | tf_op jit(solution)/shard_map/reduce_scatter | solution.py:318
  407.5 274.1 %reduce-scatter.9.cloned.1.call-start = ((), (), s32[]{:S(2)}) async-start(), calls=%async_computation.14 | async-start | bytes 4456448 | tf_op jit(solution)/shard_map/reduce_scatter | solution.py:318
  420.4 11.9 %copy-start.19 = (bf16[1024,2048]{1,0:T(8,128)(2,1)S(1)}, bf16[1024,2048]{1,0:T(8,128)(2,1)}, u32[]{:S(2)}) copy-start(bf16[1024,2048]{1,0:T(8,128)(2,1)} %all-gather.9.cloned.1.call-done) | copy-start | bytes 12582916
  430.8 48.6 %collective-permute-start.4 = (bf16[8,128,1024]{2,1,0:T(8,128)(2,1)S(1)}, bf16[8,128,1024]{2,1,0:T(8,128)(2,1)S(1)}, u32[]{:S(2)}, u32[]{:S(2)}) collective-permute-start(bf16[8,128,1024]{2,1,0:T(8,128)(2,1)S(1)} %fusion.39), channel_id=1, source_target_pairs={{0,1},{1,0},{2,3},{3,2},{4,5},{5,4},{6,7},{7,6},{8,9},{9,8},{10,11... | collective-permute-start | bytes 6291464 | tf_op jit(solution)/shard_map/ppermute | solution.py:202
  446.9 71.9 %collective-permute-start.3 = (bf16[7,128,1024]{2,1,0:T(8,128)(2,1)}, bf16[7,128,1024]{2,1,0:T(8,128)(2,1)}, u32[]{:S(2)}, u32[]{:S(2)}) collective-permute-start(bf16[7,128,1024]{2,1,0:T(8,128)(2,1)} %fusion.41), channel_id=1, source_target_pairs={{0,1},{1,0},{2,3},{3,2},{4,5},{5,4},{6,7},{7,6},{8,9},{9,8},{10,11... | collective-permute-start | bytes 5505032 | tf_op jit(solution)/shard_map/ppermute | solution.py:202
  481.6 63.9 %all-to-all-start.3 = ((bf16[8,128,1024]{2,1,0:T(8,128)(2,1)}), bf16[8,128,1024]{2,1,0:T(8,128)(2,1)}, u32[]{:S(2)}, u32[]{:S(2)}) async-start(bf16[8,128,1024]{2,1,0:T(8,128)(2,1)} %fusion.19), calls=%async_computation.3 | async-start | bytes 4194304 | tf_op jit(solution)/shard_map/all_to_all | solution.py:247
  487.5 195.8 %reduce-scatter.11.cloned.1.call-start = ((), (), s32[]{:S(2)}) async-start(), calls=%async_computation.15 | async-start | bytes 4456448 | tf_op jit(solution)/shard_map/reduce_scatter | solution.py:318
  501.2 11.4 %copy-start.12 = (bf16[512,1024]{0,1:T(8,128)(2,1)S(1)}, bf16[512,1024]{0,1:T(8,128)(2,1)}, u32[]{:S(2)}) copy-start(bf16[512,1024]{0,1:T(8,128)(2,1)} %all-gather.7.cloned.1.call-done) | copy-start | bytes 3145732
  514.9 30.5 %copy-start.14 = (f32[1024]{0:T(1024)S(1)}, f32[1024]{0:T(1024)}, u32[]{:S(2)}) copy-start(f32[1024]{0:T(1024)} %param.13) | copy-start | bytes 12292
  515.2 40.3 %collective-permute-start.1 = (bf16[7,128,1024]{2,1,0:T(8,128)(2,1)S(1)}, bf16[7,128,1024]{2,1,0:T(8,128)(2,1)}, u32[]{:S(2)}, u32[]{:S(2)}) collective-permute-start(bf16[7,128,1024]{2,1,0:T(8,128)(2,1)S(1)} %fusion.40), channel_id=1, source_target_pairs={{0,1},{1,0},{2,3},{3,2},{4,5},{5,4},{6,7},{7,6},{8,9},{9,8},{10,11... | collective-permute-start | bytes 5505032 | tf_op jit(solution)/shard_map/ppermute | solution.py:202
  517.9 37.6 %copy-start.18 = (f32[1024]{0:T(1024)S(1)}, f32[1024]{0:T(1024)}, u32[]{:S(2)}) copy-start(f32[1024]{0:T(1024)} %param.21) | copy-start | bytes 12292
  545.4 10.1 %copy-start.4 = (bf16[7,256,1024]{2,1,0:T(8,128)(2,1)S(1)}, bf16[7,256,1024]{2,1,0:T(8,128)(2,1)}, u32[]{:S(2)}) copy-start(bf16[7,256,1024]{2,1,0:T(8,128)(2,1)} %param.12) | copy-start | bytes 11010052
  545.4 10.1 %copy-start.7 = (f32[7,256,1024]{2,1,0:T(8,128)S(1)}, f32[7,256,1024]{2,1,0:T(8,128)}, u32[]{:S(2)}) copy-start(f32[7,256,1024]{2,1,0:T(8,128)} %copy-done.6) | copy-start | bytes 22020100
  545.4 17.4 %slice-start = ((s8[6291456]{0:T(1024)(128)(4,1)}), s8[4194304]{0:T(1024)(128)(4,1)S(1)}, s32[]{:S(2)}) async-start(s8[6291456]{0:T(1024)(128)(4,1)} %bitcast.143), calls=%async_computation.16 | async-start | bytes 8388608
  555.5 7.0 %copy-start.11 = (bf16[7,256,1024]{2,1,0:T(8,128)(2,1)S(1)}, bf16[7,256,1024]{2,1,0:T(8,128)(2,1)}, u32[]{:S(2)}) copy-start(bf16[7,256,1024]{2,1,0:T(8,128)(2,1)} %param.23) | copy-start | bytes 11010052
  555.5 7.3 %slice-start.1 = ((s8[6291456]{0:T(1024)(128)(4,1)}), s8[2097152]{0:T(1024)(128)(4,1)S(1)}, s32[]{:S(2)}) async-start(s8[6291456]{0:T(1024)(128)(4,1)} %bitcast.143), calls=%async_computation.17 | async-start | bytes 4194304
  560.5 112.6 %collective-permute-start.5 = (bf16[7,128,1024]{2,1,0:T(8,128)(2,1)}, bf16[7,128,1024]{2,1,0:T(8,128)(2,1)}, u32[]{:S(2)}, u32[]{:S(2)}) collective-permute-start(bf16[7,128,1024]{2,1,0:T(8,128)(2,1)} %get-tuple-element.35), channel_id=1, source_target_pairs={{0,1},{1,0},{2,3},{3,2},{4,5},{5,4},{6,7},{7,6},{8,9},{9,8},{10,11... | collective-permute-start | bytes 5505032 | tf_op jit(solution)/shard_map/ppermute | solution.py:202
  561.9 115.7 %collective-permute-start.2 = (bf16[7,128,1024]{2,1,0:T(8,128)(2,1)S(1)}, bf16[7,128,1024]{2,1,0:T(8,128)(2,1)}, u32[]{:S(2)}, u32[]{:S(2)}) collective-permute-start(bf16[7,128,1024]{2,1,0:T(8,128)(2,1)S(1)} %get-tuple-element.36), channel_id=1, source_target_pairs={{0,1},{1,0},{2,3},{3,2},{4,5},{5,4},{6,7},{7,6},{8,9},{9,8},{10,11... | collective-permute-start | bytes 5505032 | tf_op jit(solution)/shard_map/ppermute | solution.py:202
  677.6 7.6 %copy-start.1 = (s32[7,5]{1,0:T(8,128)S(1)}, s32[7,5]{1,0:T(8,128)}, u32[]{:S(2)}) copy-start(s32[7,5]{1,0:T(8,128)} %param.22) | copy-start | bytes 424
  (7 other events, 27.1 us)
Sparse Core Ops, SparseCore 0:
  10.3 41.5 all-gather.6
  54.1 58.6 all-gather.4
  115.0 61.6 all-gather.8
  178.8 49.0 all-gather.10
  321.9 65.0 reduce-scatter.4
  407.6 56.3 reduce-scatter.6
  468.4 90.2 reduce-scatter.8
  562.5 72.3 reduce-scatter.10

commit v2 on v1

v2 whole, which is shorter than its diff:
```python
import functools

import jax
import jax.numpy as jnp
from jax import lax
from jax.experimental import pallas as pl
from jax.experimental.pallas import tpu as pltpu
from jax.sharding import PartitionSpec as P

HEAD_DIM = 64
ROT_DIM = 16
LANES = 128
EPSILON = 1e-05
BF = jnp.bfloat16
F32 = jnp.float32
MIB = 1024 * 1024


def nt(a, b):
    return lax.dot_general(a, b, (((1,), (1,)), ((), ())), preferred_element_type=F32)


def nn(a, b):
    return lax.dot_general(a, b, (((1,), (0,)), ((), ())), preferred_element_type=F32)


def attn_kernel(bq, bk, part, waits, lo_ref, hi_ref, *refs):
    count = 2 if part else 1
    hidden, refs = refs[:count], refs[count + waits:]
    w_ref, bias_ref, do_ref, cos_ref, sin_ref, start_ref, o_ref = refs[:7]
    grads, refs = refs[7:7 + count], refs[7 + count:]
    (q2, qt, ks, vx, s_buf, p_buf, d_buf, dkt, dvt, keep, ahead, behind, starts) = refs
    length = do_ref.shape[0]
    nq = length // bq
    lane = lax.broadcasted_iota(jnp.int32, (1, LANES), 1)
    first = lane < HEAD_DIM
    half = ROT_DIM // 2
    to_score = HEAD_DIM ** (-0.5) * 1.4426950408889634
    mine_first = lax.axis_index("tensor") == 0 if part else None

    def load(base, size):
        if part:
            rows = []
            for n in range(size // (2 * part)):
                at = pl.ds(pl.multiple_of(base // 2 + n * part, part), part)
                a, b = hidden[0][at, :], hidden[1][at, :]
                rows += [jnp.where(mine_first, a, b), jnp.where(mine_first, b, a)]
            rows = jnp.concatenate(rows, 0)
        else:
            rows = hidden[0][pl.ds(base, size), :]
        packed = nn(rows, w_ref[...]) + bias_ref[...]
        return [packed[:, n * LANES:(n + 1) * LANES] for n in range(3)]

    def store(base, which, value):
        cols = slice(which * LANES, (which + 1) * LANES)
        size = value.shape[0]
        if not part:
            grads[0][pl.ds(base, size), cols] = value.astype(BF)
            return
        for n in range(size // (2 * part)):
            at = pl.ds(pl.multiple_of(base // 2 + n * part, part), part)
            a = value[2 * n * part:(2 * n + 1) * part]
            b = value[(2 * n + 1) * part:(2 * n + 2) * part]
            grads[0][at, cols] = jnp.where(mine_first, a, b).astype(BF)
            grads[1][at, cols] = jnp.where(mine_first, b, a).astype(BF)

    def rot(u, rows):
        return (u * keep[rows, :] + pltpu.roll(u, LANES - half, 1) * ahead[rows, :]
                + pltpu.roll(u, half, 1) * behind[rows, :])

    def rot_back(u, rows):
        return (u * keep[rows, :] + pltpu.roll(u * behind[rows, :], LANES - half, 1)
                + pltpu.roll(u * ahead[rows, :], half, 1))

    def tables(i, _):
        rows = pl.ds(pl.multiple_of(i * bq, bq), bq)
        c, s = cos_ref[:, rows], sin_ref[:, rows]
        rest = HEAD_DIM - ROT_DIM
        one, zero, gap = jnp.ones((rest, bq), F32), jnp.zeros((rest, bq), F32), jnp.zeros((half, bq), F32)
        keep[rows, :] = jnp.concatenate([c, c, one] * 2, 0).T
        ahead[rows, :] = jnp.concatenate([-s, gap, zero] * 2, 0).T
        behind[rows, :] = jnp.concatenate([gap, s, zero] * 2, 0).T
        starts[rows, :] = jnp.broadcast_to(start_ref[:, rows], (LANES, bq)).T
        return 0

    @pl.when(pl.program_id(0) == 0)
    def _():
        lax.fori_loop(0, nq, tables, 0)

    def prep(i, _):
        base = pl.multiple_of(i * bq, bq)
        rows = pl.ds(base, bq)
        q, k, v = load(base, bq)
        q = rot(q, rows)
        qs = (q * to_score).astype(BF)
        zero = jnp.zeros_like(qs)
        q2[0, rows, :] = jnp.where(first, qs, zero)
        q2[1, rows, :] = jnp.where(first, zero, qs)
        qt[:, rows] = q.T.astype(BF)
        ks[rows, :] = rot(k, rows).astype(BF)
        vx[rows, :LANES] = v.astype(BF)
        vx[rows, LANES:] = jnp.ones((bq, LANES), BF)
        dkt[:, rows] = jnp.zeros((LANES, bq), F32)
        dvt[:, rows] = jnp.zeros((LANES, bq), F32)
        return 0

    lax.fori_loop(0, nq, prep, 0)

    def q_block(i, _):
        rows = pl.ds(pl.multiple_of(i * bq, bq), bq)
        last = (i * bq) // bk
        least = lo_ref[i] // bk
        masked = jnp.clip((hi_ref[i] + bk - 1) // bk, least, last)
        q_h = (q2[0, rows, :], q2[1, rows, :])
        start = starts[rows, :]

        def scores(j, mx, mode):
            cols = pl.ds(pl.multiple_of(j * bk, bk), bk)
            k = ks[cols, :]
            out = []
            for h in range(2):
                s = nt(q_h[h], k)
                m = mx[h]
                for t in range(bk // LANES):
                    piece = s[:, t * LANES:(t + 1) * LANES]
                    if mode:
                        kidx = (j * bk + t * LANES + lane).astype(F32)
                        ok = kidx >= start
                        if mode == 2:
                            qidx = (i * bq + lax.broadcasted_iota(jnp.int32, (bq, 1), 0)).astype(F32)
                            ok = ok & (kidx <= qidx)
                        piece = jnp.where(ok, piece, -1e30)
                    s_buf[h, :, pl.ds(pl.multiple_of(j * bk + t * LANES, LANES), LANES)] = piece
                    m = jnp.maximum(m, piece)
                out.append(m)
            return tuple(out)

        mx = (jnp.full((bq, LANES), -1e30, F32),) * 2
        mx = lax.fori_loop(least, masked, lambda j, m: scores(j, m, 1), mx)
        mx = lax.fori_loop(masked, last, lambda j, m: scores(j, m, 0), mx)
        mx = scores(last, mx, 2)
        mx = [jnp.max(m, -1, keepdims=True) for m in mx]

        def weigh(j, acc):
            cols = pl.ds(pl.multiple_of(j * bk, bk), bk)
            v = vx[cols, :]
            out = []
            for h in range(2):
                p = jnp.exp2(s_buf[h, :, cols] - mx[h]).astype(BF)
                p_buf[h, :, cols] = p
                out.append(acc[h] + nn(p, v))
            return tuple(out)

        acc = (jnp.zeros((bq, 2 * LANES), F32),) * 2
        acc = lax.fori_loop(least, last + 1, weigh, acc)
        inv = [1.0 / a[:, LANES:] for a in acc]
        outs = [a[:, :LANES] * r for a, r in zip(acc, inv)]
        o = jnp.where(first, outs[0], outs[1])
        o_ref[rows, :] = o.astype(BF)
        do = do_ref[rows, :].astype(F32)
        dos, dots, deltas = [], [], []
        for h in range(2):
            mine = first if h == 0 else jnp.logical_not(first)
            d = jnp.where(mine, do * inv[h], 0.0).astype(BF)
            dos.append(d)
            df = d.astype(F32)
            deltas.append(jnp.sum(df * o, -1, keepdims=True))
            dots.append(df.T[h * HEAD_DIM:(h + 1) * HEAD_DIM].astype(BF))
        q_t = qt[:, rows]

        def back(j, acc):
            cols = pl.ds(pl.multiple_of(j * bk, bk), bk)
            v = vx[cols, :LANES]
            k = ks[cols, :]
            out = []
            for h in range(2):
                rows_h = slice(h * HEAD_DIM, (h + 1) * HEAD_DIM)
                p = p_buf[h, :, cols]
                dp = nt(dos[h], v)
                ds = (p.astype(F32) * (dp - deltas[h])).astype(BF)
                dvt[rows_h, cols] += nn(dots[h], p)
                dkt[rows_h, cols] += nn(q_t[rows_h], ds)
                out.append(acc[h] + nn(ds, k))
            return tuple(out)

        acc = (jnp.zeros((bq, LANES), F32),) * 2
        acc = lax.fori_loop(least, last + 1, back, acc)
        dq = jnp.where(first, acc[0], acc[1]) * HEAD_DIM ** (-0.5)
        store(i * bq, 0, rot_back(dq, rows))
        return 0

    def static_block(i):
        rows = slice(i * bq, (i + 1) * bq)
        width = (i + 1) * bq
        start = starts[rows, :]
        q_h = (q2[0, rows, :], q2[1, rows, :])
        mx = []
        for h in range(2):
            m = jnp.full((bq, LANES), -1e30, F32)
            for j in range(0, width, bk):
                s = nt(q_h[h], ks[j:j + bk, :])
                for t in range(0, bk, LANES):
                    kidx = (j + t + lane).astype(F32)
                    ok = kidx >= start
                    if j + t + LANES > i * bq:
                        qidx = (i * bq + lax.broadcasted_iota(jnp.int32, (bq, 1), 0)).astype(F32)
                        ok = ok & (kidx <= qidx)
                    piece = jnp.where(ok, s[:, t:t + LANES], -1e30)
                    s_buf[h, :, j + t:j + t + LANES] = piece
                    m = jnp.maximum(m, piece)
            mx.append(jnp.broadcast_to(jnp.max(m, -1, keepdims=True), (bq, LANES)))
        acc = []
        for h in range(2):
            for t in range(0, width, LANES):
                p_buf[h, :, t:t + LANES] = jnp.exp2(s_buf[h, :, t:t + LANES] - mx[h]).astype(BF)
            acc.append(nn(p_buf[h, :, :width], vx[:width, :]))
        inv = [1.0 / v[:, LANES:] for v in acc]
        outs = [v[:, :LANES] * r for v, r in zip(acc, inv)]
        o = jnp.where(first, outs[0], outs[1])
        o_ref[rows, :] = o.astype(BF)
        do = do_ref[rows, :].astype(F32)
        dq = []
        for h in range(2):
            mine = first if h == 0 else jnp.logical_not(first)
            rows_h = slice(h * HEAD_DIM, (h + 1) * HEAD_DIM)
            d = jnp.where(mine, do * inv[h], 0.0).astype(BF)
            df = d.astype(F32)
            delta = jnp.broadcast_to(jnp.sum(df * o, -1, keepdims=True), (bq, LANES))
            d_t = df.T[rows_h].astype(BF)
            q_t = qt[rows_h, rows]
            for j in range(0, width, bk):
                cols = slice(j, j + bk)
                dp = nt(d, vx[cols, :LANES])
                dvt[rows_h, cols] += nn(d_t, p_buf[h, :, cols])
                for t in range(0, bk, LANES):
                    at = slice(j + t, j + t + LANES)
                    d_buf[h, :, at] = (p_buf[h, :, at].astype(F32) * (dp[:, t:t + LANES] - delta)).astype(BF)
                dkt[rows_h, cols] += nn(q_t, d_buf[h, :, cols])
            dq.append(nn(d_buf[h, :, :width], ks[:width, :]))
        dq = jnp.where(first, dq[0], dq[1]) * HEAD_DIM ** (-0.5)
        store(i * bq, 0, rot_back(dq, rows))

    if nq <= 4:
        for i in range(nq):
            static_block(i)
    else:
        lax.fori_loop(0, nq, q_block, 0)

    def finish(i, _):
        base = pl.multiple_of(i * bq, bq)
        rows = pl.ds(base, bq)
        store(base, 1, rot_back(dkt[:, rows].T * HEAD_DIM ** (-0.5), rows))
        store(base, 2, dvt[:, rows].T)
        return 0

    lax.fori_loop(0, nq, finish, 0)


def attention(hidden, weights, bias, first_pair, do, position, start, part=0, waits=(), bq=512, bk=512):
    length, width = do.shape
    bq = min(bq, 2 ** 20 // length)
    bk = max(bq, min(bk, length))
    pairs = width // LANES
    freqs = 10000.0 ** (-jnp.arange(0, ROT_DIM, 2, dtype=F32) / ROT_DIM)
    phase = position.astype(F32)[None] * freqs[:, None]
    by_block = start.reshape(length // bq, bq)
    rows, model = hidden[0].shape
    once = pl.Buffered(1)
    columns = pl.BlockSpec((length, LANES), lambda g, *_: (0, g))
    triple = pl.BlockSpec((rows, 3 * LANES), lambda g, *_: (0, g))
    whole = lambda n: pl.BlockSpec((n, length), lambda g, *_: (0, 0), pipeline_mode=once)
    tri_out = jax.ShapeDtypeStruct((rows, 3 * width), BF)
    static = length // bq <= 4
    out = pl.pallas_call(
        functools.partial(attn_kernel, bq, bk, part, len(waits)),
        out_shape=[jax.ShapeDtypeStruct((length, width), BF)] + [tri_out] * len(hidden),
        grid_spec=pltpu.PrefetchScalarGridSpec(
            num_scalar_prefetch=2,
            grid=(pairs,),
            in_specs=[pl.BlockSpec((rows, model), lambda g, *_: (0, 0), pipeline_mode=once)] * len(hidden)
            + [pl.BlockSpec(memory_space=pl.ANY)] * len(waits)
            + [
                pl.BlockSpec((model, 3 * LANES), lambda g, *_: (0, first_pair + g)),
                pl.BlockSpec((1, 3 * LANES), lambda g, *_: (0, first_pair + g)),
                columns, whole(ROT_DIM // 2), whole(ROT_DIM // 2), whole(1),
            ],
            out_specs=[columns] + [triple] * len(hidden),
            scratch_shapes=[
                pltpu.VMEM((2, length, LANES), BF),
                pltpu.VMEM((LANES, length), BF),
                pltpu.VMEM((length, LANES), BF),
                pltpu.VMEM((length, 2 * LANES), BF),
                pltpu.VMEM((2, bq, length), F32),
                pltpu.VMEM((2, bq, length), BF),
                pltpu.VMEM((2, bq, length) if static else (8, LANES), BF),
                pltpu.VMEM((LANES, length), F32),
                pltpu.VMEM((LANES, length), F32),
            ] + [pltpu.VMEM((length, LANES), F32)] * 4,
        ),
        compiler_params=pltpu.CompilerParams(vmem_limit_bytes=56 * MIB),
        cost_estimate=pl.CostEstimate(flops=1000, bytes_accessed=1000, transcendentals=0),
    )(by_block.min(1), by_block.max(1), *hidden, *waits, weights, bias, do, jnp.cos(phase), jnp.sin(phase),
      start.astype(F32)[None])
    return out[0], list(out[1:])


def gather_kernel(x_ref, out_ref, local_sem, recv, up, down, across, over):
    size = x_ref.shape[0]
    core, block = lax.axis_index("dp"), lax.axis_index("blk")
    z, y = block // 2, lax.rem(block, 2)
    depth = lax.axis_size("blk") // 2
    above, below = {"blk": block + 2}, {"blk": block - 2}
    beside, sibling = {"blk": block + 1 - 2 * y}, {"dp": 1 - core}

    def place(c, zz, yy):
        return (c * depth + zz) * 2 + yy

    def chunk(at):
        return out_ref.at[pl.ds(pl.multiple_of(at * size, size), size)]

    def copy(src, at, sem, target):
        return pltpu.make_async_remote_copy(
            src_ref=src, dst_ref=chunk(at), send_sem=sem, recv_sem=recv.at[at],
            device_id=target, device_id_type=pl.DeviceIdType.MESH,
        )

    def arrived(at):
        copy(chunk(at), at, local_sem, sibling).wait_recv()

    barrier = pltpu.get_barrier_semaphore()

    def greet(target):
        pl.semaphore_signal(barrier, inc=1, device_id=target, device_id_type=pl.DeviceIdType.MESH)

    def not_top(action):
        pl.when(z < depth - 1)(action)

    def not_bottom(action):
        pl.when(z > 0)(action)

    not_top(lambda: greet(above))
    not_bottom(lambda: greet(below))
    greet(beside)
    greet(sibling)
    pl.semaphore_wait(barrier, 2 + jnp.where(z > 0, 1, 0) + jnp.where(z < depth - 1, 1, 0))

    mine = place(core, z, y)
    keep = pltpu.make_async_copy(x_ref, chunk(mine), local_sem)
    not_top(lambda: copy(x_ref, mine, up.at[z], above).start())
    not_bottom(lambda: copy(x_ref, mine, down.at[z], below).start())
    copy(x_ref, mine, across.at[z], beside).start()
    copy(x_ref, mine, over.at[z * 2 + y], sibling).start()
    keep.start()

    def from_beside(zz):
        at = place(core, zz, 1 - y)
        arrived(at)
        copy(chunk(at), at, over.at[zz * 2 + 1 - y], sibling).start()

    def from_line(zz, onward, sems, target):
        at = place(core, zz, y)
        arrived(at)
        onward(lambda: copy(chunk(at), at, sems.at[zz], target).start())
        copy(chunk(at), at, across.at[zz], beside).start()
        copy(chunk(at), at, over.at[zz * 2 + y], sibling).start()

    for step in range(1, depth):
        pl.when(z >= step)(lambda: from_line(z - step, not_top, up, above))
        pl.when(z + step < depth)(lambda: from_line(z + step, not_bottom, down, below))
    from_beside(z)
    for step in range(1, depth):
        pl.when(z >= step)(lambda: from_beside(z - step))
        pl.when(z + step < depth)(lambda: from_beside(z + step))

    keep.wait()
    for zz in range(depth):
        for yy in range(2):
            arrived(place(1 - core, zz, yy))
            copy(x_ref, mine, over.at[zz * 2 + yy], sibling).wait_send()
        copy(x_ref, mine, across.at[zz], beside).wait_send()
        pl.when((zz <= z) & (z < depth - 1))(lambda: copy(x_ref, mine, up.at[zz], above).wait_send())
        pl.when((zz >= z) & (z > 0))(lambda: copy(x_ref, mine, down.at[zz], below).wait_send())


def gather_weights(shard):
    cores, blocks = lax.axis_size("dp"), lax.axis_size("blk")
    if (cores, blocks) != (2, 8):
        return lax.all_gather(shard, ("dp", "blk"), axis=0, tiled=True)
    rows, columns = shard.shape
    dma = pltpu.SemaphoreType.DMA
    return pl.pallas_call(
        gather_kernel,
        out_shape=jax.ShapeDtypeStruct((cores * blocks * rows, columns), shard.dtype),
        in_specs=[pl.BlockSpec(memory_space=pl.ANY)],
        out_specs=pl.BlockSpec(memory_space=pl.ANY),
        scratch_shapes=[
            dma, dma((cores * blocks,)), dma((blocks // 2,)), dma((blocks // 2,)),
            dma((blocks // 2,)), dma((blocks,)),
        ],
        compiler_params=pltpu.CompilerParams(collective_id=0, has_side_effects=True),
    )(shard)


def weight_grad_kernel(half, waits, a_ref, b_ref, *refs):
    x_ref, y_ref, out_ref, turned = refs[waits:]
    step = pl.program_id(0)

    @pl.when(step == 0)
    def _():
        turned[...] = a_ref[...].T

    @pl.when(step == half)
    def _():
        turned[...] = b_ref[...].T

    @pl.when(step < half)
    def _():
        out_ref[...] = nn(turned[...], x_ref[...]).astype(BF)

    @pl.when(step >= half)
    def _():
        out_ref[...] = nn(turned[...], y_ref[...]).astype(BF)


def weight_grads(a, x, b, y, waits=(), tile=512):
    count, model = a.shape
    inner = x.shape[1]
    tile = min(tile, inner)
    half = inner // tile
    whole = pl.BlockSpec((count, model), lambda i: (0, 0), pipeline_mode=pl.Buffered(1))
    return pl.pallas_call(
        functools.partial(weight_grad_kernel, half, len(waits)),
        grid=(2 * half,),
        out_shape=jax.ShapeDtypeStruct((model, 2 * inner), BF),
        in_specs=[
            whole, whole, *[pl.BlockSpec(memory_space=pl.ANY)] * len(waits),
            pl.BlockSpec((count, tile), lambda i: (0, jnp.minimum(i, half - 1))),
            pl.BlockSpec((count, tile), lambda i: (0, jnp.maximum(i - half, 0))),
        ],
        out_specs=pl.BlockSpec((model, tile), lambda i: (0, i)),
        scratch_shapes=[pltpu.VMEM((model, count), BF)],
        compiler_params=pltpu.CompilerParams(vmem_limit_bytes=48 * MIB),
        cost_estimate=pl.CostEstimate(flops=1000, bytes_accessed=1000, transcendentals=0),
    )(a, b, *waits, x, y)


def back_kernel(waits, g_ref, w_ref, *refs):
    out_ref = refs[waits]
    out_ref[...] = nt(g_ref[...], w_ref[...]).astype(BF)


def input_grad(grad, weights, waits=(), size=256):
    count, depth = grad.shape
    model = weights.shape[0]
    return pl.pallas_call(
        functools.partial(back_kernel, len(waits)),
        grid=(count // size,),
        out_shape=jax.ShapeDtypeStruct((count, model), BF),
        in_specs=[
            pl.BlockSpec((size, depth), lambda i: (i, 0)),
            pl.BlockSpec((model, depth), lambda i: (0, 0), pipeline_mode=pl.Buffered(1)),
            *[pl.BlockSpec(memory_space=pl.ANY)] * len(waits),
        ],
        out_specs=pl.BlockSpec((size, model), lambda i: (i, 0)),
        compiler_params=pltpu.CompilerParams(vmem_limit_bytes=32 * MIB),
        cost_estimate=pl.CostEstimate(flops=1000, bytes_accessed=1000, transcendentals=0),
    )(grad, weights, *waits)


def mlp_kernel(tile, waits, hid_ref, cot_ref, wf_ref, wp_ref, bias_ref, *refs):
    act_ref, gin_ref, res_ref, back_ref, gb_ref = refs[waits:]
    hid, cot = hid_ref[...], cot_ref[...]

    @pl.when(pl.program_id(0) == 0)
    def _():
        gb_ref[...] = jnp.zeros_like(gb_ref)

    res = back = None
    for n in range(wf_ref.shape[1] // tile):
        cols = slice(n * tile, (n + 1) * tile)
        wf, wp = wf_ref[:, cols], wp_ref[:, cols]
        inner = nn(hid, wf) + bias_ref[:, cols]
        grad_act = nn(cot, wp)
        size = jnp.abs(inner)
        t = 1.0 / (1.0 + (0.3275911 * 0.7071067811865476) * size)
        bell = jnp.exp2((-0.5 * 1.4426950408889634) * inner * inner)
        tail = ((((0.5 * 1.061405429 * t - 0.5 * 1.453152027) * t + 0.5 * 1.421413741) * t
                 - 0.5 * 0.284496736) * t + 0.5 * 0.254829592) * t * bell
        below = jnp.where(inner < 0, tail, 1.0 - tail)
        act = (inner * below).astype(BF)
        grad_inner = (grad_act * (below + inner * (bell * 0.3989422804014327))).astype(BF)
        act_ref[:, cols] = act
        gin_ref[:, cols] = grad_inner
        gb_ref[:, cols] += jnp.sum(grad_inner.astype(F32), 0, keepdims=True)
        r, b = nt(act, wp), nt(grad_inner, wf)
        res, back = (r, b) if res is None else (res + r, back + b)
    res_ref[...] = res.astype(BF)
    back_ref[...] = back.astype(BF)


def mlp(hidden, cot, weights, first_block, bias, waits=(), size=256, tile=512):
    count, model = hidden.shape
    inner = bias.shape[1]
    tile = min(tile, inner)
    rows = lambda n: pl.BlockSpec((size, n), lambda i: (i, 0))
    matrix = lambda n: pl.BlockSpec((model, inner), lambda i: (0, first_block + n), pipeline_mode=pl.Buffered(1))
    vector = pl.BlockSpec((1, inner), lambda i: (0, 0))
    shape = lambda n: jax.ShapeDtypeStruct((count, n), BF)
    return pl.pallas_call(
        functools.partial(mlp_kernel, tile, len(waits)),
        grid=(count // size,),
        out_shape=[shape(inner), shape(inner), shape(model), shape(model), jax.ShapeDtypeStruct((1, inner), F32)],
        in_specs=[rows(model), rows(model), matrix(0), matrix(1), vector]
        + [pl.BlockSpec(memory_space=pl.ANY)] * len(waits),
        out_specs=[rows(inner), rows(inner), rows(model), rows(model), vector],
        compiler_params=pltpu.CompilerParams(vmem_limit_bytes=56 * MIB),
        cost_estimate=pl.CostEstimate(flops=1000, bytes_accessed=1000, transcendentals=0),
    )(hidden, cot, weights, weights, bias, *waits)


def normalize(values):
    center = values - jnp.mean(values, -1, keepdims=True)
    spread = jnp.mean(center * center, -1, keepdims=True)
    scale = lax.rsqrt(spread + EPSILON)
    return center * scale, scale


def swap(value):
    return lax.ppermute(value, "tensor", [(0, 1), (1, 0)])


def split_tensor(value, axis):
    shape = value.shape
    parts = lax.axis_size("tensor")
    return value.reshape(shape[:axis] + (parts, shape[axis] // parts) + shape[axis + 1:])


def part_of(value, axis, which):
    return lax.dynamic_index_in_dim(split_tensor(value, axis), which, axis, keepdims=False)


def sum_parts(value, axis):
    mine = lax.axis_index("tensor")
    if lax.axis_size("tensor") == 2:
        other = swap(part_of(value, axis, 1 - mine).astype(BF))
        return part_of(value, axis, mine).astype(F32) + other.astype(F32)
    return lax.psum_scatter(
        value.astype(BF), "tensor", scatter_dimension=axis, tiled=True
    ).astype(F32)


def join_parts(value, axis):
    if lax.axis_size("tensor") != 2:
        return lax.all_gather(value, "tensor", axis=axis, tiled=True)
    other = swap(value)
    first = lax.axis_index("tensor") == 0
    low, high = jnp.where(first, value, other), jnp.where(first, other, value)
    return jnp.concatenate([low, high], axis)


def to_rows(value):
    blocks = lax.axis_size("blk")
    pad = jnp.zeros((blocks - value.shape[0],) + value.shape[1:], value.dtype)
    return lax.all_to_all(jnp.concatenate([value, pad], 0), "blk", 0, 0, tiled=True)


def to_blocks(value, rows):
    return lax.all_to_all(value, "blk", 0, 0, tiled=True)[:rows]


def sum_all(value, axes):
    for axis in axes:
        size = lax.axis_size(axis)
        step = 1
        while step < size:
            value = value + lax.ppermute(value, axis, [(i, i ^ step) for i in range(size)])
            step *= 2
    return value


def by_pair(value, width):
    count = value.shape[0]
    return value.reshape(count, 3, width // LANES, LANES).transpose(0, 2, 1, 3).reshape(count, 3 * width)


def by_kind(value, width):
    count = value.shape[0]
    return value.reshape(count, width // LANES, 3, LANES).transpose(0, 2, 1, 3).reshape(count, 3, width)


def scatter(value):
    return lax.psum_scatter(value, ("dp", "blk"), scatter_dimension=0, tiled=True).astype(F32)


def dot(a, b):
    return jnp.dot(a, b, preferred_element_type=F32)


def local(
    tokens, ln_gain, ln_bias, w_qkv, b_qkv, w_out, w_fc, b_fc, w_proj, b_out, bounds, cotangent
):
    rows, group, model = tokens.shape
    width, inner = b_qkv.shape[1], b_fc.shape[0]
    blocks, parts = lax.axis_size("blk"), lax.axis_size("tensor")
    length = blocks * group
    count = rows * group
    part = group // parts

    mine = lax.axis_index("tensor")
    pair = parts == 2
    hidden = (normalize(tokens.astype(F32))[0] * ln_gain + ln_bias).astype(BF)
    flat_hidden, cot = hidden.reshape(count, model), cotangent.reshape(count, model)

    shard = jnp.concatenate([by_pair(w_qkv, width), w_out.T, w_fc, w_proj.T], 1)
    weights = gather_weights(shard)
    full_qkv, full_out = weights[:, :3 * width], weights[:, 3 * width:4 * width]

    row_hidden = to_rows(part_of(hidden, 1, mine) + weights[0, 0] * 0)

    row_bounds = lax.dynamic_index_in_dim(
        bounds, jnp.minimum(lax.axis_index("blk"), rows - 1), 0, keepdims=False
    )
    index = jnp.arange(length, dtype=jnp.int32)
    start = jnp.max(jnp.where(row_bounds[:, None] <= index[None], row_bounds[:, None], 0), 0)

    groups = max(1, width // (2 * LANES))
    wide = width // groups
    cuts = [slice(n * wide, (n + 1) * wide) for n in range(groups)]
    grad_mixed = dot(cot, full_out).astype(BF).reshape(rows, group, width)
    row_grads = [to_rows(grad_mixed[:, :, cut]).reshape(length, wide) for cut in cuts]

    if pair:
        row_hidden = row_hidden.reshape(length // 2, model)
        row_hidden = [row_hidden, swap(row_hidden)]
    else:
        row_hidden = [join_parts(row_hidden, 1).reshape(length, model)]
    activated, grad_inner, mlp_out, mlp_back, grad_bfc = mlp(
        flat_hidden, cot, weights, 4 * width // inner, b_fc[None], (grad_mixed,)
    )
    grad_mlp = weight_grads(flat_hidden, grad_inner, cot, activated, (row_hidden[0],))
    other_out = swap(full_out + row_hidden[1][0, 0] * 0) if pair else None
    if pair:
        clear = row_hidden[1][0, 0] * 0
        mlp_back = sum_parts(mlp_back.reshape(rows, group, model) + clear, 1)
        other_mlp = [swap(mlp_out + clear)]
    else:
        mlp_back = sum_parts(mlp_back.reshape(rows, group, model), 1)

    bias = by_pair(b_qkv[None], width)
    grad_packed, mixed, other_mixed = [], [], []
    waits = [grad_mlp, *row_grads]
    for n, (cut, row_grad) in enumerate(zip(cuts, row_grads)):
        attended, grads = attention(
            row_hidden, weights, bias, n * (wide // LANES), row_grad, index - start, start,
            part if pair else 0, waits,
        )
        mixed.append(to_blocks(attended.reshape(blocks, group, wide), rows).reshape(count, wide))
        other_mixed.append(swap(mixed[-1]) if pair else None)
        grad_packed.append(grads)
        waits = [attended, mlp_back]
    grad_mlp = scatter(grad_mlp)
    grad_packed = [jnp.concatenate(grads, 1) for grads in zip(*grad_packed)]
    if pair:
        sent = swap(input_grad(grad_packed[1], weights))
        waits = [*other_mlp, other_out, *other_mixed[:-1], grad_mlp]
        kept = input_grad(grad_packed[0], weights, waits)
        back = [(kept.astype(F32) + sent.astype(F32)).astype(BF).reshape(blocks, part, model)]
    else:
        back = [sum_parts(nt(grad_packed[0], full_qkv).reshape(blocks, group, model), 1).astype(BF)]
    back = jnp.concatenate([to_blocks(piece, rows) for piece in back], 2).astype(F32)
    grad_bqkv = sum(jnp.sum(g.astype(F32), 0) for g in grad_packed)
    grad_qkv = sum(dot(h.T, g) for h, g in zip(row_hidden, grad_packed))

    own_tokens = part_of(tokens, 1, mine).astype(F32)
    if pair:
        branches = mlp_out.astype(F32) + jnp.concatenate(other_mlp, 0).astype(F32)
        for cut, piece, other in zip(cuts, mixed, other_mixed):
            branches += nt(piece, full_out[:, cut]) + nt(other, other_out[:, cut])
        result = (tokens.astype(F32) + branches.reshape(rows, group, model) + b_out).astype(BF)
    else:
        branches = mlp_out.astype(F32) + sum(nt(m, full_out[:, cut]) for m, cut in zip(mixed, cuts))
        branches = sum_parts(branches.reshape(rows, group, model), 1)
        result = join_parts((own_tokens + branches + b_out).astype(BF), 1)
    mixed = jnp.concatenate(mixed, 1)
    grad_hidden = mlp_back + back

    normal, scale = normalize(own_tokens)
    own_cot = part_of(cotangent, 1, mine).astype(F32)
    grad_normal = grad_hidden * ln_gain
    grad_inputs = scale * (
        grad_normal
        - jnp.mean(grad_normal, -1, keepdims=True)
        - normal * jnp.mean(grad_normal * normal, -1, keepdims=True)
    )
    grad_tokens = join_parts((own_cot + grad_inputs).astype(BF), 1)

    grad_attn = scatter(
        jnp.concatenate([grad_qkv.astype(BF), dot(cot.T, mixed).astype(BF)], 1)
    )

    norm_sums = jnp.concatenate(
        [jnp.sum(grad_hidden * normal, (0, 1)), jnp.sum(grad_hidden, (0, 1)), jnp.sum(own_cot, (0, 1))]
    ).reshape(-1, LANES)
    sums = jnp.concatenate([norm_sums, grad_bqkv.reshape(-1, LANES), grad_bfc.reshape(-1, LANES)], 0)
    sums = sum_all(sums, ("dp", "blk"))
    bias_sums = sums[norm_sums.shape[0]:].reshape(-1)
    norm_sums = sum_all(sums[:norm_sums.shape[0]], ("tensor",)).reshape(3, model)
    return (
        result,
        grad_tokens,
        norm_sums[0],
        norm_sums[1],
        by_kind(grad_attn[:, :3 * width], width),
        by_kind(bias_sums[None, :3 * width], width)[0],
        grad_attn[:, 3 * width:].T,
        grad_mlp[:, :inner],
        bias_sums[3 * width:],
        grad_mlp[:, inner:].T,
        norm_sums[2],
    )


def solution(mesh):
    in_specs = (
        P("dp", "blk", None),
        P(),
        P(),
        P(("dp", "blk"), None, "tensor"),
        P(None, "tensor"),
        P("tensor", ("dp", "blk")),
        P(("dp", "blk"), "tensor"),
        P("tensor"),
        P("tensor", ("dp", "blk")),
        P(),
        P("dp", None),
        P("dp", "blk", None),
    )
    out_specs = (
        P("dp", "blk", None),
        P("dp", "blk", None),
        P(),
        P(),
        P(("dp", "blk"), None, "tensor"),
        P(None, "tensor"),
        P("tensor", ("dp", "blk")),
        P(("dp", "blk"), "tensor"),
        P("tensor"),
        P("tensor", ("dp", "blk")),
        P(),
    )
    return jax.shard_map(local, mesh=mesh, in_specs=in_specs, out_specs=out_specs, check_vma=False)
```

time: 700 us -> 666 us (0.951)
  blocking collectives: 168 us -> 0 us
  Pallas kernels: 133 us -> 299 us
  matrix products: 134 us -> 39.6 us
  waiting for transfers between devices: 77.4 us -> 137 us
  starting transfers between devices: 26.3 us -> 56.2 us
  other arithmetic: 82.4 us -> 56.8 us
    pallas_call x1 -> x7, Pallas kernels: 133 us -> 299 us  [the longest x2 147 us: attention(): pl.pallas_call(functools.partial(attn_kernel, bq, bk, part, len(waits)),...]
    psum x2 -> x0, blocking collectives: 106 us -> none  [the longest x1 59.1 us: local(): grad_bqkv, grad_bfc = lax.psum((grad_bqkv, grad_bfc), ('dp', 'blk'))]
    dot_general x12 -> x8, matrix products: 134 us -> 39.6 us  [the longest x4 20.9 us: dot(): return jnp.dot(a, b, preferred_element_type=F32)]
    all_to_all x1 -> x0, blocking collectives: 62.3 us -> none  [to_rows(): lax.all_to_all(jnp.concatenate([value, pad], 0), 'blk', 0, 0, tiled=True)]
    all_to_all x1 -> x3, waiting for transfers between devices: 0.01 us -> 40.8 us  [to_rows(): lax.all_to_all(jnp.concatenate([value, pad], 0), 'blk', 0, 0, tiled=True)]
    convert_element_type x7 -> x5, other arithmetic: 43.6 us -> 10.1 us  [the longest x1 3.92 us: local(): (kept.astype(F32) + sent.astype(F32)).astype(BF)]
    ppermute x0 -> x5, waiting for transfers between devices: none -> 20.2 us  [sum_all(): lax.ppermute(value, axis, [(i, i ^ step) for i in range(size)])]
    concatenate x4 -> x3, local copies, waits for them, and re-layouts: 17.8 us -> 2.93 us  [the longest x2 2.79 us: local(): grad_packed = [jnp.concatenate(grads, 1) for grads in zip(*grad_packed)]]
  transfers between devices with their start and end apart: 17 -> 21, of which waited for: 5 -> 8; matrix products, arithmetic and copies ran while one was open for 38% -> 18% of each run, Pallas kernels for 19% -> 31%
where the time goes in v2:
time: 666 us; the launch traced here: 656 us
  Pallas kernels  299 us (45%)
  waiting for transfers between devices  137 us (21%)
  other arithmetic  56.8 us (9%)
  starting transfers between devices  56.2 us (8%)
  local copies, waits for them, and re-layouts  52 us (8%)
  matrix products  39.6 us (6%)
  between operations  16.1 us (2%)
    pallas_call x2, Pallas kernels, attention(): pl.pallas_call(functools.partial(attn_kernel, bq, bk, part, len(waits)),...  147 us
    pallas_call x1, Pallas kernels, gather_weights(): pl.pallas_call(gather_kernel, out_shape=jax.ShapeDtypeStruct((cores * blo...  73.4 us
    ppermute x8, waiting for transfers between devices, swap(): return lax.ppermute(value, 'tensor', [(0, 1), (1, 0)])  54.4 us
    pallas_call x1, Pallas kernels, mlp(): pl.pallas_call(functools.partial(mlp_kernel, tile, len(waits)), grid=(cou...  43.7 us
    all_to_all x3, waiting for transfers between devices, to_rows(): lax.all_to_all(jnp.concatenate([value, pad], 0), 'blk', 0, 0, tiled=True)  40.8 us
    pallas_call x1, Pallas kernels, weight_grads(): pl.pallas_call(functools.partial(weight_grad_kernel, half, len(waits)), g...  23 us
    all_to_all x3, waiting for transfers between devices, to_blocks(): return lax.all_to_all(value, 'blk', 0, 0, tiled=True)[:rows]  21.1 us
    dot_general x4, matrix products, dot(): return jnp.dot(a, b, preferred_element_type=F32)  20.9 us
  transfers between devices with their start and end apart: 21, of which 8 were waited for; matrix products, arithmetic and copies ran while one was open for 18% of the time, Pallas kernels for 31%

profile of v2, /device:TPU:28, one launch (start us, length us, event | category | flops | bytes accessed | tf_op | source)
XLA Modules:
  0.0 656.4 jit_solution(9288253013963478259)
XLA Ops:
  10.5 73.4 %shard_map.203.wf_ref.wp_ref.refs_5_.refs_4_.w_ref = bf16[1024,6144]{1,0:T(8,128)(2,1)} custom-call(bf16[64,6144]{1,0:T(8,128)(2,1)} %pad_maximum_fusion.2.x_ref), custom_call_target="tpu_custom_call" | custom-call | tf_op jit(solution)/shard_map/pallas_call | solution.py:391
  96.2 8.3 %all-to-all-start = ((bf16[8,128,1024]{2,1,0:T(8,128)(2,1)}), bf16[8,128,1024]{2,1,0:T(8,128)(2,1)S(1)}, u32[]{:S(2)}, u32[]{:S(2)}) async-start(bf16[8,128,1024]{2,1,0:T(8,128)(2,1)} %concatenate.40), calls=%async_computation | async-start | bytes 4194304 | tf_op jit(solution)/shard_map/all_to_all | solution.py:564
  104.9 5.7 fusion.21
  114.5 43.7 %shard_map.204 = (bf16[1792,2048]{1,0:T(8,128)(2,1)}, bf16[1792,2048]{1,0:T(8,128)(2,1)}, bf16[1792,1024]{1,0:T(8,128)(2,1)}, bf16[1792,1024]{1,0:T(8,128)(2,1)}, f32[1,2048]{1,0:T(1,128)}) custom-call(bf16[1792,1024]{1,0:T(8,128)(2,1)} %bitcast.125, bf16[1792,1024]{1,0:T(8,128)(2,1)} %bitcast.137, ...), custom_call_target="tpu_custom_call" | custom-call | flops 1000 | bytes 1000 | tf_op jit(solution)/shard_map/pallas_call | solution.py:509
  161.0 23.0 %shard_map.205.refs_2_ = bf16[1024,4096]{1,0:T(8,128)(2,1)} custom-call(bf16[1792,1024]{1,0:T(8,128)(2,1)S(1)} %bitcast.126, bf16[1792,1024]{1,0:T(8,128)(2,1)} %bitcast.138, bf16[1024,1024]{1,0:T(8,128)(2,1)S(1)} %bitcast.127, bf16[1792,2048]{1,0:T(8,128)(2,1)} %get-tuple-element.23.refs_1_, bf16[1792,2048]{1,0:T(8,128)(2,1)} %get-tuple-element.24.refs_2_), custom_call_target="tpu_custom_call" | custom-call | flops 1000 | bytes 1000 | tf_op jit(solution)/shard_map/pallas_call | solution.py:431
  187.6 6.0 all-to-all-start.2
  197.5 19.7 %all-to-all-done.2 = bf16[8,256,256]{2,1,0:T(8,128)(2,1)S(1)} async-done(((bf16[8,256,256]{2,1,0:T(8,128)(2,1)}), bf16[8,256,256]{2,1,0:T(8,128)(2,1)S(1)}, u32[]{:S(2)}, u32[]{:S(2)}) %all-to-all-start.2) | async-done | bytes 1048608 | tf_op jit(solution)/shard_map/all_to_all | solution.py:564
  217.3 6.6 all-to-all-start.1
  225.9 14.9 %collective-permute-done.refs_1_ = bf16[1024,1024]{1,0:T(8,128)(2,1)} collective-permute-done((bf16[1024,1024]{1,0:T(8,128)(2,1)S(1)}, bf16[1024,1024]{1,0:T(8,128)(2,1)}, u32[]{:S(2)}, u32[]{:S(2)}) %collective-permute-start) | collective-permute-done | bytes 2097184 | tf_op jit(solution)/shard_map/ppermute | solution.py:529
  250.6 21.0 %all-to-all-done.1 = bf16[8,256,256]{2,1,0:T(8,128)(2,1)} async-done(((bf16[8,256,256]{2,1,0:T(8,128)(2,1)}), bf16[8,256,256]{2,1,0:T(8,128)(2,1)}, u32[]{:S(2)}, u32[]{:S(2)}) %all-to-all-start.1) | async-done | bytes 1048608 | tf_op jit(solution)/shard_map/all_to_all | solution.py:564
  271.7 74.1 %shard_map.206 = (bf16[2048,256]{1,0:T(8,128)(2,1)}, bf16[1024,768]{1,0:T(8,128)(2,1)}, bf16[1024,768]{1,0:T(8,128)(2,1)}) custom-call(s32[4]{0:T(128)} %get-tuple-element.38.lo_ref, s32[4]{0:T(128)} %get-tuple-element.37.hi_ref, bf16[1024,1024]{1,0:T(8,128)(2,1)} %bitcast.129, bf16[1024,1024]{1,0:T(8,128)(2,1)} %collective-permute-done.refs_1_, ...), custom_call_target="tpu_custom_call" | custom-call | flops 1000 | bytes 1000 | tf_op jit(solution)/shard_map/pallas_call | solution.py:274
  345.8 7.3 %all-to-all-start.3 = ((bf16[8,256,256]{2,1,0:T(8,128)(2,1)}), bf16[8,256,256]{2,1,0:T(8,128)(2,1)}, u32[]{:S(2)}, u32[]{:S(2)}) async-start(bf16[8,256,256]{2,1,0:T(8,128)(2,1)} %bitcast.153), calls=%async_computation.3 | async-start | bytes 2097152 | tf_op jit(solution)/shard_map/all_to_all | solution.py:568
  354.9 4.2 broadcast_add_fusion.1
  364.6 3.9 convert_add_fusion.1.refs_3_
  369.1 73.2 %shard_map.207 = (bf16[2048,256]{1,0:T(8,128)(2,1)}, bf16[1024,768]{1,0:T(8,128)(2,1)}, bf16[1024,768]{1,0:T(8,128)(2,1)}) custom-call(s32[4]{0:T(128)} %get-tuple-element.38.lo_ref, s32[4]{0:T(128)} %get-tuple-element.37.hi_ref, bf16[1024,1024]{1,0:T(8,128)(2,1)} %bitcast.130, bf16[1024,1024]{1,0:T(8,128)(2,1)} %collective-permute-done.refs_1_, ...), custom_call_target="tpu_custom_call" | custom-call | flops 1000 | bytes 1000 | tf_op jit(solution)/shard_map/pallas_call | solution.py:274
  442.3 6.0 all-to-all-start.4
  454.7 4.6 copy-done.2
  461.1 5.1 shard_map.209
  466.9 5.3 fusion.47
  472.3 5.3 add_convert_fusion
  479.8 4.6 fusion.30
  492.2 6.5 shard_map.208
  498.7 28.4 %collective-permute-done.6 = bf16[1024,1024]{1,0:T(8,128)(2,1)} collective-permute-done((bf16[1024,1024]{1,0:T(8,128)(2,1)}, bf16[1024,1024]{1,0:T(8,128)(2,1)}, u32[]{:S(2)}, u32[]{:S(2)}) %collective-permute-start.6) | collective-permute-done | bytes 2097184 | tf_op jit(solution)/shard_map/ppermute | solution.py:529
  527.1 3.9 add_convert_fusion.1
  531.0 6.2 all-to-all-start.5
  546.2 5.1 fusion.37
  551.3 11.1 %collective-permute-done.5 = bf16[1792,256]{1,0:T(8,128)(2,1)S(1)} collective-permute-done((bf16[1792,256]{1,0:T(8,128)(2,1)S(1)}, bf16[1792,256]{1,0:T(8,128)(2,1)S(1)}, u32[]{:S(2)}, u32[]{:S(2)}) %collective-permute-start.5) | collective-permute-done | bytes 917536 | tf_op jit(solution)/shard_map/ppermute | solution.py:529
  562.4 8.5 %add_add_fusion = f32[1792,1024]{1,0:T(8,128)} fusion(f32[1792,1024]{1,0:T(8,128)} %fusion.37, f32[1792,1024]{1,0:T(8,128)S(1)} %fusion.39, f32[1792,1024]{1,0:T(8,128)S(1)} %fusion.35, bf16[1792,1024]{1,0:T(8,128)(2,1)} %collective-permute-done.1.refs_0_, bf16[1792,1024]{1,0:T(8,128)(2,1)} %get-tuple-element.22, ...), kind=kOutput, calls=%fused_computation.11 | convolution fusion | flops 952369152 | bytes 38141952 | tf_op jit(solution)/shard_map/dot_general | solution.py:20
  570.9 21.1 %all-to-all-done.5 = bf16[8,128,1024]{2,1,0:T(8,128)(2,1)} async-done(((bf16[8,128,1024]{2,1,0:T(8,128)(2,1)}), bf16[8,128,1024]{2,1,0:T(8,128)(2,1)}, u32[]{:S(2)}, u32[]{:S(2)}) %all-to-all-start.5) | async-done | bytes 2097184 | tf_op jit(solution)/shard_map/all_to_all | solution.py:568
  592.1 5.1 fusion.19
  597.4 4.7 fusion.9
  625.1 19.7 %collective-permute-done.12 = f32[24,128]{1,0:T(8,128)S(1)} collective-permute-done((f32[24,128]{1,0:T(8,128)S(1)}, f32[24,128]{1,0:T(8,128)S(1)}, u32[]{:S(2)}, u32[]{:S(2)}) %collective-permute-start.12) | collective-permute-done | bytes 12320 | tf_op jit(solution)/shard_map/ppermute | solution.py:576
  (157 shorter events, 103.9 us)
Async XLA Ops:
  7.2 216.6 %copy-start = (s32[7,5]{1,0:T(8,128)S(1)}, s32[7,5]{1,0:T(8,128)}, u32[]{:S(2)}) copy-start(s32[7,5]{1,0:T(8,128)} %param.22) | copy-start | bytes 424
  96.2 62.0 %all-to-all-start = ((bf16[8,128,1024]{2,1,0:T(8,128)(2,1)}), bf16[8,128,1024]{2,1,0:T(8,128)(2,1)S(1)}, u32[]{:S(2)}, u32[]{:S(2)}) async-start(bf16[8,128,1024]{2,1,0:T(8,128)(2,1)} %concatenate.40), calls=%async_computation | async-start | bytes 4194304 | tf_op jit(solution)/shard_map/all_to_all | solution.py:564
  104.5 386.5 %reduce-scatter.3.cloned.1.call-start = ((), (), s32[]{:S(2)}) async-start(), calls=%async_computation.8 | async-start | bytes 8912896 | tf_op jit(solution)/shard_map/reduce_scatter | solution.py:592
  158.2 35.4 %copy-start.5 = (bf16[8,128,1024]{2,1,0:T(8,128)(2,1)}, bf16[8,128,1024]{2,1,0:T(8,128)(2,1)S(1)}, u32[]{:S(2)}) copy-start(bf16[8,128,1024]{2,1,0:T(8,128)(2,1)S(1)} %all-to-all-done) | copy-start | bytes 6291460
  186.6 37.4 %copy-start.26 = (f32[3,512]{1,0:T(4,128)S(1)}, f32[3,512]{1,0:T(4,128)}, u32[]{:S(2)}) copy-start(f32[3,512]{1,0:T(4,128)} %param.16) | copy-start | bytes 18436
  187.6 29.7 %all-to-all-start.2 = ((bf16[8,256,256]{2,1,0:T(8,128)(2,1)}), bf16[8,256,256]{2,1,0:T(8,128)(2,1)S(1)}, u32[]{:S(2)}, u32[]{:S(2)}) async-start(bf16[8,256,256]{2,1,0:T(8,128)(2,1)} %concatenate.42), calls=%async_computation.2 | async-start | bytes 2097152 | tf_op jit(solution)/shard_map/all_to_all | solution.py:564
  193.6 47.2 %collective-permute-start = (bf16[1024,1024]{1,0:T(8,128)(2,1)S(1)}, bf16[1024,1024]{1,0:T(8,128)(2,1)}, u32[]{:S(2)}, u32[]{:S(2)}) collective-permute-start(bf16[1024,1024]{1,0:T(8,128)(2,1)S(1)} %bitcast.128), channel_id=1, source_target_pairs={{0,1},{1,0},{2,3},{3,2},{4,5},{5,4},{6,7},{7,6},{8,9},{9,8},{10,11... | collective-permute-start | bytes 6291464 | tf_op jit(solution)/shard_map/ppermute | solution.py:529
  217.3 27.6 %copy-start.16 = (bf16[8,256,256]{2,1,0:T(8,128)(2,1)}, bf16[8,256,256]{2,1,0:T(8,128)(2,1)S(1)}, u32[]{:S(2)}) copy-start(bf16[8,256,256]{2,1,0:T(8,128)(2,1)S(1)} %all-to-all-done.2) | copy-start | bytes 3145732
  217.3 54.4 %all-to-all-start.1 = ((bf16[8,256,256]{2,1,0:T(8,128)(2,1)}), bf16[8,256,256]{2,1,0:T(8,128)(2,1)}, u32[]{:S(2)}, u32[]{:S(2)}) async-start(bf16[8,256,256]{2,1,0:T(8,128)(2,1)} %concatenate.41), calls=%async_computation.1 | async-start | bytes 2097152 | tf_op jit(solution)/shard_map/all_to_all | solution.py:564
  248.2 116.4 %collective-permute-start.4 = (bf16[7,128,1024]{2,1,0:T(8,128)(2,1)}, bf16[7,128,1024]{2,1,0:T(8,128)(2,1)}, u32[]{:S(2)}, u32[]{:S(2)}) collective-permute-start(bf16[7,128,1024]{2,1,0:T(8,128)(2,1)} %dynamic-slice_bitcast_fusion), channel_id=1, source_target_pairs={{0,1},{1,0},{2,3},{3,2},{4,5},{5,4},{6,7},{7,6},{8,9},{9,8},{10,11... | collective-permute-start | bytes 5505032 | tf_op jit(solution)/shard_map/ppermute | solution.py:529
  345.8 96.5 %all-to-all-start.3 = ((bf16[8,256,256]{2,1,0:T(8,128)(2,1)}), bf16[8,256,256]{2,1,0:T(8,128)(2,1)}, u32[]{:S(2)}, u32[]{:S(2)}) async-start(bf16[8,256,256]{2,1,0:T(8,128)(2,1)} %bitcast.153), calls=%async_computation.3 | async-start | bytes 2097152 | tf_op jit(solution)/shard_map/all_to_all | solution.py:568
  354.9 7.0 %copy-start.22 = (bf16[1024,768]{1,0:T(8,128)(2,1)S(1)}, bf16[1024,768]{1,0:T(8,128)(2,1)}, u32[]{:S(2)}) copy-start(bf16[1024,768]{1,0:T(8,128)(2,1)} %get-tuple-element.28) | copy-start | bytes 4718596
  359.2 133.0 %collective-permute-start.1 = (bf16[1792,1024]{1,0:T(8,128)(2,1)}, bf16[1792,1024]{1,0:T(8,128)(2,1)}, u32[]{:S(2)}, u32[]{:S(2)}) collective-permute-start(bf16[1792,1024]{1,0:T(8,128)(2,1)} %broadcast_add_fusion.1), channel_id=1, source_target_pairs={{0,1},{1,0},{2,3},{3,2},{4,5},{5,4},{6,7},{7,6},{8,9},{9,8},{10,11... | collective-permute-start | bytes 11010056 | tf_op jit(solution)/shard_map/ppermute | solution.py:529
  368.5 123.6 %collective-permute-start.3 = (bf16[1024,512]{1,0:T(8,128)(2,1)}, bf16[1024,512]{1,0:T(8,128)(2,1)}, u32[]{:S(2)}, u32[]{:S(2)}) collective-permute-start(bf16[1024,512]{1,0:T(8,128)(2,1)} %slice_add_fusion), channel_id=1, source_target_pairs={{0,1},{1,0},{2,3},{3,2},{4,5},{5,4},{6,7},{7,6},{8,9},{9,8},{10,11... | collective-permute-start | bytes 3145736 | tf_op jit(solution)/shard_map/ppermute | solution.py:529
  442.3 35.3 %all-to-all-start.4 = ((bf16[8,256,256]{2,1,0:T(8,128)(2,1)}), bf16[8,256,256]{2,1,0:T(8,128)(2,1)}, u32[]{:S(2)}, u32[]{:S(2)}) async-start(bf16[8,256,256]{2,1,0:T(8,128)(2,1)} %bitcast.156), calls=%async_computation.4 | async-start | bytes 2097152 | tf_op jit(solution)/shard_map/all_to_all | solution.py:568
  448.4 160.6 %reduce-scatter.5.cloned.1.call-start = ((), (), s32[]{:S(2)}) async-start(), calls=%async_computation.9 | async-start | bytes 4456448 | tf_op jit(solution)/shard_map/reduce_scatter | solution.py:592
  453.2 39.0 %collective-permute-start.2 = (bf16[1792,256]{1,0:T(8,128)(2,1)}, bf16[1792,256]{1,0:T(8,128)(2,1)}, u32[]{:S(2)}, u32[]{:S(2)}) collective-permute-start(bf16[1792,256]{1,0:T(8,128)(2,1)} %bitcast.20), channel_id=1, source_target_pairs={{0,1},{1,0},{2,3},{3,2},{4,5},{5,4},{6,7},{7,6},{8,9},{9,8},{10,11... | collective-permute-start | bytes 2752520 | tf_op jit(solution)/shard_map/ppermute | solution.py:529
  466.2 60.9 %collective-permute-start.6 = (bf16[1024,1024]{1,0:T(8,128)(2,1)}, bf16[1024,1024]{1,0:T(8,128)(2,1)}, u32[]{:S(2)}, u32[]{:S(2)}) collective-permute-start(bf16[1024,1024]{1,0:T(8,128)(2,1)} %shard_map.209), channel_id=1, source_target_pairs={{0,1},{1,0},{2,3},{3,2},{4,5},{5,4},{6,7},{7,6},{8,9},{9,8},{10,11... | collective-permute-start | bytes 6291464 | tf_op jit(solution)/shard_map/ppermute | solution.py:529
  531.0 61.0 %all-to-all-start.5 = ((bf16[8,128,1024]{2,1,0:T(8,128)(2,1)}), bf16[8,128,1024]{2,1,0:T(8,128)(2,1)}, u32[]{:S(2)}, u32[]{:S(2)}) async-start(bf16[8,128,1024]{2,1,0:T(8,128)(2,1)} %bitcast.149), calls=%async_computation.6 | async-start | bytes 4194304 | tf_op jit(solution)/shard_map/all_to_all | solution.py:568
  542.3 20.2 %collective-permute-start.5 = (bf16[1792,256]{1,0:T(8,128)(2,1)S(1)}, bf16[1792,256]{1,0:T(8,128)(2,1)S(1)}, u32[]{:S(2)}, u32[]{:S(2)}) collective-permute-start(bf16[1792,256]{1,0:T(8,128)(2,1)S(1)} %bitcast.151), channel_id=1, source_target_pairs={{0,1},{1,0},{2,3},{3,2},{4,5},{5,4},{6,7},{7,6},{8,9},{9,8},{10,11... | collective-permute-start | bytes 2752520 | tf_op jit(solution)/shard_map/ppermute | solution.py:529
  570.9 26.2 %copy-start.25 = (f32[1,2048]{1,0:T(1,128)S(1)}, f32[1,2048]{1,0:T(1,128)}, u32[]{:S(2)}) copy-start(f32[1,2048]{1,0:T(1,128)} %get-tuple-element.32) | copy-start | bytes 24580
  597.3 6.4 collective-permute-start.8
  597.4 8.2 %copy-start.12 = (bf16[7,256,1024]{2,1,0:T(8,128)(2,1)S(1)}, bf16[7,256,1024]{2,1,0:T(8,128)(2,1)}, u32[]{:S(2)}) copy-start(bf16[7,256,1024]{2,1,0:T(8,128)(2,1)} %param.12) | copy-start | bytes 11010052
  597.4 8.2 %copy-start.13 = (f32[1792,1024]{1,0:T(8,128)S(1)}, f32[1792,1024]{1,0:T(8,128)}, u32[]{:S(2)}) copy-start(f32[1792,1024]{1,0:T(8,128)} %add_add_fusion) | copy-start | bytes 22020100
  597.4 8.1 %copy-start.28 = (f32[1024]{0:T(1024)S(1)}, f32[1024]{0:T(1024)}, u32[]{:S(2)}) copy-start(f32[1024]{0:T(1024)} %param.21) | copy-start | bytes 12292
  602.1 43.3 %collective-permute-start.7 = (bf16[7,128,1024]{2,1,0:T(8,128)(2,1)S(1)}, bf16[7,128,1024]{2,1,0:T(8,128)(2,1)}, u32[]{:S(2)}, u32[]{:S(2)}) collective-permute-start(bf16[7,128,1024]{2,1,0:T(8,128)(2,1)S(1)} %fusion.9), channel_id=1, source_target_pairs={{0,1},{1,0},{2,3},{3,2},{4,5},{5,4},{6,7},{7,6},{8,9},{9,8},{10,11... | collective-permute-start | bytes 5505032 | tf_op jit(solution)/shard_map/ppermute | solution.py:529
  603.7 6.3 collective-permute-start.9
  608.9 12.5 %copy-start.10 = (f32[64,4096]{1,0:T(8,128)S(1)}, f32[64,4096]{1,0:T(8,128)}, u32[]{:S(2)}) copy-start(f32[64,4096]{1,0:T(8,128)} %copy-done.9) | copy-start | bytes 3145732
  608.9 13.3 %copy-start.20 = (bf16[64,4096]{1,0:T(8,128)(2,1)S(1)}, bf16[64,4096]{1,0:T(8,128)(2,1)}, u32[]{:S(2)}) copy-start(bf16[64,4096]{1,0:T(8,128)(2,1)} %reduce-scatter.3.cloned.1.call-done) | copy-start | bytes 1572868
  610.0 8.3 %collective-permute-start.10 = (f32[52,128]{1,0:T(8,128)S(1)}, f32[52,128]{1,0:T(8,128)S(1)}, u32[]{:S(2)}, u32[]{:S(2)}) collective-permute-start(f32[52,128]{1,0:T(8,128)S(1)} %add.180), channel_id=1, source_target_pairs={{0,4},{2,6},{4,0},{6,2},{8,12},{10,14},{12,8},{14,10},{1,5},{3,7},... | collective-permute-start | bytes 79880 | tf_op jit(solution)/shard_map/ppermute | solution.py:576
  618.4 5.2 collective-permute-start.11
  623.5 21.3 %collective-permute-start.12 = (f32[24,128]{1,0:T(8,128)S(1)}, f32[24,128]{1,0:T(8,128)S(1)}, u32[]{:S(2)}, u32[]{:S(2)}) collective-permute-start(f32[24,128]{1,0:T(8,128)S(1)} %slice.110), channel_id=1, source_target_pairs={{0,1},{1,0},{2,3},{3,2},{4,5},{5,4},{6,7},{7,6},{8,9},{9,8},{10,11... | collective-permute-start | bytes 36872 | tf_op jit(solution)/shard_map/ppermute | solution.py:576
  (18 other events, 65.3 us)
Sparse Core Ops, SparseCore 0:
  184.2 127.8 reduce-scatter.2
  487.2 89.8 reduce-scatter.4

commit v3 on v2

--- a/solution.py
+++ b/solution.py
@@ -304,6 +304,22 @@
     return out[0], list(out[1:])
 
 
+MESH = pl.DeviceIdType.MESH
+
+
+def remote(src, dst, send, recv, target):
+    return pltpu.make_async_remote_copy(
+        src_ref=src, dst_ref=dst, send_sem=send, recv_sem=recv, device_id=target, device_id_type=MESH
+    )
+
+
+def meet(others):
+    barrier = pltpu.get_barrier_semaphore()
+    for target in others:
+        pl.semaphore_signal(barrier, inc=1, device_id=target, device_id_type=MESH)
+    pl.semaphore_wait(barrier, len(others))
+
+
 def gather_kernel(x_ref, out_ref, local_sem, recv, up, down, across, over):
     size = x_ref.shape[0]
     core, block = lax.axis_index("dp"), lax.axis_index("blk")
@@ -384,8 +400,6 @@
 
 def gather_weights(shard):
     cores, blocks = lax.axis_size("dp"), lax.axis_size("blk")
-    if (cores, blocks) != (2, 8):
-        return lax.all_gather(shard, ("dp", "blk"), axis=0, tiled=True)
     rows, columns = shard.shape
     dma = pltpu.SemaphoreType.DMA
     return pl.pallas_call(
@@ -401,8 +415,209 @@
     )(shard)
 
 
+class RowTransfer:
+    def __init__(self, hid_ref, mine_ref, other_ref, blank, blank_sem, hid_send, hid_recv, side_send, side_recv):
+        self.refs = hid_ref, mine_ref, other_ref, blank
+        self.sems = blank_sem, hid_send, hid_recv, side_send, side_recv
+        self.rows, group, _ = hid_ref.shape
+        self.part = group // 2
+        self.block, self.half = lax.axis_index("blk"), lax.axis_index("tensor")
+        self.blocks = lax.axis_size("blk")
+        self.has_row = self.block < self.rows
+        self.facing = {"tensor": 1 - self.half}
+
+    def piece(self, ref, at):
+        return ref.at[pl.ds(pl.multiple_of(at * self.part, self.part), self.part)]
+
+    def source(self, r):
+        return self.refs[0].at[r, pl.ds(pl.multiple_of(self.half * self.part, self.part), self.part)]
+
+    def row_copy(self, r):
+        _, hid_send, hid_recv, _, _ = self.sems
+        mine = self.piece(self.refs[1], self.block)
+        return remote(self.source(r), mine, hid_send.at[r], hid_recv.at[self.block], {"blk": r})
+
+    def own_row(self):
+        return pltpu.make_async_copy(
+            self.source(self.block), self.piece(self.refs[1], self.block), self.sems[1].at[self.block]
+        )
+
+    def side_copy(self, s):
+        _, _, _, side_send, side_recv = self.sems
+        _, mine, other, _ = self.refs
+        return remote(self.piece(mine, s), self.piece(other, s), side_send.at[s], side_recv.at[s], self.facing)
+
+    def blanks(self):
+        _, mine, other, blank = self.refs
+        return [
+            pltpu.make_async_copy(blank, self.piece(ref, s), self.sems[0].at[n * self.blocks + s])
+            for n, ref in enumerate((mine, other)) for s in range(self.blocks)
+        ]
+
+    def to_block(self, n, action):
+        r = lax.rem(self.block + n, self.blocks)
+        pl.when(r < self.rows)(lambda: action(self.row_copy(r)))
+
+    def start(self):
+        meet([{"blk": lax.rem(self.block + n, self.blocks)} for n in range(1, self.blocks)] + [self.facing])
+        for n in range(1, self.blocks):
+            self.to_block(n, lambda copy: copy.start())
+
+        @pl.when(self.has_row)
+        def _():
+            self.own_row().start()
+            self.own_row().wait()
+            self.side_copy(self.block).start()
+
+        @pl.when(jnp.logical_not(self.has_row))
+        def _():
+            self.refs[3][...] = jnp.zeros_like(self.refs[3])
+            for copy in self.blanks():
+                copy.start()
+
+    def onward(self, n):
+        @pl.when(self.has_row)
+        def _():
+            s = lax.rem(self.block + self.blocks - n, self.blocks)
+            mine = self.piece(self.refs[1], s)
+            remote(mine, mine, self.sems[3].at[s], self.sems[2].at[s], self.facing).wait_recv()
+            self.side_copy(s).start()
+
+    def finish(self):
+        for n in range(1, self.blocks):
+            self.to_block(n, lambda copy: copy.wait_send())
+
+        @pl.when(self.has_row)
+        def _():
+            for s in range(self.blocks):
+                self.side_copy(s).wait()
+
+        @pl.when(jnp.logical_not(self.has_row))
+        def _():
+            for copy in self.blanks():
+                copy.wait()
+
+
+def tail_kernel(groups, waits, *refs):
+    g_mine, g_other = refs[:groups], refs[groups:2 * groups]
+    (w_ref, tok_ref, cot_ref, add_ref, gain_ref, out_ref, sum_ref,
+     sent, got, home_send, home, grads, a_send, a_recv, b_send, b_recv, c_send, c_recv, c_local) = refs[2 * groups + waits:]
+    rows, part, model = tok_ref.shape
+    block, half = lax.axis_index("blk"), lax.axis_index("tensor")
+    blocks = lax.axis_size("blk")
+    facing = {"tensor": 1 - half}
+    has_row = block < rows
+    meet([{"blk": lax.rem(block + n, blocks)} for n in range(1, blocks)] + [facing])
+
+    def product(parts, s):
+        at, total, first = pl.ds(pl.multiple_of(s * part, part), part), None, 0
+        for g in parts:
+            width = g.shape[1]
+            term = nt(g[at, :], w_ref[:, first:first + width])
+            total, first = term if total is None else total + term, first + width
+        return total
+
+    def across(s):
+        return remote(sent.at[s], got.at[s], a_send.at[s], a_recv.at[s], facing)
+
+    def homeward(s):
+        return remote(home_send.at[s], home.at[block], b_send.at[s], b_recv.at[block], {"blk": s})
+
+    def own_half(ref, r):
+        return ref.at[r, pl.ds(pl.multiple_of(half * part, part), part)]
+
+    def share(r):
+        return remote(grads.at[r], own_half(out_ref, r), c_send.at[r], c_recv.at[r], facing)
+
+    def keep(r):
+        return pltpu.make_async_copy(grads.at[r], own_half(out_ref, r), c_local.at[r])
+
+    @pl.when(has_row)
+    def _():
+        for n in range(blocks):
+            s = lax.rem(block + n, blocks)
+            sent[s] = product(g_other, s).astype(BF)
+            across(s).start()
+
+    sum_ref[...] = jnp.zeros_like(sum_ref)
+
+    def forward(n):
+        s = lax.rem(block + n, blocks)
+
+        @pl.when(has_row)
+        def _():
+            total = product(g_mine, s)
+            across(s).wait_recv()
+            total = (total + got[s].astype(F32)).astype(BF)
+            if n == 0:
+                home[s] = total
+            else:
+                home_send[s] = total
+                homeward(s).start()
+
+    def norm(n):
+        r = lax.rem(block + blocks - n, blocks)
+
+        @pl.when(r < rows)
+        def _():
+            if n:
+                remote(home_send.at[r], home.at[r], b_send.at[r], b_recv.at[r], facing).wait_recv()
+            grad = home[r].astype(F32) + add_ref[r].astype(F32)
+            x = tok_ref[r].astype(F32)
+            x = x - jnp.mean(x, -1, keepdims=True)
+            scale = lax.rsqrt(jnp.mean(x * x, -1, keepdims=True) + EPSILON)
+            x = x * scale
+            sum_ref[0:1, :] += jnp.sum(grad * x, 0, keepdims=True)
+            sum_ref[1:2, :] += jnp.sum(grad, 0, keepdims=True)
+            grad = grad * gain_ref[...]
+            grad = grad - jnp.mean(grad, -1, keepdims=True) - x * jnp.mean(grad * x, -1, keepdims=True)
+            grads[r] = (cot_ref[r].astype(F32) + scale * grad).astype(BF)
+            share(r).start()
+            keep(r).start()
+
+    lag = 2
+    for n in range(blocks + lag):
+        if n < blocks:
+            forward(n)
+        if n >= lag:
+            norm(n - lag)
+
+    for r in range(rows):
+        share(r).wait()
+        keep(r).wait()
+
+    @pl.when(has_row)
+    def _():
+        for s in range(blocks):
+            across(s).wait_send()
+        for n in range(1, blocks):
+            homeward(lax.rem(block + n, blocks)).wait_send()
+
+
+def input_grads(g_mine, g_other, weights, tokens, cot, add, gain, waits=()):
+    rows, part, model = tokens.shape
+    blocks = lax.axis_size("blk")
+    wide = sum(g.shape[1] for g in g_mine)
+    dma = pltpu.SemaphoreType.DMA
+    vmem = pl.BlockSpec(memory_space=pltpu.VMEM)
+    return pl.pallas_call(
+        functools.partial(tail_kernel, len(g_mine), len(waits)),
+        grid=(1,),
+        out_shape=[jax.ShapeDtypeStruct((rows, 2 * part, model), BF), jax.ShapeDtypeStruct((8, model), F32)],
+        in_specs=[vmem] * (2 * len(g_mine)) + [pl.BlockSpec(memory_space=pl.ANY)] * len(waits)
+        + [pl.BlockSpec((model, wide), lambda i: (0, 0))] + [vmem] * 4,
+        out_specs=[pl.BlockSpec(memory_space=pl.ANY), vmem],
+        scratch_shapes=[pltpu.VMEM((blocks, part, model), BF)] * 4 + [pltpu.VMEM((rows, part, model), BF)]
+        + [dma((blocks,))] * 4 + [dma((rows,))] * 3,
+        compiler_params=pltpu.CompilerParams(
+            collective_id=1, has_side_effects=True, vmem_limit_bytes=48 * MIB
+        ),
+        cost_estimate=pl.CostEstimate(flops=1000, bytes_accessed=1000, transcendentals=0),
+    )(*g_mine, *g_other, *waits, weights, tokens, cot, add, gain)
+
+
 def weight_grad_kernel(half, waits, a_ref, b_ref, *refs):
-    x_ref, y_ref, out_ref, turned = refs[waits:]
+    x_ref, y_ref, ax_ref, by_ref, turned = refs[waits:]
     step = pl.program_id(0)
 
     @pl.when(step == 0)
@@ -415,11 +630,11 @@
 
     @pl.when(step < half)
     def _():
-        out_ref[...] = nn(turned[...], x_ref[...]).astype(BF)
+        ax_ref[...] = nn(turned[...], x_ref[...]).astype(BF)
 
     @pl.when(step >= half)
     def _():
-        out_ref[...] = nn(turned[...], y_ref[...]).astype(BF)
+        by_ref[...] = nn(turned[...], y_ref[...]).astype(BF)
 
 
 def weight_grads(a, x, b, y, waits=(), tile=512):
@@ -431,44 +646,31 @@
     return pl.pallas_call(
         functools.partial(weight_grad_kernel, half, len(waits)),
         grid=(2 * half,),
-        out_shape=jax.ShapeDtypeStruct((model, 2 * inner), BF),
+        out_shape=[jax.ShapeDtypeStruct((model, inner), BF)] * 2,
         in_specs=[
             whole, whole, *[pl.BlockSpec(memory_space=pl.ANY)] * len(waits),
             pl.BlockSpec((count, tile), lambda i: (0, jnp.minimum(i, half - 1))),
             pl.BlockSpec((count, tile), lambda i: (0, jnp.maximum(i - half, 0))),
         ],
-        out_specs=pl.BlockSpec((model, tile), lambda i: (0, i)),
+        out_specs=[
+            pl.BlockSpec((model, tile), lambda i: (0, jnp.minimum(i, half - 1))),
+            pl.BlockSpec((model, tile), lambda i: (0, jnp.maximum(i - half, 0))),
+        ],
         scratch_shapes=[pltpu.VMEM((model, count), BF)],
         compiler_params=pltpu.CompilerParams(vmem_limit_bytes=48 * MIB),
         cost_estimate=pl.CostEstimate(flops=1000, bytes_accessed=1000, transcendentals=0),
     )(a, b, *waits, x, y)
 
 
-def back_kernel(waits, g_ref, w_ref, *refs):
-    out_ref = refs[waits]
-    out_ref[...] = nt(g_ref[...], w_ref[...]).astype(BF)
-
-
-def input_grad(grad, weights, waits=(), size=256):
-    count, depth = grad.shape
-    model = weights.shape[0]
-    return pl.pallas_call(
-        functools.partial(back_kernel, len(waits)),
-        grid=(count // size,),
-        out_shape=jax.ShapeDtypeStruct((count, model), BF),
-        in_specs=[
-            pl.BlockSpec((size, depth), lambda i: (i, 0)),
-            pl.BlockSpec((model, depth), lambda i: (0, 0), pipeline_mode=pl.Buffered(1)),
-            *[pl.BlockSpec(memory_space=pl.ANY)] * len(waits),
-        ],
-        out_specs=pl.BlockSpec((size, model), lambda i: (i, 0)),
-        compiler_params=pltpu.CompilerParams(vmem_limit_bytes=32 * MIB),
-        cost_estimate=pl.CostEstimate(flops=1000, bytes_accessed=1000, transcendentals=0),
-    )(grad, weights, *waits)
-
-
-def mlp_kernel(tile, waits, hid_ref, cot_ref, wf_ref, wp_ref, bias_ref, *refs):
-    act_ref, gin_ref, res_ref, back_ref, gb_ref = refs[waits:]
+def mlp_kernel(tile, waits, moves, hid_ref, cot_ref, wf_ref, wp_ref, bias_ref, *refs):
+    refs = refs[waits:]
+    act_ref, gin_ref, res_ref, back_ref, gb_ref = refs[moves:moves + 5]
+    if moves:
+        step, steps = pl.program_id(0), pl.num_programs(0)
+        rows = RowTransfer(refs[0], *refs[moves + 5:])
+        pl.when(step == 0)(rows.start)
+        for n in range(1, rows.blocks):
+            pl.when(step == jnp.minimum(n, steps - 1))(lambda: rows.onward(n))
     hid, cot = hid_ref[...], cot_ref[...]
 
     @pl.when(pl.program_id(0) == 0)
@@ -496,26 +698,36 @@
         res, back = (r, b) if res is None else (res + r, back + b)
     res_ref[...] = res.astype(BF)
     back_ref[...] = back.astype(BF)
-
-
-def mlp(hidden, cot, weights, first_block, bias, waits=(), size=256, tile=512):
+    if moves:
+        pl.when(step == steps - 1)(rows.finish)
+
+
+def mlp(hidden, cot, weights, first_block, bias, waits=(), moved=None, size=256, tile=512):
     count, model = hidden.shape
     inner = bias.shape[1]
     tile = min(tile, inner)
     rows = lambda n: pl.BlockSpec((size, n), lambda i: (i, 0))
     matrix = lambda n: pl.BlockSpec((model, inner), lambda i: (0, first_block + n), pipeline_mode=pl.Buffered(1))
     vector = pl.BlockSpec((1, inner), lambda i: (0, 0))
+    hbm = pl.BlockSpec(memory_space=pl.ANY)
     shape = lambda n: jax.ShapeDtypeStruct((count, n), BF)
+    moves, outs, scratch, params = (), [], [], {}
+    if moved is not None:
+        blocks, dma = lax.axis_size("blk"), pltpu.SemaphoreType.DMA
+        part = moved.shape[1] // 2
+        moves, outs = (moved,), [jax.ShapeDtypeStruct((blocks * part, model), BF)] * 2
+        scratch = [pltpu.VMEM((part, model), BF), dma((2 * blocks,))] + [dma((blocks,))] * 4
+        params = dict(collective_id=2, has_side_effects=True)
     return pl.pallas_call(
-        functools.partial(mlp_kernel, tile, len(waits)),
+        functools.partial(mlp_kernel, tile, len(waits), len(moves)),
         grid=(count // size,),
-        out_shape=[shape(inner), shape(inner), shape(model), shape(model), jax.ShapeDtypeStruct((1, inner), F32)],
-        in_specs=[rows(model), rows(model), matrix(0), matrix(1), vector]
-        + [pl.BlockSpec(memory_space=pl.ANY)] * len(waits),
-        out_specs=[rows(inner), rows(inner), rows(model), rows(model), vector],
-        compiler_params=pltpu.CompilerParams(vmem_limit_bytes=56 * MIB),
+        out_shape=[shape(inner), shape(inner), shape(model), shape(model), jax.ShapeDtypeStruct((1, inner), F32)] + outs,
+        in_specs=[rows(model), rows(model), matrix(0), matrix(1), vector] + [hbm] * (len(waits) + len(moves)),
+        out_specs=[rows(inner), rows(inner), rows(model), rows(model), vector] + [hbm] * len(outs),
+        scratch_shapes=scratch,
+        compiler_params=pltpu.CompilerParams(vmem_limit_bytes=56 * MIB, **params),
         cost_estimate=pl.CostEstimate(flops=1000, bytes_accessed=1000, transcendentals=0),
-    )(hidden, cot, weights, weights, bias, *waits)
+    )(hidden, cot, weights, weights, bias, *waits, *moves)
 
 
 def normalize(values):
@@ -607,15 +819,17 @@
     part = group // parts
 
     mine = lax.axis_index("tensor")
-    pair = parts == 2
+    pair = parts == 2 and (lax.axis_size("dp"), blocks) == (2, 8)
     hidden = (normalize(tokens.astype(F32))[0] * ln_gain + ln_bias).astype(BF)
     flat_hidden, cot = hidden.reshape(count, model), cotangent.reshape(count, model)
 
     shard = jnp.concatenate([by_pair(w_qkv, width), w_out.T, w_fc, w_proj.T], 1)
-    weights = gather_weights(shard)
+    if pair:
+        weights = gather_weights(shard)
+    else:
+        weights = lax.all_gather(shard, ("dp", "blk"), axis=0, tiled=True)
+        row_hidden = [join_parts(to_rows(part_of(hidden, 1, mine)), 1).reshape(length, model)]
     full_qkv, full_out = weights[:, :3 * width], weights[:, 3 * width:4 * width]
-
-    row_hidden = to_rows(part_of(hidden, 1, mine) + weights[0, 0] * 0)
 
     row_bounds = lax.dynamic_index_in_dim(
         bounds, jnp.minimum(lax.axis_index("blk"), rows - 1), 0, keepdims=False
@@ -627,80 +841,73 @@
     wide = width // groups
     cuts = [slice(n * wide, (n + 1) * wide) for n in range(groups)]
     grad_mixed = dot(cot, full_out).astype(BF).reshape(rows, group, width)
+
+    activated, grad_inner, mlp_out, mlp_back, grad_bfc, *moved = mlp(
+        flat_hidden, cot, weights, 4 * width // inner, b_fc[None], (grad_mixed,), hidden if pair else None
+    )
+    grad_mixed += grad_inner[0, 0] * 0
     row_grads = [to_rows(grad_mixed[:, :, cut]).reshape(length, wide) for cut in cuts]
-
+    row_hidden = moved or row_hidden
+    mlp_back = sum_parts(mlp_back.reshape(rows, group, model), 1)
+    grad_fc, grad_proj = weight_grads(flat_hidden, grad_inner, cot, activated)
+    grad_fc_sum, grad_proj_sum = scatter(grad_fc), scatter(grad_proj)
     if pair:
-        row_hidden = row_hidden.reshape(length // 2, model)
-        row_hidden = [row_hidden, swap(row_hidden)]
-    else:
-        row_hidden = [join_parts(row_hidden, 1).reshape(length, model)]
-    activated, grad_inner, mlp_out, mlp_back, grad_bfc = mlp(
-        flat_hidden, cot, weights, 4 * width // inner, b_fc[None], (grad_mixed,)
-    )
-    grad_mlp = weight_grads(flat_hidden, grad_inner, cot, activated, (row_hidden[0],))
-    other_out = swap(full_out + row_hidden[1][0, 0] * 0) if pair else None
-    if pair:
-        clear = row_hidden[1][0, 0] * 0
-        mlp_back = sum_parts(mlp_back.reshape(rows, group, model) + clear, 1)
-        other_mlp = [swap(mlp_out + clear)]
-    else:
-        mlp_back = sum_parts(mlp_back.reshape(rows, group, model), 1)
+        mlp_back = mlp_back.astype(BF)
+        other_out = swap(full_out)
+        other_mlp = swap(mlp_out + mlp_back[0, 0, 0] * 0)
 
     bias = by_pair(b_qkv[None], width)
-    grad_packed, mixed, other_mixed = [], [], []
-    waits = [grad_mlp, *row_grads]
-    for n, (cut, row_grad) in enumerate(zip(cuts, row_grads)):
-        attended, grads = attention(
+    own_tokens, own_cot = part_of(tokens, 1, mine), part_of(cotangent, 1, mine)
+    grad_packed, grad_qkv, attended = [], [], []
+    waits = [grad_fc, own_tokens, own_cot]
+    for n, row_grad in enumerate(row_grads):
+        out, grads = attention(
             row_hidden, weights, bias, n * (wide // LANES), row_grad, index - start, start,
             part if pair else 0, waits,
         )
-        mixed.append(to_blocks(attended.reshape(blocks, group, wide), rows).reshape(count, wide))
-        other_mixed.append(swap(mixed[-1]) if pair else None)
+        attended.append(out)
         grad_packed.append(grads)
-        waits = [attended, mlp_back]
-    grad_mlp = scatter(grad_mlp)
-    grad_packed = [jnp.concatenate(grads, 1) for grads in zip(*grad_packed)]
+        grad_qkv.append(sum(dot(h.T, g) for h, g in zip(row_hidden, grads)).astype(BF))
+        waits = [out, grad_fc_sum, mlp_back]
+        if pair:
+            waits.append(other_out)
+    mixed = to_blocks(jnp.concatenate(attended, 1).reshape(blocks, group, width), rows).reshape(count, width)
+    grad_bqkv = jnp.concatenate([sum(jnp.sum(g.astype(F32), 0) for g in grads) for grads in grad_packed])
+    grad_qkv = jnp.concatenate(grad_qkv, 1)
+    grad_qkv_sum = scatter(grad_qkv)
+
     if pair:
-        sent = swap(input_grad(grad_packed[1], weights))
-        waits = [*other_mlp, other_out, *other_mixed[:-1], grad_mlp]
-        kept = input_grad(grad_packed[0], weights, waits)
-        back = [(kept.astype(F32) + sent.astype(F32)).astype(BF).reshape(blocks, part, model)]
+        grad_tokens, norm_sums = input_grads(
+            [g[0] for g in grad_packed], [g[1] for g in grad_packed], weights, own_tokens, own_cot, mlp_back,
+            ln_gain[None], [grad_qkv, grad_proj_sum, other_mlp],
+        )
+        norm_sums = norm_sums[:2]
+        branches = mlp_out.astype(F32) + other_mlp.astype(F32)
+        branches += tokens.reshape(count, model).astype(F32) + (b_out + norm_sums[0, 0] * 0)
+        branches += dot(jnp.concatenate([mixed, swap(mixed)], 1), jnp.concatenate([full_out, other_out], 1).T)
+        result = branches.astype(BF).reshape(rows, group, model)
+        norm_sums = norm_sums + mixed[0, 0].astype(F32) * 0
     else:
-        back = [sum_parts(nt(grad_packed[0], full_qkv).reshape(blocks, group, model), 1).astype(BF)]
-    back = jnp.concatenate([to_blocks(piece, rows) for piece in back], 2).astype(F32)
-    grad_bqkv = sum(jnp.sum(g.astype(F32), 0) for g in grad_packed)
-    grad_qkv = sum(dot(h.T, g) for h, g in zip(row_hidden, grad_packed))
-
-    own_tokens = part_of(tokens, 1, mine).astype(F32)
-    if pair:
-        branches = mlp_out.astype(F32) + jnp.concatenate(other_mlp, 0).astype(F32)
-        for cut, piece, other in zip(cuts, mixed, other_mixed):
-            branches += nt(piece, full_out[:, cut]) + nt(other, other_out[:, cut])
-        result = (tokens.astype(F32) + branches.reshape(rows, group, model) + b_out).astype(BF)
-    else:
-        branches = mlp_out.astype(F32) + sum(nt(m, full_out[:, cut]) for m, cut in zip(mixed, cuts))
+        grads = jnp.concatenate([g[0] for g in grad_packed], 1)
+        back = sum_parts(nt(grads, full_qkv).reshape(blocks, group, model), 1).astype(BF)
+        grad_hidden = mlp_back + to_blocks(back, rows).astype(F32)
+        branches = mlp_out.astype(F32) + nt(mixed, full_out)
         branches = sum_parts(branches.reshape(rows, group, model), 1)
-        result = join_parts((own_tokens + branches + b_out).astype(BF), 1)
-    mixed = jnp.concatenate(mixed, 1)
-    grad_hidden = mlp_back + back
-
-    normal, scale = normalize(own_tokens)
-    own_cot = part_of(cotangent, 1, mine).astype(F32)
-    grad_normal = grad_hidden * ln_gain
-    grad_inputs = scale * (
-        grad_normal
-        - jnp.mean(grad_normal, -1, keepdims=True)
-        - normal * jnp.mean(grad_normal * normal, -1, keepdims=True)
-    )
-    grad_tokens = join_parts((own_cot + grad_inputs).astype(BF), 1)
-
-    grad_attn = scatter(
-        jnp.concatenate([grad_qkv.astype(BF), dot(cot.T, mixed).astype(BF)], 1)
-    )
-
-    norm_sums = jnp.concatenate(
-        [jnp.sum(grad_hidden * normal, (0, 1)), jnp.sum(grad_hidden, (0, 1)), jnp.sum(own_cot, (0, 1))]
-    ).reshape(-1, LANES)
+        result = join_parts((own_tokens.astype(F32) + branches + b_out).astype(BF), 1)
+        normal, scale = normalize(own_tokens.astype(F32))
+        grad_normal = grad_hidden * ln_gain
+        grad_inputs = scale * (
+            grad_normal
+            - jnp.mean(grad_normal, -1, keepdims=True)
+            - normal * jnp.mean(grad_normal * normal, -1, keepdims=True)
+        )
+        grad_tokens = join_parts((own_cot.astype(F32) + grad_inputs).astype(BF), 1)
+        norm_sums = jnp.stack([jnp.sum(grad_hidden * normal, (0, 1)), jnp.sum(grad_hidden, (0, 1))])
+
+    grad_out = lax.all_to_all(dot(cot.T, mixed).astype(BF), ("dp", "blk"), 0, 0, tiled=True)
+    grad_out_sum = jnp.sum(grad_out.reshape(-1, shard.shape[0], width).astype(F32), 0)
+
+    norm_sums = jnp.concatenate([norm_sums, jnp.sum(own_cot.astype(F32), (0, 1))[None]]).reshape(-1, LANES)
     sums = jnp.concatenate([norm_sums, grad_bqkv.reshape(-1, LANES), grad_bfc.reshape(-1, LANES)], 0)
     sums = sum_all(sums, ("dp", "blk"))
     bias_sums = sums[norm_sums.shape[0]:].reshape(-1)
@@ -710,12 +917,12 @@
         grad_tokens,
         norm_sums[0],
         norm_sums[1],
-        by_kind(grad_attn[:, :3 * width], width),
+        by_kind(grad_qkv_sum, width),
         by_kind(bias_sums[None, :3 * width], width)[0],
-        grad_attn[:, 3 * width:].T,
-        grad_mlp[:, :inner],
+        grad_out_sum.T,
+        grad_fc_sum,
         bias_sums[3 * width:],
-        grad_mlp[:, inner:].T,
+        grad_proj_sum.T,
         norm_sums[2],
     )
 

time: 666 us -> 629 us (0.944)
  Pallas kernels: 299 us -> 401 us
  waiting for transfers between devices: 137 us -> 44.4 us
  other arithmetic: 56.8 us -> 29.9 us
  local copies, waits for them, and re-layouts: 52 us -> 40.8 us
    pallas_call x3 -> x2, Pallas kernels: 55.3 us -> 168 us  [the longest x1 117 us: input_grads(): pl.pallas_call(functools.partial(tail_kernel, len(g_mine), len(waits)), g...]
    ppermute x8 -> x4, waiting for transfers between devices: 54.4 us -> 10.5 us  [swap(): return lax.ppermute(value, 'tensor', [(0, 1), (1, 0)])]
    all_to_all x3 -> x2, waiting for transfers between devices: 40.8 us -> 10.6 us  [to_rows(): lax.all_to_all(jnp.concatenate([value, pad], 0), 'blk', 0, 0, tiled=True)]
    all_to_all x3 -> x1, waiting for transfers between devices: 21.1 us -> 0.01 us  [to_blocks(): return lax.all_to_all(value, 'blk', 0, 0, tiled=True)[:rows]]
    all_to_all x3 -> x2, starting transfers between devices: 20.8 us -> 40.6 us  [to_rows(): lax.all_to_all(jnp.concatenate([value, pad], 0), 'blk', 0, 0, tiled=True)]
    dot_general x4 -> x0, matrix products: 18.6 us -> none  [nt(): lax.dot_general(a, b, (((1,), (1,)), ((), ())), preferred_element_type=F32)]
    all_to_all x3 -> x1, starting transfers between devices: 19.5 us -> 6.13 us  [to_blocks(): return lax.all_to_all(value, 'blk', 0, 0, tiled=True)[:rows]]
    dot_general x4 -> x7, matrix products: 20.9 us -> 33.6 us  [dot(): return jnp.dot(a, b, preferred_element_type=F32)]
  transfers between devices with their start and end apart: 21 -> 16, of which waited for: 8 -> 6; matrix products, arithmetic and copies ran while one was open for 18% -> 12% of each run, Pallas kernels for 31% -> 40%
where the time goes in v3:
time: 629 us; the launch traced here: 625 us
  Pallas kernels  401 us (64%)
  starting transfers between devices  58.5 us (9%)
  waiting for transfers between devices  44.4 us (7%)
  local copies, waits for them, and re-layouts  40.8 us (6%)
  matrix products  33.6 us (5%)
  other arithmetic  29.9 us (5%)
  between operations  17.2 us (3%)
    pallas_call x2, Pallas kernels, attention(): pl.pallas_call(functools.partial(attn_kernel, bq, bk, part, len(waits)),...  136 us
    pallas_call x1, Pallas kernels, input_grads(): pl.pallas_call(functools.partial(tail_kernel, len(g_mine), len(waits)), g...  117 us
    pallas_call x1, Pallas kernels, gather_weights(): pl.pallas_call(gather_kernel, out_shape=jax.ShapeDtypeStruct((cores * blo...  73.4 us
    pallas_call x1, Pallas kernels, mlp(): pl.pallas_call(functools.partial(mlp_kernel, tile, len(waits), len(moves)...  51 us
    all_to_all x2, starting transfers between devices, to_rows(): lax.all_to_all(jnp.concatenate([value, pad], 0), 'blk', 0, 0, tiled=True)  40.6 us
    dot_general x7, matrix products, dot(): return jnp.dot(a, b, preferred_element_type=F32)  33.6 us
    pallas_call x1, Pallas kernels, weight_grads(): pl.pallas_call(functools.partial(weight_grad_kernel, half, len(waits)), g...  23.5 us
    ppermute x5, waiting for transfers between devices, sum_all(): lax.ppermute(value, axis, [(i, i ^ step) for i in range(size)])  22.5 us
  transfers between devices with their start and end apart: 16, of which 6 were waited for; matrix products, arithmetic and copies ran while one was open for 12% of the time, Pallas kernels for 40%

profile of v3, /device:TPU:28, one launch (start us, length us, event | category | flops | bytes accessed | tf_op | source)
XLA Modules:
  0.0 625.4 jit_solution(14881400581523690396)
XLA Ops:
  10.5 73.4 %shard_map.203.wf_ref.wp_ref.refs_5_.refs_6_.refs_7_ = bf16[1024,6144]{1,0:T(8,128)(2,1)} custom-call(bf16[64,6144]{1,0:T(8,128)(2,1)} %pad_maximum_fusion.2.x_ref), custom_call_target="tpu_custom_call" | custom-call | tf_op jit(solution)/shard_map/pallas_call | solution.py:405
  84.0 4.5 fusion.10
  88.4 2.8 copy.64
  91.2 2.7 convert_reduce_fusion
  95.5 2.7 add_convert_fusion.refs_1_
  98.2 51.0 %shard_map.204 = (bf16[1792,2048]{1,0:T(8,128)(2,1)}, bf16[1792,2048]{1,0:T(8,128)(2,1)}, bf16[1792,1024]{1,0:T(8,128)(2,1)}, bf16[1792,1024]{1,0:T(8,128)(2,1)}...) custom-call(bf16[1792,1024]{1,0:T(8,128)(2,1)} %bitcast.97, ...), custom_call_target="tpu_custom_call" | custom-call | flops 1000 | bytes 1000 | tf_op jit(solution)/shard_map/pallas_call | solution.py:721
  149.3 23.5 %shard_map.205 = (bf16[1024,2048]{1,0:T(8,128)(2,1)}, bf16[1024,2048]{1,0:T(8,128)(2,1)}) custom-call(bf16[1792,1024]{1,0:T(8,128)(2,1)S(1)} %bitcast.98, bf16[1792,1024]{1,0:T(8,128)(2,1)} %bitcast.103, bf16[1792,2048]{1,0:T(8,128)(2,1)} %get-tuple-element.32.refs_0_, bf16[1792,2048]{1,0:T(8,128)(2,1)} %get-tuple-element.33.refs_1_), custom_call_target="tpu_custom_call" | custom-call | flops 1000 | bytes 1000 | tf_op jit(solution)/shard_map/pallas_call | solution.py:646
  176.7 32.0 %all-to-all-start = ((bf16[8,256,256]{2,1,0:T(8,128)(2,1)}), bf16[8,256,256]{2,1,0:T(8,128)(2,1)S(1)}, u32[]{:S(2)}, u32[]{:S(2)}) async-start(bf16[8,256,256]{2,1,0:T(8,128)(2,1)} %concatenate.31), calls=%async_computation | async-start | bytes 2097152 | tf_op jit(solution)/shard_map/all_to_all | solution.py:776
  208.7 3.1 dynamic-slice_bitcast_fusion.2
  212.3 2.3 slice.56
  218.6 3.8 convert_reduce_fusion.1
  225.4 10.6 %all-to-all-done = bf16[8,256,256]{2,1,0:T(8,128)(2,1)S(1)} async-done(((bf16[8,256,256]{2,1,0:T(8,128)(2,1)}), bf16[8,256,256]{2,1,0:T(8,128)(2,1)S(1)}, u32[]{:S(2)}, u32[]{:S(2)}) %all-to-all-start) | async-done | bytes 1048608 | tf_op jit(solution)/shard_map/all_to_all | solution.py:776
  236.1 8.5 %all-to-all-start.1 = ((bf16[8,256,256]{2,1,0:T(8,128)(2,1)}), bf16[8,256,256]{2,1,0:T(8,128)(2,1)S(1)}, u32[]{:S(2)}, u32[]{:S(2)}) async-start(bf16[8,256,256]{2,1,0:T(8,128)(2,1)} %concatenate.32), calls=%async_computation.2 | async-start | bytes 2097152 | tf_op jit(solution)/shard_map/all_to_all | solution.py:776
  244.6 10.5 %collective-permute-done = bf16[7,128,1024]{2,1,0:T(8,128)(2,1)} collective-permute-done((bf16[7,128,1024]{2,1,0:T(8,128)(2,1)}, bf16[7,128,1024]{2,1,0:T(8,128)(2,1)}, u32[]{:S(2)}, u32[]{:S(2)}) %collective-permute-start) | collective-permute-done | bytes 1835040 | tf_op jit(solution)/shard_map/ppermute | solution.py:741
  255.1 2.9 fusion.7.refs_4_.refs_10_
  261.9 73.4 %shard_map.206 = (bf16[2048,256]{1,0:T(8,128)(2,1)}, bf16[1024,768]{1,0:T(8,128)(2,1)}, bf16[1024,768]{1,0:T(8,128)(2,1)}) custom-call(s32[4]{0:T(128)} %get-tuple-element.46.lo_ref, s32[4]{0:T(128)} %get-tuple-element.45.hi_ref, bf16[1024,1024]{1,0:T(8,128)(2,1)} %get-tuple-element.30.refs_0_, bf16[1024,1024]{1,0:T(8,128)(2,1)} %get-tuple-element.31.refs_1_, ...), custom_call_target="tpu_custom_call" | custom-call | flops 1000 | bytes 1000 | tf_op jit(solution)/shard_map/pallas_call | solution.py:274
  335.3 3.5 fusion.22
  338.9 3.2 add_convert_fusion.2
  344.8 62.9 %shard_map.207 = (bf16[2048,256]{1,0:T(8,128)(2,1)}, bf16[1024,768]{1,0:T(8,128)(2,1)}, bf16[1024,768]{1,0:T(8,128)(2,1)}) custom-call(s32[4]{0:T(128)} %get-tuple-element.46.lo_ref, s32[4]{0:T(128)} %get-tuple-element.45.hi_ref, bf16[1024,1024]{1,0:T(8,128)(2,1)} %get-tuple-element.30.refs_0_, bf16[1024,1024]{1,0:T(8,128)(2,1)} %get-tuple-element.31.refs_1_, ...), custom_call_target="tpu_custom_call" | custom-call | flops 1000 | bytes 1000 | tf_op jit(solution)/shard_map/pallas_call | solution.py:274
  407.7 2.7 pad_maximum_fusion.1
  410.4 3.9 copy.73
  414.3 6.1 all-to-all-start.2
  420.5 3.7 fusion.23
  433.3 116.8 %shard_map.208 = (bf16[7,256,1024]{2,1,0:T(8,128)(2,1)}, f32[8,1024]{1,0:T(8,128)S(1)}) custom-call(bf16[1024,768]{1,0:T(8,128)(2,1)S(1)} %copy-done.3, bf16[1024,768]{1,0:T(8,128)(2,1)S(1)} %copy-done.6, bf16[1024,768]{1,0:T(8,128)(2,1)S(1)} %copy-done.4, bf16[1024,768]{1,0:T(8,128)(2,1)} %get-tuple-element.39.refs_3_, ...), custom_call_target="tpu_custom_call" | custom-call | flops 1000 | bytes 1000 | tf_op jit(solution)/shard_map/pallas_call | solution.py:603
  552.3 2.3 copy.74
  559.8 2.7 collective-permute-done.5
  562.5 3.8 collective-permute-done.6
  566.4 4.7 fusion.14
  572.4 6.9 %all-to-all-start.3 = ((bf16[16,64,512]{2,1,0:T(8,128)(2,1)}), bf16[16,64,512]{2,1,0:T(8,128)(2,1)S(1)}, u32[]{:S(2)}, u32[]{:S(2)}) async-start(bf16[16,64,512]{2,1,0:T(8,128)(2,1)} %bitcast.41), calls=%async_computation.6 | async-start | bytes 2097152 | tf_op jit(solution)/shard_map/all_to_all | solution.py:907
  581.8 14.8 %collective-permute-done.8 = f32[24,128]{1,0:T(8,128)S(1)} collective-permute-done((f32[24,128]{1,0:T(8,128)S(1)}, f32[24,128]{1,0:T(8,128)S(1)}, u32[]{:S(2)}, u32[]{:S(2)}) %collective-permute-start.8) | collective-permute-done | bytes 12320 | tf_op jit(solution)/shard_map/ppermute | solution.py:788
  601.3 12.1 %fusion.2 = bf16[1792,1024]{1,0:T(8,128)(2,1)} fusion(bf16[1792,1024]{1,0:T(8,128)(2,1)} %collective-permute-done.1.refs_6_, bf16[1792,1024]{1,0:T(8,128)(2,1)} %get-tuple-element.28, bf16[7,256,1024]{2,1,0:T(8,128)(2,1)} %param.12, f32[1024]{0:T(1024)S(1)} %broadcast_add_fusion.2, bf16[1792,512]{1,0:T(8,128)(2,1)} %collective-permute-done.3, ...), kind=kOutput, calls=%fused_computation.3 | convolution fusion | flops 3784310784 | bytes 20451328 | tf_op jit(solution)/shard_map/dot_general | solution.py:808
  614.2 4.4 copy.87
  (134 shorter events, 45.9 us)
Async XLA Ops:
  7.2 209.0 %copy-start = (s32[7,5]{1,0:T(8,128)S(1)}, s32[7,5]{1,0:T(8,128)}, u32[]{:S(2)}) copy-start(s32[7,5]{1,0:T(8,128)} %param.22) | copy-start | bytes 424
  7.2 334.9 %reduce-scatter.4.cloned.1.call-start = ((), (), s32[]{:S(2)}) async-start(), calls=%async_computation.7 | async-start | bytes 4456448 | tf_op jit(solution)/shard_map/reduce_scatter | solution.py:804
  91.2 4.3 copy-start.7
  91.2 4.3 copy-start.25
  98.2 51.0 %copy-start.2 = (bf16[7,256,1024]{2,1,0:T(8,128)(2,1)S(1)}, bf16[7,256,1024]{2,1,0:T(8,128)(2,1)}, u32[]{:S(2)}) copy-start(bf16[7,256,1024]{2,1,0:T(8,128)(2,1)} %add_convert_fusion.refs_1_) | copy-start | bytes 11010052
  172.8 257.3 %reduce-scatter.6.cloned.1.call-start = ((), (), s32[]{:S(2)}) async-start(), calls=%async_computation.8 | async-start | bytes 4456448 | tf_op jit(solution)/shard_map/reduce_scatter | solution.py:804
  176.7 59.4 %all-to-all-start = ((bf16[8,256,256]{2,1,0:T(8,128)(2,1)}), bf16[8,256,256]{2,1,0:T(8,128)(2,1)S(1)}, u32[]{:S(2)}, u32[]{:S(2)}) async-start(bf16[8,256,256]{2,1,0:T(8,128)(2,1)} %concatenate.31), calls=%async_computation | async-start | bytes 2097152 | tf_op jit(solution)/shard_map/all_to_all | solution.py:776
  208.7 7.6 %copy-start.24 = (f32[3,512]{1,0:T(4,128)S(1)}, f32[3,512]{1,0:T(4,128)}, u32[]{:S(2)}) copy-start(f32[3,512]{1,0:T(4,128)} %param.16) | copy-start | bytes 18436
  211.8 43.3 %collective-permute-start = (bf16[7,128,1024]{2,1,0:T(8,128)(2,1)}, bf16[7,128,1024]{2,1,0:T(8,128)(2,1)}, u32[]{:S(2)}, u32[]{:S(2)}) collective-permute-start(bf16[7,128,1024]{2,1,0:T(8,128)(2,1)} %dynamic-slice_bitcast_fusion.2), channel_id=1, source_target_pairs={{0,1},{1,0},{2,3},{3,2},{4,5},{5,4},{6,7},{7,6},{8,9},{9,8},{10,11... | collective-permute-start | bytes 5505032 | tf_op jit(solution)/shard_map/ppermute | solution.py:741
  214.6 129.2 %collective-permute-start.2 = (bf16[1024,512]{1,0:T(8,128)(2,1)}, bf16[1024,512]{1,0:T(8,128)(2,1)}, u32[]{:S(2)}, u32[]{:S(2)}) collective-permute-start(bf16[1024,512]{1,0:T(8,128)(2,1)} %slice.56), channel_id=1, source_target_pairs={{0,1},{1,0},{2,3},{3,2},{4,5},{5,4},{6,7},{7,6},{8,9},{9,8},{10,11... | collective-permute-start | bytes 3145736 | tf_op jit(solution)/shard_map/ppermute | solution.py:741
  218.0 4.5 copy-start.9
  236.1 21.9 %copy-start.17 = (bf16[8,256,256]{2,1,0:T(8,128)(2,1)}, bf16[8,256,256]{2,1,0:T(8,128)(2,1)S(1)}, u32[]{:S(2)}) copy-start(bf16[8,256,256]{2,1,0:T(8,128)(2,1)S(1)} %all-to-all-done) | copy-start | bytes 3145732
  236.1 107.8 %all-to-all-start.1 = ((bf16[8,256,256]{2,1,0:T(8,128)(2,1)}), bf16[8,256,256]{2,1,0:T(8,128)(2,1)S(1)}, u32[]{:S(2)}, u32[]{:S(2)}) async-start(bf16[8,256,256]{2,1,0:T(8,128)(2,1)} %concatenate.32), calls=%async_computation.2 | async-start | bytes 2097152 | tf_op jit(solution)/shard_map/all_to_all | solution.py:776
  244.6 14.7 %copy-start.20 = (bf16[1792,1024]{1,0:T(8,128)(2,1)S(1)}, bf16[1792,1024]{1,0:T(8,128)(2,1)}, u32[]{:S(2)}) copy-start(bf16[1792,1024]{1,0:T(8,128)(2,1)} %get-tuple-element.28) | copy-start | bytes 11010052
  261.3 170.6 %collective-permute-start.1 = (bf16[1792,1024]{1,0:T(8,128)(2,1)}, bf16[1792,1024]{1,0:T(8,128)(2,1)}, u32[]{:S(2)}, u32[]{:S(2)}) collective-permute-start(bf16[1792,1024]{1,0:T(8,128)(2,1)} %broadcast_add_fusion), channel_id=1, source_target_pairs={{0,1},{1,0},{2,3},{3,2},{4,5},{5,4},{6,7},{7,6},{8,9},{9,8},{10,11... | collective-permute-start | bytes 11010056 | tf_op jit(solution)/shard_map/ppermute | solution.py:741
  261.9 73.4 %copy-start.12 = (bf16[1024,1024]{1,0:T(8,128)(2,1)S(1)}, bf16[1024,1024]{1,0:T(8,128)(2,1)}, u32[]{:S(2)}) copy-start(bf16[1024,1024]{1,0:T(8,128)(2,1)} %get-tuple-element.30.refs_0_) | copy-start | bytes 6291460
  344.8 62.9 %copy-start.19 = (bf16[2048,256]{1,0:T(8,128)(2,1)S(1)}, bf16[2048,256]{1,0:T(8,128)(2,1)}, u32[]{:S(2)}) copy-start(bf16[2048,256]{1,0:T(8,128)(2,1)} %get-tuple-element.36.refs_2_) | copy-start | bytes 3145732
  414.3 6.1 copy-start.15
  414.3 136.3 %all-to-all-start.2 = ((bf16[8,256,512]{1,2,0:T(8,128)(2,1)}), bf16[8,256,512]{1,2,0:T(8,128)(2,1)}, u32[]{:S(2)}, u32[]{:S(2)}) async-start(bf16[8,256,512]{1,2,0:T(8,128)(2,1)} %copy.73), calls=%async_computation.4 | async-start | bytes 4194304 | tf_op jit(solution)/shard_map/all_to_all | solution.py:780
  420.5 176.8 %reduce-scatter.8.cloned.1.call-start = ((), (), s32[]{:S(2)}) async-start(), calls=%async_computation.9 | async-start | bytes 3342336 | tf_op jit(solution)/shard_map/reduce_scatter | solution.py:804
  433.3 116.8 %copy-start.16 = (bf16[1024,768]{1,0:T(8,128)(2,1)S(1)}, bf16[1024,768]{1,0:T(8,128)(2,1)}, u32[]{:S(2)}) copy-start(bf16[1024,768]{1,0:T(8,128)(2,1)} %get-tuple-element.39.refs_3_) | copy-start | bytes 4718596
  550.6 6.6 %copy-start.23 = (f32[1,2048]{1,0:T(1,128)S(1)}, f32[1,2048]{1,0:T(1,128)}, u32[]{:S(2)}) copy-start(f32[1,2048]{1,0:T(1,128)} %get-tuple-element.44) | copy-start | bytes 24580
  550.7 11.8 %copy-start.26 = (f32[1024]{0:T(1024)S(1)}, f32[1024]{0:T(1024)}, u32[]{:S(2)}) copy-start(f32[1024]{0:T(1024)} %param.21) | copy-start | bytes 12292
  555.8 45.5 %collective-permute-start.3 = (bf16[1792,512]{1,0:T(8,128)(2,1)}, bf16[1792,512]{1,0:T(8,128)(2,1)}, u32[]{:S(2)}, u32[]{:S(2)}) collective-permute-start(bf16[1792,512]{1,0:T(8,128)(2,1)} %bitcast.114), channel_id=1, source_target_pairs={{0,1},{1,0},{2,3},{3,2},{4,5},{5,4},{6,7},{7,6},{8,9},{9,8},{10,11... | collective-permute-start | bytes 5505032 | tf_op jit(solution)/shard_map/ppermute | solution.py:741
  557.3 1.3 collective-permute-start.4
  558.5 3.9 collective-permute-start.5
  562.5 3.9 collective-permute-start.6
  566.4 12.9 %collective-permute-start.7 = (f32[52,128]{1,0:T(8,128)S(1)}, f32[52,128]{1,0:T(8,128)S(1)}, u32[]{:S(2)}, u32[]{:S(2)}) collective-permute-start(f32[52,128]{1,0:T(8,128)S(1)} %add.151), channel_id=1, source_target_pairs={{0,8},{2,10},{4,12},{6,14},{8,0},{10,2},{12,4},{14,6},{1,9},{3,11}... | collective-permute-start | bytes 79880 | tf_op jit(solution)/shard_map/ppermute | solution.py:788
  571.0 30.3 %copy-start.21 = (bf16[7,256,512]{2,1,0:T(8,128)(2,1)S(1)}, bf16[7,256,512]{2,1,0:T(8,128)(2,1)}, u32[]{:S(2)}) copy-start(bf16[7,256,512]{2,1,0:T(8,128)(2,1)} %copy.74) | copy-start | bytes 5505028
  572.4 41.0 %all-to-all-start.3 = ((bf16[16,64,512]{2,1,0:T(8,128)(2,1)}), bf16[16,64,512]{2,1,0:T(8,128)(2,1)S(1)}, u32[]{:S(2)}, u32[]{:S(2)}) async-start(bf16[16,64,512]{2,1,0:T(8,128)(2,1)} %bitcast.41), calls=%async_computation.6 | async-start | bytes 2097152 | tf_op jit(solution)/shard_map/all_to_all | solution.py:907
  579.3 17.4 %collective-permute-start.8 = (f32[24,128]{1,0:T(8,128)S(1)}, f32[24,128]{1,0:T(8,128)S(1)}, u32[]{:S(2)}, u32[]{:S(2)}) collective-permute-start(f32[24,128]{1,0:T(8,128)S(1)} %slice.77), channel_id=1, source_target_pairs={{0,1},{1,0},{2,3},{3,2},{4,5},{5,4},{6,7},{7,6},{8,9},{9,8},{10,11... | collective-permute-start | bytes 36872 | tf_op jit(solution)/shard_map/ppermute | solution.py:788
  614.2 4.4 copy-start.1
  (11 other events, 29.3 us)
Sparse Core Ops, SparseCore 0:
  172.9 111.5 reduce-scatter.3
  288.8 71.4 reduce-scatter.5
  428.3 90.3 reduce-scatter.7

commit v4 on v3

--- a/solution.py
+++ b/solution.py
@@ -320,7 +320,7 @@
     pl.semaphore_wait(barrier, len(others))
 
 
-def gather_kernel(x_ref, out_ref, local_sem, recv, up, down, across, over):
+def gather_kernel(x_ref, tok_ref, gain_ref, bias_ref, out_ref, hid_ref, local_sem, recv, up, down, across, over):
     size = x_ref.shape[0]
     core, block = lax.axis_index("dp"), lax.axis_index("blk")
     z, y = block // 2, lax.rem(block, 2)
@@ -367,6 +367,12 @@
     copy(x_ref, mine, across.at[z], beside).start()
     copy(x_ref, mine, over.at[z * 2 + y], sibling).start()
     keep.start()
+
+    for r in range(tok_ref.shape[0]):
+        x = tok_ref[r].astype(F32)
+        x = x - jnp.mean(x, -1, keepdims=True)
+        x = x * lax.rsqrt(jnp.mean(x * x, -1, keepdims=True) + EPSILON)
+        hid_ref[r] = (x * gain_ref[...] + bias_ref[...]).astype(BF)
 
     def from_beside(zz):
         at = place(core, zz, 1 - y)
@@ -398,21 +404,27 @@
         pl.when((zz >= z) & (z > 0))(lambda: copy(x_ref, mine, down.at[zz], below).wait_send())
 
 
-def gather_weights(shard):
+def gather_weights(shard, tokens, gain, bias):
     cores, blocks = lax.axis_size("dp"), lax.axis_size("blk")
     rows, columns = shard.shape
     dma = pltpu.SemaphoreType.DMA
+    hbm, vmem = pl.BlockSpec(memory_space=pl.ANY), pl.BlockSpec(memory_space=pltpu.VMEM)
     return pl.pallas_call(
         gather_kernel,
-        out_shape=jax.ShapeDtypeStruct((cores * blocks * rows, columns), shard.dtype),
-        in_specs=[pl.BlockSpec(memory_space=pl.ANY)],
-        out_specs=pl.BlockSpec(memory_space=pl.ANY),
+        out_shape=[
+            jax.ShapeDtypeStruct((cores * blocks * rows, columns), shard.dtype),
+            jax.ShapeDtypeStruct(tokens.shape, BF),
+        ],
+        in_specs=[hbm, vmem, vmem, vmem],
+        out_specs=[hbm, vmem],
         scratch_shapes=[
             dma, dma((cores * blocks,)), dma((blocks // 2,)), dma((blocks // 2,)),
             dma((blocks // 2,)), dma((blocks,)),
         ],
-        compiler_params=pltpu.CompilerParams(collective_id=0, has_side_effects=True),
-    )(shard)
+        compiler_params=pltpu.CompilerParams(
+            collective_id=0, has_side_effects=True, vmem_limit_bytes=32 * MIB
+        ),
+    )(shard, tokens, gain, bias)
 
 
 class RowTransfer:
@@ -499,15 +511,26 @@
 
 
 def tail_kernel(groups, waits, *refs):
-    g_mine, g_other = refs[:groups], refs[groups:2 * groups]
-    (w_ref, tok_ref, cot_ref, add_ref, gain_ref, out_ref, sum_ref,
-     sent, got, home_send, home, grads, a_send, a_recv, b_send, b_recv, c_send, c_recv, c_local) = refs[2 * groups + waits:]
+    g_mine, g_other, heads = refs[:groups], refs[groups:2 * groups], refs[2 * groups:3 * groups]
+    (w_ref, tok_ref, cot_ref, add_ref, gain_ref, extra_ref, out_ref, sum_ref, wgrad_ref, mixed_ref, facing_ref,
+     sent, got, home_send, home, grads, mix, total, terms, inbox, norms, small, small_in, small_box, small_out,
+     a_send, a_recv, b_send, b_recv, c_send, c_recv, c_local, d_send, d_recv, e_send, e_recv, e_local,
+     f_send, f_recv, g_send, g_recv, h_send, h_recv, i_send, i_recv) = refs[3 * groups + waits:]
     rows, part, model = tok_ref.shape
     block, half = lax.axis_index("blk"), lax.axis_index("tensor")
     blocks = lax.axis_size("blk")
     facing = {"tensor": 1 - half}
     has_row = block < rows
-    meet([{"blk": lax.rem(block + n, blocks)} for n in range(1, blocks)] + [facing])
+    count = lax.axis_size("dp") * blocks
+    me = lax.axis_index("dp") * blocks + block
+
+    def peers():
+        return [lax.rem(me + n, count) for n in range(1, count)]
+
+    def device(j):
+        return {"dp": j // blocks, "blk": lax.rem(j, blocks)}
+
+    meet([device(j) for j in peers()] + [facing])
 
     def product(parts, s):
         at, total, first = pl.ds(pl.multiple_of(s * part, part), part), None, 0
@@ -532,27 +555,54 @@
     def keep(r):
         return pltpu.make_async_copy(grads.at[r], own_half(out_ref, r), c_local.at[r])
 
+    def heads_of(ref, k, r):
+        wide = heads[k].shape[1]
+        return ref.at[r, :, k * wide:(k + 1) * wide]
+
+    def attended(k, s):
+        return heads[k].at[pl.ds(pl.multiple_of(s * 2 * part, 2 * part), 2 * part)]
+
+    def heads_home(k, s):
+        return remote(attended(k, s), heads_of(mix, k, block), d_send.at[k * blocks + s],
+                      d_recv.at[k * blocks + block], {"blk": s})
+
+    def own_heads(k):
+        return pltpu.make_async_copy(attended(k, block), heads_of(mix, k, block), d_send.at[k * blocks + block])
+
+    def heads_across(k, r):
+        return remote(heads_of(mix, k, r), heads_of(facing_ref, k, r), e_send.at[k * blocks + r],
+                      e_recv.at[k * blocks + r], facing)
+
     @pl.when(has_row)
     def _():
         for n in range(blocks):
             s = lax.rem(block + n, blocks)
             sent[s] = product(g_other, s).astype(BF)
             across(s).start()
-
-    sum_ref[...] = jnp.zeros_like(sum_ref)
+            for k in range(groups):
+                if n == 0:
+                    own_heads(k).start()
+                else:
+                    heads_home(k, s).start()
+
+    def keep_heads(r):
+        return pltpu.make_async_copy(mix.at[r], mixed_ref.at[r], e_local.at[r])
+
+    norms[...] = jnp.zeros_like(norms)
+    total[...] = jnp.zeros_like(total)
 
     def forward(n):
         s = lax.rem(block + n, blocks)
 
         @pl.when(has_row)
         def _():
-            total = product(g_mine, s)
+            grad = product(g_mine, s)
             across(s).wait_recv()
-            total = (total + got[s].astype(F32)).astype(BF)
+            grad = (grad + got[s].astype(F32)).astype(BF)
             if n == 0:
-                home[s] = total
+                home[s] = grad
             else:
-                home_send[s] = total
+                home_send[s] = grad
                 homeward(s).start()
 
     def norm(n):
@@ -560,6 +610,14 @@
 
         @pl.when(r < rows)
         def _():
+            for k in range(groups):
+                if n:
+                    here = heads_of(mix, k, r)
+                    remote(here, here, e_send.at[k * blocks + r], d_recv.at[k * blocks + r], facing).wait_recv()
+                else:
+                    own_heads(k).wait()
+                heads_across(k, r).start()
+            keep_heads(r).start()
             if n:
                 remote(home_send.at[r], home.at[r], b_send.at[r], b_recv.at[r], facing).wait_recv()
             grad = home[r].astype(F32) + add_ref[r].astype(F32)
@@ -567,13 +625,15 @@
             x = x - jnp.mean(x, -1, keepdims=True)
             scale = lax.rsqrt(jnp.mean(x * x, -1, keepdims=True) + EPSILON)
             x = x * scale
-            sum_ref[0:1, :] += jnp.sum(grad * x, 0, keepdims=True)
-            sum_ref[1:2, :] += jnp.sum(grad, 0, keepdims=True)
+            norms[0:1, :] += jnp.sum(grad * x, 0, keepdims=True)
+            norms[1:2, :] += jnp.sum(grad, 0, keepdims=True)
             grad = grad * gain_ref[...]
             grad = grad - jnp.mean(grad, -1, keepdims=True) - x * jnp.mean(grad * x, -1, keepdims=True)
-            grads[r] = (cot_ref[r].astype(F32) + scale * grad).astype(BF)
+            own = cot_ref[r, pl.ds(pl.multiple_of(half * part, part), part), :]
+            grads[r] = (own.astype(F32) + scale * grad).astype(BF)
             share(r).start()
             keep(r).start()
+            total[...] += nn(cot_ref[r].T, mix[r])
 
     lag = 2
     for n in range(blocks + lag):
@@ -582,9 +642,68 @@
         if n >= lag:
             norm(n - lag)
 
+    size = terms.shape[1]
+    for j in range(count):
+        terms[j] = total[j * size:(j + 1) * size].astype(BF)
+
+    def term(j):
+        return remote(terms.at[j], inbox.at[me], f_send.at[j], f_recv.at[me], device(j))
+
+    for j in peers():
+        term(j).start()
+
+    small[...] = extra_ref[...]
+    lines = norms.shape[1] // LANES
+    for n in range(2):
+        for k in range(lines):
+            small[n * lines + k:n * lines + k + 1, :] = norms[n:n + 1, k * LANES:(k + 1) * LANES]
+    shared = small.at[pl.ds(0, 3 * lines)]
+    swapped = remote(shared, small_in, g_send, g_recv, facing)
+    swapped.start()
+    swapped.wait()
+    small[:3 * lines, :] += small_in[...]
+
+    def line(ref, j):
+        return ref.at[pl.ds(pl.multiple_of(j * 8, 8), 8)]
+
+    def small_term(j):
+        return remote(line(small, j), small_box.at[me], h_send.at[j], h_recv.at[me], device(j))
+
+    def small_sum(j):
+        return remote(line(small_out, me), line(small_out, me), i_send.at[j], i_recv.at[me], device(j))
+
+    for j in peers():
+        small_term(j).start()
+    small_box[me] = small[pl.ds(pl.multiple_of(me * 8, 8), 8), :]
+    for j in peers():
+        remote(small_box.at[j], small_box.at[j], h_send.at[j], h_recv.at[j], device(j)).wait_recv()
+    added = small_box[0]
+    for j in range(1, count):
+        added = added + small_box[j]
+    small_out[pl.ds(pl.multiple_of(me * 8, 8), 8), :] = added
+    for j in peers():
+        small_sum(j).start()
+    inbox[me] = terms[me]
+    for j in peers():
+        remote(inbox.at[j], inbox.at[j], f_send.at[j], f_recv.at[j], device(j)).wait_recv()
+    added = inbox[0].astype(F32)
+    for j in range(1, count):
+        added = added + inbox[j].astype(F32)
+    wgrad_ref[...] = added
+    for j in peers():
+        remote(line(small_out, j), line(small_out, j), i_send.at[j], i_recv.at[j], device(j)).wait_recv()
+    sum_ref[...] = small_out[...]
+    for j in peers():
+        term(j).wait_send()
+        small_term(j).wait_send()
+        small_sum(j).wait_send()
+
     for r in range(rows):
         share(r).wait()
         keep(r).wait()
+        keep_heads(r).wait()
+        for k in range(groups):
+            heads_across(k, r).wait()
 
     @pl.when(has_row)
     def _():
@@ -592,28 +711,41 @@
             across(s).wait_send()
         for n in range(1, blocks):
             homeward(lax.rem(block + n, blocks)).wait_send()
-
-
-def input_grads(g_mine, g_other, weights, tokens, cot, add, gain, waits=()):
+            for k in range(groups):
+                heads_home(k, lax.rem(block + n, blocks)).wait_send()
+
+
+def go_home(g_mine, g_other, attended, weights, tokens, cot, add, gain, extra, waits=()):
     rows, part, model = tokens.shape
     blocks = lax.axis_size("blk")
     wide = sum(g.shape[1] for g in g_mine)
     dma = pltpu.SemaphoreType.DMA
+    groups, hbm = len(g_mine), pl.BlockSpec(memory_space=pl.ANY)
+    count = lax.axis_size("dp") * blocks
+    wide_heads = sum(o.shape[1] for o in attended)
+    lines = 3 * model // LANES
+    heads = jax.ShapeDtypeStruct((rows, 2 * part, wide_heads), BF)
     vmem = pl.BlockSpec(memory_space=pltpu.VMEM)
     return pl.pallas_call(
-        functools.partial(tail_kernel, len(g_mine), len(waits)),
+        functools.partial(tail_kernel, groups, len(waits)),
         grid=(1,),
-        out_shape=[jax.ShapeDtypeStruct((rows, 2 * part, model), BF), jax.ShapeDtypeStruct((8, model), F32)],
-        in_specs=[vmem] * (2 * len(g_mine)) + [pl.BlockSpec(memory_space=pl.ANY)] * len(waits)
-        + [pl.BlockSpec((model, wide), lambda i: (0, 0))] + [vmem] * 4,
-        out_specs=[pl.BlockSpec(memory_space=pl.ANY), vmem],
+        out_shape=[jax.ShapeDtypeStruct((rows, 2 * part, model), BF), jax.ShapeDtypeStruct((8 * count, LANES), F32),
+                   jax.ShapeDtypeStruct((model // count, wide_heads), F32), heads, heads],
+        in_specs=[vmem] * (2 * groups) + [hbm] * (groups + len(waits))
+        + [pl.BlockSpec((model, wide), lambda i: (0, 0))] + [vmem] * 5,
+        out_specs=[hbm, vmem, vmem, hbm, hbm],
         scratch_shapes=[pltpu.VMEM((blocks, part, model), BF)] * 4 + [pltpu.VMEM((rows, part, model), BF)]
-        + [dma((blocks,))] * 4 + [dma((rows,))] * 3,
+        + [pltpu.VMEM(heads.shape, BF), pltpu.VMEM((model, wide_heads), F32)]
+        + [pltpu.VMEM((count, model // count, wide_heads), BF)] * 2
+        + [pltpu.VMEM((8, model), F32), pltpu.VMEM((8 * count, LANES), F32), pltpu.VMEM((lines, LANES), F32)]
+        + [pltpu.VMEM((count, 8, LANES), F32), pltpu.VMEM((8 * count, LANES), F32)]
+        + [dma((blocks,))] * 4 + [dma((rows,))] * 3 + [dma((groups * blocks,))] * 4 + [dma((rows,))]
+        + [dma((count,))] * 2 + [dma] * 2 + [dma((count,))] * 4,
         compiler_params=pltpu.CompilerParams(
-            collective_id=1, has_side_effects=True, vmem_limit_bytes=48 * MIB
+            collective_id=1, has_side_effects=True, vmem_limit_bytes=56 * MIB
         ),
         cost_estimate=pl.CostEstimate(flops=1000, bytes_accessed=1000, transcendentals=0),
-    )(*g_mine, *g_other, *waits, weights, tokens, cot, add, gain)
+    )(*g_mine, *g_other, *attended, *waits, weights, tokens, cot, add, gain, extra)
 
 
 def weight_grad_kernel(half, waits, a_ref, b_ref, *refs):
@@ -820,15 +952,16 @@
 
     mine = lax.axis_index("tensor")
     pair = parts == 2 and (lax.axis_size("dp"), blocks) == (2, 8)
-    hidden = (normalize(tokens.astype(F32))[0] * ln_gain + ln_bias).astype(BF)
-    flat_hidden, cot = hidden.reshape(count, model), cotangent.reshape(count, model)
+    cot = cotangent.reshape(count, model)
 
     shard = jnp.concatenate([by_pair(w_qkv, width), w_out.T, w_fc, w_proj.T], 1)
     if pair:
-        weights = gather_weights(shard)
+        weights, hidden = gather_weights(shard, tokens, ln_gain[None], ln_bias[None])
     else:
+        hidden = (normalize(tokens.astype(F32))[0] * ln_gain + ln_bias).astype(BF)
         weights = lax.all_gather(shard, ("dp", "blk"), axis=0, tiled=True)
         row_hidden = [join_parts(to_rows(part_of(hidden, 1, mine)), 1).reshape(length, model)]
+    flat_hidden = hidden.reshape(count, model)
     full_qkv, full_out = weights[:, :3 * width], weights[:, 3 * width:4 * width]
 
     row_bounds = lax.dynamic_index_in_dim(
@@ -841,20 +974,19 @@
     wide = width // groups
     cuts = [slice(n * wide, (n + 1) * wide) for n in range(groups)]
     grad_mixed = dot(cot, full_out).astype(BF).reshape(rows, group, width)
+    row_grads = [to_rows(grad_mixed[:, :, cut]).reshape(length, wide) for cut in cuts]
 
     activated, grad_inner, mlp_out, mlp_back, grad_bfc, *moved = mlp(
         flat_hidden, cot, weights, 4 * width // inner, b_fc[None], (grad_mixed,), hidden if pair else None
     )
-    grad_mixed += grad_inner[0, 0] * 0
-    row_grads = [to_rows(grad_mixed[:, :, cut]).reshape(length, wide) for cut in cuts]
     row_hidden = moved or row_hidden
     mlp_back = sum_parts(mlp_back.reshape(rows, group, model), 1)
-    grad_fc, grad_proj = weight_grads(flat_hidden, grad_inner, cot, activated)
+    grad_fc, grad_proj = weight_grads(flat_hidden, grad_inner, cot, activated, [row_grads[0]])
     grad_fc_sum, grad_proj_sum = scatter(grad_fc), scatter(grad_proj)
     if pair:
         mlp_back = mlp_back.astype(BF)
         other_out = swap(full_out)
-        other_mlp = swap(mlp_out + mlp_back[0, 0, 0] * 0)
+        other_mlp = swap(mlp_out)
 
     bias = by_pair(b_qkv[None], width)
     own_tokens, own_cot = part_of(tokens, 1, mine), part_of(cotangent, 1, mine)
@@ -868,26 +1000,31 @@
         attended.append(out)
         grad_packed.append(grads)
         grad_qkv.append(sum(dot(h.T, g) for h, g in zip(row_hidden, grads)).astype(BF))
-        waits = [out, grad_fc_sum, mlp_back]
-        if pair:
-            waits.append(other_out)
-    mixed = to_blocks(jnp.concatenate(attended, 1).reshape(blocks, group, width), rows).reshape(count, width)
+        waits = [out, grad_fc_sum]
     grad_bqkv = jnp.concatenate([sum(jnp.sum(g.astype(F32), 0) for g in grads) for grads in grad_packed])
     grad_qkv = jnp.concatenate(grad_qkv, 1)
     grad_qkv_sum = scatter(grad_qkv)
 
+    tensor_sums = jnp.sum(own_cot.astype(F32), (0, 1)).reshape(-1, LANES)
+    bias_sums = jnp.concatenate([grad_bfc[0], grad_bqkv]).reshape(-1, LANES)
+    lines = model // LANES
     if pair:
-        grad_tokens, norm_sums = input_grads(
-            [g[0] for g in grad_packed], [g[1] for g in grad_packed], weights, own_tokens, own_cot, mlp_back,
-            ln_gain[None], [grad_qkv, grad_proj_sum, other_mlp],
+        used = 3 * lines + bias_sums.shape[0]
+        extra = jnp.zeros((8 * (model // shard.shape[0]), LANES), F32)
+        extra = extra.at[2 * lines:3 * lines].set(tensor_sums).at[3 * lines:used].set(bias_sums)
+        grad_tokens, sums, grad_out_sum, mixed, other_mixed = go_home(
+            [g[0] for g in grad_packed], [g[1] for g in grad_packed], attended, weights, own_tokens, cotangent,
+            mlp_back, ln_gain[None], extra, [grad_qkv, grad_proj_sum, other_mlp, other_out],
         )
-        norm_sums = norm_sums[:2]
+        norm_sums, bias_sums = sums[:3 * lines].reshape(3, model), sums[3 * lines:used].reshape(-1)
+        mixed, other_mixed = mixed.reshape(count, width), other_mixed.reshape(count, width)
         branches = mlp_out.astype(F32) + other_mlp.astype(F32)
-        branches += tokens.reshape(count, model).astype(F32) + (b_out + norm_sums[0, 0] * 0)
-        branches += dot(jnp.concatenate([mixed, swap(mixed)], 1), jnp.concatenate([full_out, other_out], 1).T)
+        branches += tokens.reshape(count, model).astype(F32) + b_out
+        branches += nt(mixed, full_out) + nt(other_mixed, other_out)
         result = branches.astype(BF).reshape(rows, group, model)
-        norm_sums = norm_sums + mixed[0, 0].astype(F32) * 0
     else:
+        mixed = jnp.concatenate(attended, 1).reshape(blocks, group, width)
+        mixed = to_blocks(mixed, rows).reshape(count, width)
         grads = jnp.concatenate([g[0] for g in grad_packed], 1)
         back = sum_parts(nt(grads, full_qkv).reshape(blocks, group, model), 1).astype(BF)
         grad_hidden = mlp_back + to_blocks(back, rows).astype(F32)
@@ -902,26 +1039,24 @@
             - normal * jnp.mean(grad_normal * normal, -1, keepdims=True)
         )
         grad_tokens = join_parts((own_cot.astype(F32) + grad_inputs).astype(BF), 1)
-        norm_sums = jnp.stack([jnp.sum(grad_hidden * normal, (0, 1)), jnp.sum(grad_hidden, (0, 1))])
-
-    grad_out = lax.all_to_all(dot(cot.T, mixed).astype(BF), ("dp", "blk"), 0, 0, tiled=True)
-    grad_out_sum = jnp.sum(grad_out.reshape(-1, shard.shape[0], width).astype(F32), 0)
-
-    norm_sums = jnp.concatenate([norm_sums, jnp.sum(own_cot.astype(F32), (0, 1))[None]]).reshape(-1, LANES)
-    sums = jnp.concatenate([norm_sums, grad_bqkv.reshape(-1, LANES), grad_bfc.reshape(-1, LANES)], 0)
-    sums = sum_all(sums, ("dp", "blk"))
-    bias_sums = sums[norm_sums.shape[0]:].reshape(-1)
-    norm_sums = sum_all(sums[:norm_sums.shape[0]], ("tensor",)).reshape(3, model)
+        norm_sums = jnp.concatenate([jnp.sum(grad_hidden * normal, (0, 1)), jnp.sum(grad_hidden, (0, 1))])
+        sums = jnp.concatenate([norm_sums.reshape(-1, LANES), tensor_sums, bias_sums], 0)
+        sums = sum_all(sums, ("dp", "blk"))
+        norm_sums = sum_all(sums[:3 * lines], ("tensor",)).reshape(3, model)
+        bias_sums = sums[3 * lines:].reshape(-1)
+        grad_out = lax.all_to_all(dot(cot.T, mixed).astype(BF), ("dp", "blk"), 0, 0, tiled=True)
+        grad_out_sum = jnp.sum(grad_out.reshape(-1, shard.shape[0], width).astype(F32), 0)
+
     return (
         result,
         grad_tokens,
         norm_sums[0],
         norm_sums[1],
         by_kind(grad_qkv_sum, width),
-        by_kind(bias_sums[None, :3 * width], width)[0],
+        by_kind(bias_sums[None, inner:], width)[0],
         grad_out_sum.T,
         grad_fc_sum,
-        bias_sums[3 * width:],
+        bias_sums[:inner],
         grad_proj_sum.T,
         norm_sums[2],
     )

time: 629 us -> 621 us (0.987)
  Pallas kernels: 401 us -> 445 us
  waiting for transfers between devices: 44.4 us -> 16.9 us
  other arithmetic: 29.9 us -> 17.5 us
  matrix products: 33.6 us -> 24.9 us
    pallas_call x2, Pallas kernels: 190 us -> 244 us  [the longest x1 172 us: go_home(): pl.pallas_call(functools.partial(tail_kernel, groups, len(waits)), grid=(...]
    ppermute x5 -> x0, waiting for transfers between devices: 22.5 us -> none  [sum_all(): lax.ppermute(value, axis, [(i, i ^ step) for i in range(size)])]
    dot_general x7 -> x5, matrix products: 33.6 us -> 14.4 us  [dot(): return jnp.dot(a, b, preferred_element_type=F32)]
    all_to_all x2 -> x0, starting transfers between devices: 13 us -> none  [the longest x1 6.86 us: local(): lax.all_to_all(dot(cot.T, mixed).astype(BF), ('dp', 'blk'), 0, 0, tiled=T...]
    pallas_call x2, Pallas kernels: 136 us -> 124 us  [attention(): pl.pallas_call(functools.partial(attn_kernel, bq, bk, part, len(waits)),...]
    all_to_all x2, starting transfers between devices: 40.6 us -> 51.2 us  [to_rows(): lax.all_to_all(jnp.concatenate([value, pad], 0), 'blk', 0, 0, tiled=True)]
    all_to_all x2, waiting for transfers between devices: 10.6 us -> 0.01 us  [to_rows(): lax.all_to_all(jnp.concatenate([value, pad], 0), 'blk', 0, 0, tiled=True)]
    dot_general x0 -> x2, matrix products: none -> 10.5 us  [nt(): lax.dot_general(a, b, (((1,), (1,)), ((), ())), preferred_element_type=F32)]
  transfers between devices with their start and end apart: 16 -> 8, of which waited for: 6 -> 1; matrix products, arithmetic and copies ran while one was open for 12% -> 8% of each run, Pallas kernels for 40% -> 57%
where the time goes in v4:
time: 621 us; the launch traced here: 611 us
  Pallas kernels  445 us (72%)
  starting transfers between devices  54.5 us (9%)
  local copies, waits for them, and re-layouts  37.8 us (6%)
  matrix products  24.9 us (4%)
  other arithmetic  17.5 us (3%)
  waiting for transfers between devices  16.9 us (3%)
  between operations  14.4 us (2%)
    pallas_call x1, Pallas kernels, go_home(): pl.pallas_call(functools.partial(tail_kernel, groups, len(waits)), grid=(...  172 us
    pallas_call x2, Pallas kernels, attention(): pl.pallas_call(functools.partial(attn_kernel, bq, bk, part, len(waits)),...  124 us
    pallas_call x1, Pallas kernels, gather_weights(): pl.pallas_call(gather_kernel, out_shape=[jax.ShapeDtypeStruct((cores * bl...  72.4 us
    pallas_call x1, Pallas kernels, mlp(): pl.pallas_call(functools.partial(mlp_kernel, tile, len(waits), len(moves)...  53.2 us
    all_to_all x2, starting transfers between devices, to_rows(): lax.all_to_all(jnp.concatenate([value, pad], 0), 'blk', 0, 0, tiled=True)  51.2 us
    pallas_call x1, Pallas kernels, weight_grads(): pl.pallas_call(functools.partial(weight_grad_kernel, half, len(waits)), g...  23.5 us
    unnamed x64, local copies, waits for them, and re-layouts  17.5 us
    ppermute x3, waiting for transfers between devices, swap(): return lax.ppermute(value, 'tensor', [(0, 1), (1, 0)])  16.2 us
  transfers between devices with their start and end apart: 8, of which 1 were waited for; matrix products, arithmetic and copies ran while one was open for 8% of the time, Pallas kernels for 57%

profile of v4, /device:TPU:28, one launch (start us, length us, event | category | flops | bytes accessed | tf_op | source)
XLA Modules:
  0.0 611.3 jit_solution(345153369588686943)
XLA Ops:
  9.7 2.0 copy-done.6
  11.7 72.4 %shard_map.203 = (bf16[1024,6144]{1,0:T(8,128)(2,1)S(1)}, bf16[7,256,1024]{2,1,0:T(8,128)(2,1)S(1)}) custom-call(bf16[64,6144]{1,0:T(8,128)(2,1)S(1)} %pad_maximum_fusion.1.x_ref, bf16[7,256,1024]{2,1,0:T(8,128)(2,1)S(1)} %copy-done.6, f32[1,1024]{1,0:T(1,128)S(1)} %bitcast.87, f32[1,1024]{1,0:T(1,128)S(1)} %bitcast.88), custom_call_target="tpu_custom_call" | custom-call | tf_op jit(solution)/shard_map/pallas_call | solution.py:412
  84.2 1.8 copy-done.3
  86.0 4.5 copy-done.2
  90.5 3.4 fusion.4
  93.9 2.8 copy.56
  98.3 7.6 %all-to-all-start = ((bf16[8,256,256]{2,1,0:T(8,128)(2,1)}), bf16[8,256,256]{2,1,0:T(8,128)(2,1)S(1)}, u32[]{:S(2)}, u32[]{:S(2)}) async-start(bf16[8,256,256]{2,1,0:T(8,128)(2,1)} %concatenate.20), calls=%async_computation | async-start | bytes 2097152 | tf_op jit(solution)/shard_map/all_to_all | solution.py:908
  106.4 53.2 %shard_map.204 = (bf16[1792,2048]{1,0:T(8,128)(2,1)}, bf16[1792,2048]{1,0:T(8,128)(2,1)}, bf16[1792,1024]{1,0:T(8,128)(2,1)}, bf16[1792,1024]{1,0:T(8,128)(2,1)}...) custom-call(bf16[1792,1024]{1,0:T(8,128)(2,1)} %bitcast.80, ...), custom_call_target="tpu_custom_call" | custom-call | flops 1000 | bytes 1000 | tf_op jit(solution)/shard_map/pallas_call | solution.py:853
  159.7 2.4 copy-done.4
  162.1 23.5 %shard_map.205 = (bf16[1024,2048]{1,0:T(8,128)(2,1)}, bf16[1024,2048]{1,0:T(8,128)(2,1)}) custom-call(bf16[1792,1024]{1,0:T(8,128)(2,1)S(1)} %bitcast.81, bf16[1792,1024]{1,0:T(8,128)(2,1)} %bitcast.90, bf16[2048,256]{1,0:T(8,128)(2,1)S(1)} %bitcast.82, bf16[1792,2048]{1,0:T(8,128)(2,1)} %get-tuple-element.62.refs_1_, ...), custom_call_target="tpu_custom_call" | custom-call | flops 1000 | bytes 1000 | tf_op jit(solution)/shard_map/pallas_call | solution.py:778
  187.4 43.6 %all-to-all-start.1 = ((bf16[8,256,256]{2,1,0:T(8,128)(2,1)}), bf16[8,256,256]{2,1,0:T(8,128)(2,1)S(1)}, u32[]{:S(2)}, u32[]{:S(2)}) async-start(bf16[8,256,256]{2,1,0:T(8,128)(2,1)} %concatenate.21), calls=%async_computation.2 | async-start | bytes 2097152 | tf_op jit(solution)/shard_map/all_to_all | solution.py:908
  231.0 3.0 dynamic-slice_bitcast_fusion
  234.6 1.5 collective-permute-start
  237.5 3.9 convert_reduce_fusion
  241.4 1.4 dynamic-slice_bitcast_fusion.2.refs_3_.refs_11_
  244.3 60.1 %shard_map.206 = (bf16[2048,256]{1,0:T(8,128)(2,1)}, bf16[1024,768]{1,0:T(8,128)(2,1)}, bf16[1024,768]{1,0:T(8,128)(2,1)}) custom-call(s32[4]{0:T(128)} %get-tuple-element.80.lo_ref, s32[4]{0:T(128)} %get-tuple-element.79.hi_ref, bf16[1024,1024]{1,0:T(8,128)(2,1)} %get-tuple-element.60.refs_0_, bf16[1024,1024]{1,0:T(8,128)(2,1)} %get-tuple-element.61.refs_1_, ...), custom_call_target="tpu_custom_call" | custom-call | flops 1000 | bytes 1000 | tf_op jit(solution)/shard_map/pallas_call | solution.py:274
  304.4 3.5 fusion.11
  307.9 2.0 add_convert_fusion.1
  310.0 1.8 convert_element_type.92.refs_3_
  312.8 64.1 %shard_map.207 = (bf16[2048,256]{1,0:T(8,128)(2,1)}, bf16[1024,768]{1,0:T(8,128)(2,1)}, bf16[1024,768]{1,0:T(8,128)(2,1)}) custom-call(s32[4]{0:T(128)} %get-tuple-element.80.lo_ref, s32[4]{0:T(128)} %get-tuple-element.79.hi_ref, bf16[1024,1024]{1,0:T(8,128)(2,1)} %get-tuple-element.60.refs_0_, bf16[1024,1024]{1,0:T(8,128)(2,1)} %get-tuple-element.61.refs_1_, ...), custom_call_target="tpu_custom_call" | custom-call | flops 1000 | bytes 1000 | tf_op jit(solution)/shard_map/pallas_call | solution.py:274
  376.9 3.5 fusion.12
  380.4 2.0 add_convert_fusion
  382.4 1.9 pad_maximum_fusion.refs_6_
  384.4 2.4 slice.71
  388.1 3.5 fusion.3.refs_13_
  392.5 2.0 convert_bitcast_fusion
  394.5 16.2 %collective-permute-done.1.refs_9_ = bf16[1024,512]{1,0:T(8,128)(2,1)} collective-permute-done((bf16[1024,512]{1,0:T(8,128)(2,1)}, bf16[1024,512]{1,0:T(8,128)(2,1)}, u32[]{:S(2)}, u32[]{:S(2)}) %collective-permute-start.1) | collective-permute-done | bytes 1048608 | tf_op jit(solution)/shard_map/ppermute | solution.py:873
  410.7 172.0 %shard_map.208 = (bf16[7,256,1024]{2,1,0:T(8,128)(2,1)}, f32[128,128]{1,0:T(8,128)}, f32[64,512]{1,0:T(8,128)}, bf16[7,256,512]{2,1,0:T(8,128)(2,1)}, bf16[7,256,512]{2,1,0:T(8,128)(2,1)}) custom-call(bf16[1024,768]{1,0:T(8,128)(2,1)} %get-tuple-element.65.refs_0_, bf16[1024,768]{1,0:T(8,128)(2,1)} %get-tuple-element.67.refs_1_, ...), custom_call_target="tpu_custom_call" | custom-call | flops 1000 | bytes 1000 | tf_op jit(solution)/shard_map/pallas_call | solution.py:729
  584.0 1.3 slice_bitcast_fusion.1
  586.6 4.0 fusion.13
  590.7 6.4 %fusion.2 = bf16[1792,1024]{1,0:T(8,128)(2,1)} fusion(bf16[1792,1024]{1,0:T(8,128)(2,1)S(1)} %bitcast.85, f32[1792,1024]{1,0:T(8,128)S(1)} %fusion.13, bf16[1792,1024]{1,0:T(8,128)(2,1)} %collective-permute-done.refs_8_, bf16[1792,1024]{1,0:T(8,128)(2,1)} %get-tuple-element.59, bf16[1792,512]{1,0:T(8,128)(2,1)S(1)} %bitcast.110, f32[1024]{0:T(1024)S(1)} %copy-done.30, ...), kind=kOutput, calls=%fused_computation.3 | convolution fusion | flops 1895563264 | bytes 24907776 | tf_op jit(solution)/shard_map/dot_general | solution.py:20
  599.4 4.5 copy.78
  (102 shorter events, 18.6 us)
Async XLA Ops:
  7.2 228.9 %copy-start = (s32[7,5]{1,0:T(8,128)S(1)}, s32[7,5]{1,0:T(8,128)}, u32[]{:S(2)}) copy-start(s32[7,5]{1,0:T(8,128)} %param.26) | copy-start | bytes 424
  7.2 2.5 copy-start.9
  11.7 78.8 %copy-start.11 = (bf16[7,256,1024]{2,1,0:T(8,128)(2,1)S(1)}, bf16[7,256,1024]{2,1,0:T(8,128)(2,1)}, u32[]{:S(2)}) copy-start(bf16[7,256,1024]{2,1,0:T(8,128)(2,1)} %refs_12_.1) | copy-start | bytes 11010052
  86.0 4.5 copy-start.2
  98.3 61.3 %all-to-all-start = ((bf16[8,256,256]{2,1,0:T(8,128)(2,1)}), bf16[8,256,256]{2,1,0:T(8,128)(2,1)S(1)}, u32[]{:S(2)}, u32[]{:S(2)}) async-start(bf16[8,256,256]{2,1,0:T(8,128)(2,1)} %concatenate.20), calls=%async_computation | async-start | bytes 2097152 | tf_op jit(solution)/shard_map/all_to_all | solution.py:908
  105.9 204.1 %reduce-scatter.4.cloned.1.call-start = ((), (), s32[]{:S(2)}) async-start(), calls=%async_computation.5 | async-start | bytes 4456448 | tf_op jit(solution)/shard_map/reduce_scatter | solution.py:936
  159.6 25.9 %copy-start.5 = (bf16[8,256,256]{2,1,0:T(8,128)(2,1)}, bf16[8,256,256]{2,1,0:T(8,128)(2,1)S(1)}, u32[]{:S(2)}) copy-start(bf16[8,256,256]{2,1,0:T(8,128)(2,1)S(1)} %all-to-all-done) | copy-start | bytes 3145732
  185.6 206.9 %reduce-scatter.6.cloned.1.call-start = ((), (), s32[]{:S(2)}) async-start(), calls=%async_computation.6 | async-start | bytes 4456448 | tf_op jit(solution)/shard_map/reduce_scatter | solution.py:936
  187.4 124.4 %all-to-all-start.1 = ((bf16[8,256,256]{2,1,0:T(8,128)(2,1)}), bf16[8,256,256]{2,1,0:T(8,128)(2,1)S(1)}, u32[]{:S(2)}, u32[]{:S(2)}) async-start(bf16[8,256,256]{2,1,0:T(8,128)(2,1)} %concatenate.21), calls=%async_computation.2 | async-start | bytes 2097152 | tf_op jit(solution)/shard_map/all_to_all | solution.py:908
  231.0 5.2 copy-start.27
  231.0 366.1 %reduce-scatter.8.cloned.1.call-start = ((), (), s32[]{:S(2)}) async-start(), calls=%async_computation.7 | async-start | bytes 3342336 | tf_op jit(solution)/shard_map/reduce_scatter | solution.py:936
  234.0 153.9 %collective-permute-start.2 = (bf16[7,128,1024]{2,1,0:T(8,128)(2,1)}, bf16[7,128,1024]{2,1,0:T(8,128)(2,1)}, u32[]{:S(2)}, u32[]{:S(2)}) collective-permute-start(bf16[7,128,1024]{2,1,0:T(8,128)(2,1)} %dynamic-slice_bitcast_fusion), channel_id=1, source_target_pairs={{0,1},{1,0},{2,3},{3,2},{4,5},{5,4},{6,7},{7,6},{8,9},{9,8},{10,11... | collective-permute-start | bytes 5505032 | tf_op jit(solution)/shard_map/ppermute | solution.py:873
  234.6 176.1 %collective-permute-start = (bf16[1792,1024]{1,0:T(8,128)(2,1)}, bf16[1792,1024]{1,0:T(8,128)(2,1)}, u32[]{:S(2)}, u32[]{:S(2)}) collective-permute-start(bf16[1792,1024]{1,0:T(8,128)(2,1)} %get-tuple-element.59), channel_id=1, source_target_pairs={{0,1},{1,0},{2,3},{3,2},{4,5},{5,4},{6,7},{7,6},{8,9},{9,8},{10,11... | collective-permute-start | bytes 11010056 | tf_op jit(solution)/shard_map/ppermute | solution.py:873
  236.8 4.5 copy-start.7
  244.3 60.1 %copy-start.15 = (bf16[1024,1024]{1,0:T(8,128)(2,1)S(1)}, bf16[1024,1024]{1,0:T(8,128)(2,1)}, u32[]{:S(2)}) copy-start(bf16[1024,1024]{1,0:T(8,128)(2,1)} %get-tuple-element.60.refs_0_) | copy-start | bytes 6291460
  304.4 3.5 copy-start.13
  304.4 3.5 copy-start.18
  312.8 64.1 %copy-start.16 = (bf16[1024,1024]{1,0:T(8,128)(2,1)S(1)}, bf16[1024,1024]{1,0:T(8,128)(2,1)}, u32[]{:S(2)}) copy-start(bf16[1024,1024]{1,0:T(8,128)(2,1)} %get-tuple-element.60.refs_0_) | copy-start | bytes 6291460
  376.9 3.5 copy-start.14
  376.9 3.5 copy-start.21
  384.3 3.1 copy-start.17
  384.4 3.1 copy-start.19
  384.4 3.7 copy-start.24
  386.8 23.9 %collective-permute-start.1 = (bf16[1024,512]{1,0:T(8,128)(2,1)}, bf16[1024,512]{1,0:T(8,128)(2,1)}, u32[]{:S(2)}, u32[]{:S(2)}) collective-permute-start(bf16[1024,512]{1,0:T(8,128)(2,1)} %slice.71), channel_id=1, source_target_pairs={{0,1},{1,0},{2,3},{3,2},{4,5},{5,4},{6,7},{7,6},{8,9},{9,8},{10,11... | collective-permute-start | bytes 3145736 | tf_op jit(solution)/shard_map/ppermute | solution.py:873
  387.9 3.6 copy-start.20
  388.0 3.6 copy-start.22
  392.5 18.2 %copy-start.25 = (f32[128,128]{1,0:T(8,128)}, f32[128,128]{1,0:T(8,128)S(1)}, u32[]{:S(2)}) copy-start(f32[128,128]{1,0:T(8,128)S(1)} %scatter.9.refs_15_) | copy-start | bytes 196612
  586.6 4.0 copy-start.8
  586.6 4.0 copy-start.29
  586.6 4.1 copy-start.30
  599.4 5.1 copy-start.1
  599.4 4.5 copy-start.26
  (7 other events, 12.0 us)
Sparse Core Ops, SparseCore 0:
  185.7 107.8 reduce-scatter.3
  298.0 71.4 reduce-scatter.5
  384.5 91.0 reduce-scatter.7

commit v5 on v4

--- a/solution.py
+++ b/solution.py
@@ -569,6 +569,12 @@
     def own_heads(k):
         return pltpu.make_async_copy(attended(k, block), heads_of(mix, k, block), d_send.at[k * blocks + block])
 
+    def send_heads(k, n):
+        if n == 0:
+            own_heads(k).start()
+        else:
+            heads_home(k, lax.rem(block + n, blocks)).start()
+
     def heads_across(k, r):
         return remote(heads_of(mix, k, r), heads_of(facing_ref, k, r), e_send.at[k * blocks + r],
                       e_recv.at[k * blocks + r], facing)
@@ -579,11 +585,7 @@
             s = lax.rem(block + n, blocks)
             sent[s] = product(g_other, s).astype(BF)
             across(s).start()
-            for k in range(groups):
-                if n == 0:
-                    own_heads(k).start()
-                else:
-                    heads_home(k, s).start()
+            send_heads(0, n)
 
     def keep_heads(r):
         return pltpu.make_async_copy(mix.at[r], mixed_ref.at[r], e_local.at[r])
@@ -605,19 +607,20 @@
                 home_send[s] = grad
                 homeward(s).start()
 
+    def heads_arrive(k, n, r):
+        if n:
+            here = heads_of(mix, k, r)
+            remote(here, here, e_send.at[k * blocks + r], d_recv.at[k * blocks + r], facing).wait_recv()
+        else:
+            own_heads(k).wait()
+        heads_across(k, r).start()
+
     def norm(n):
         r = lax.rem(block + blocks - n, blocks)
 
         @pl.when(r < rows)
         def _():
-            for k in range(groups):
-                if n:
-                    here = heads_of(mix, k, r)
-                    remote(here, here, e_send.at[k * blocks + r], d_recv.at[k * blocks + r], facing).wait_recv()
-                else:
-                    own_heads(k).wait()
-                heads_across(k, r).start()
-            keep_heads(r).start()
+            heads_arrive(0, n, r)
             if n:
                 remote(home_send.at[r], home.at[r], b_send.at[r], b_recv.at[r], facing).wait_recv()
             grad = home[r].astype(F32) + add_ref[r].astype(F32)
@@ -631,9 +634,7 @@
             grad = grad - jnp.mean(grad, -1, keepdims=True) - x * jnp.mean(grad * x, -1, keepdims=True)
             own = cot_ref[r, pl.ds(pl.multiple_of(half * part, part), part), :]
             grads[r] = (own.astype(F32) + scale * grad).astype(BF)
-            share(r).start()
             keep(r).start()
-            total[...] += nn(cot_ref[r].T, mix[r])
 
     lag = 2
     for n in range(blocks + lag):
@@ -641,16 +642,12 @@
             forward(n)
         if n >= lag:
             norm(n - lag)
-
-    size = terms.shape[1]
-    for j in range(count):
-        terms[j] = total[j * size:(j + 1) * size].astype(BF)
-
-    def term(j):
-        return remote(terms.at[j], inbox.at[me], f_send.at[j], f_recv.at[me], device(j))
-
-    for j in peers():
-        term(j).start()
+        if n == blocks - 1:
+            @pl.when(has_row)
+            def _():
+                for k in range(1, groups):
+                    for other in range(blocks):
+                        send_heads(k, other)
 
     small[...] = extra_ref[...]
     lines = norms.shape[1] // LANES
@@ -660,6 +657,29 @@
     shared = small.at[pl.ds(0, 3 * lines)]
     swapped = remote(shared, small_in, g_send, g_recv, facing)
     swapped.start()
+    for r in range(rows):
+        share(r).start()
+
+    for n in range(blocks):
+        r = lax.rem(block + blocks - n, blocks)
+
+        @pl.when(r < rows)
+        def _():
+            for k in range(1, groups):
+                heads_arrive(k, n, r)
+            keep_heads(r).start()
+            total[...] += nn(cot_ref[r].T, mix[r])
+
+    size = terms.shape[1]
+    for j in range(count):
+        terms[j] = total[j * size:(j + 1) * size].astype(BF)
+
+    def term(j):
+        return remote(terms.at[j], inbox.at[me], f_send.at[j], f_recv.at[me], device(j))
+
+    for j in peers():
+        term(j).start()
+
     swapped.wait()
     small[:3 * lines, :] += small_in[...]
 
@@ -976,16 +996,18 @@
     grad_mixed = dot(cot, full_out).astype(BF).reshape(rows, group, width)
     row_grads = [to_rows(grad_mixed[:, :, cut]).reshape(length, wide) for cut in cuts]
 
+    other_out = swap(full_out) if pair else None
     activated, grad_inner, mlp_out, mlp_back, grad_bfc, *moved = mlp(
         flat_hidden, cot, weights, 4 * width // inner, b_fc[None], (grad_mixed,), hidden if pair else None
     )
     row_hidden = moved or row_hidden
     mlp_back = sum_parts(mlp_back.reshape(rows, group, model), 1)
-    grad_fc, grad_proj = weight_grads(flat_hidden, grad_inner, cot, activated, [row_grads[0]])
+    grad_fc, grad_proj = weight_grads(
+        flat_hidden, grad_inner, cot, activated, [row_grads[0]] + [other_out] * pair
+    )
     grad_fc_sum, grad_proj_sum = scatter(grad_fc), scatter(grad_proj)
     if pair:
         mlp_back = mlp_back.astype(BF)
-        other_out = swap(full_out)
         other_mlp = swap(mlp_out)
 
     bias = by_pair(b_qkv[None], width)

time: 621 us -> 610 us (0.982)
  waiting for transfers between devices: 16.9 us -> 0.79 us
  Pallas kernels: 445 us -> 452 us
    ppermute x3, waiting for transfers between devices: 16.2 us -> 0.01 us  [swap(): return lax.ppermute(value, 'tensor', [(0, 1), (1, 0)])]
    pallas_call x1, Pallas kernels: 172 us -> 182 us  [go_home(): pl.pallas_call(functools.partial(tail_kernel, groups, len(waits)), grid=(...]
    unnamed x64 -> x66, local copies, waits for them, and re-layouts: 17.5 us -> 19.6 us
  transfers between devices with their start and end apart: 8 -> 8, of which waited for: 1 -> 0; matrix products, arithmetic and copies ran while one was open for 8% -> 8% of each run, Pallas kernels for 57% -> 59%
where the time goes in v5:
time: 610 us; the launch traced here: 605 us
  Pallas kernels  452 us (74%)
  starting transfers between devices  55.3 us (9%)
  local copies, waits for them, and re-layouts  38.8 us (6%)
  matrix products  24.6 us (4%)
  other arithmetic  18.4 us (3%)
  between operations  14.4 us (2%)
    pallas_call x1, Pallas kernels, go_home(): pl.pallas_call(functools.partial(tail_kernel, groups, len(waits)), grid=(...  182 us
    pallas_call x2, Pallas kernels, attention(): pl.pallas_call(functools.partial(attn_kernel, bq, bk, part, len(waits)),...  124 us
    pallas_call x1, Pallas kernels, gather_weights(): pl.pallas_call(gather_kernel, out_shape=[jax.ShapeDtypeStruct((cores * bl...  72.4 us
    all_to_all x2, starting transfers between devices, to_rows(): lax.all_to_all(jnp.concatenate([value, pad], 0), 'blk', 0, 0, tiled=True)  51.2 us
    pallas_call x1, Pallas kernels, mlp(): pl.pallas_call(functools.partial(mlp_kernel, tile, len(waits), len(moves)...  50.3 us
    pallas_call x1, Pallas kernels, weight_grads(): pl.pallas_call(functools.partial(weight_grad_kernel, half, len(waits)), g...  23.5 us
    unnamed x66, local copies, waits for them, and re-layouts  19.6 us
    dot_general x5, matrix products, dot(): return jnp.dot(a, b, preferred_element_type=F32)  14.4 us
  transfers between devices with their start and end apart: 8, of which 0 were waited for; matrix products, arithmetic and copies ran while one was open for 8% of the time, Pallas kernels for 59%

profile of v5, /device:TPU:28, one launch (start us, length us, event | category | flops | bytes accessed | tf_op | source)
XLA Modules:
  0.0 604.5 jit_solution(15247103383970841500)
XLA Ops:
  9.7 2.0 copy-done.6
  11.7 72.4 %shard_map.203 = (bf16[1024,6144]{1,0:T(8,128)(2,1)S(1)}, bf16[7,256,1024]{2,1,0:T(8,128)(2,1)S(1)}) custom-call(bf16[64,6144]{1,0:T(8,128)(2,1)S(1)} %pad_maximum_fusion.1.x_ref, bf16[7,256,1024]{2,1,0:T(8,128)(2,1)S(1)} %copy-done.6, f32[1,1024]{1,0:T(1,128)S(1)} %bitcast.87, f32[1,1024]{1,0:T(1,128)S(1)} %bitcast.88), custom_call_target="tpu_custom_call" | custom-call | tf_op jit(solution)/shard_map/pallas_call | solution.py:412
  84.2 1.8 copy-done.3
  86.0 4.5 copy-done.2
  90.5 3.4 fusion.4
  93.9 2.8 copy.56
  98.3 7.6 %all-to-all-start = ((bf16[8,256,256]{2,1,0:T(8,128)(2,1)}), bf16[8,256,256]{2,1,0:T(8,128)(2,1)S(1)}, u32[]{:S(2)}, u32[]{:S(2)}) async-start(bf16[8,256,256]{2,1,0:T(8,128)(2,1)} %concatenate.20), calls=%async_computation | async-start | bytes 2097152 | tf_op jit(solution)/shard_map/all_to_all | solution.py:928
  107.7 1.6 collective-permute-start.1
  109.3 50.3 %shard_map.204 = (bf16[1792,2048]{1,0:T(8,128)(2,1)}, bf16[1792,2048]{1,0:T(8,128)(2,1)}, bf16[1792,1024]{1,0:T(8,128)(2,1)}, bf16[1792,1024]{1,0:T(8,128)(2,1)}...) custom-call(bf16[1792,1024]{1,0:T(8,128)(2,1)} %bitcast.80, ...), custom_call_target="tpu_custom_call" | custom-call | flops 1000 | bytes 1000 | tf_op jit(solution)/shard_map/pallas_call | solution.py:873
  159.6 2.8 copy-done.4
  162.4 23.5 %shard_map.205 = (bf16[1024,2048]{1,0:T(8,128)(2,1)}, bf16[1024,2048]{1,0:T(8,128)(2,1)}) custom-call(bf16[1792,1024]{1,0:T(8,128)(2,1)S(1)} %bitcast.81, bf16[1792,1024]{1,0:T(8,128)(2,1)} %bitcast.90, bf16[2048,256]{1,0:T(8,128)(2,1)S(1)} %bitcast.82, bf16[1024,512]{1,0:T(8,128)(2,1)S(1)} %collective-permute-done.1.refs_1_.refs_9_, ...), custom_call_target="tpu_custom_call" | custom-call | flops 1000 | bytes 1000 | tf_op jit(solution)/shard_map/pallas_call | solution.py:798
  187.7 43.6 %all-to-all-start.1 = ((bf16[8,256,256]{2,1,0:T(8,128)(2,1)}), bf16[8,256,256]{2,1,0:T(8,128)(2,1)S(1)}, u32[]{:S(2)}, u32[]{:S(2)}) async-start(bf16[8,256,256]{2,1,0:T(8,128)(2,1)} %concatenate.21), calls=%async_computation.2 | async-start | bytes 2097152 | tf_op jit(solution)/shard_map/all_to_all | solution.py:928
  231.3 3.0 dynamic-slice_bitcast_fusion
  234.9 1.5 collective-permute-start
  237.8 3.9 convert_reduce_fusion
  241.7 1.4 dynamic-slice_bitcast_fusion.2.refs_3_.refs_11_
  244.6 59.8 %shard_map.206 = (bf16[2048,256]{1,0:T(8,128)(2,1)}, bf16[1024,768]{1,0:T(8,128)(2,1)}, bf16[1024,768]{1,0:T(8,128)(2,1)}) custom-call(s32[4]{0:T(128)} %get-tuple-element.80.lo_ref, s32[4]{0:T(128)} %get-tuple-element.79.hi_ref, bf16[1024,1024]{1,0:T(8,128)(2,1)} %get-tuple-element.60.refs_0_, bf16[1024,1024]{1,0:T(8,128)(2,1)} %get-tuple-element.61.refs_1_, ...), custom_call_target="tpu_custom_call" | custom-call | flops 1000 | bytes 1000 | tf_op jit(solution)/shard_map/pallas_call | solution.py:274
  304.4 3.6 fusion.11
  308.0 2.0 add_convert_fusion.1
  310.1 1.8 convert_element_type.92.refs_3_
  312.8 64.2 %shard_map.207 = (bf16[2048,256]{1,0:T(8,128)(2,1)}, bf16[1024,768]{1,0:T(8,128)(2,1)}, bf16[1024,768]{1,0:T(8,128)(2,1)}) custom-call(s32[4]{0:T(128)} %get-tuple-element.80.lo_ref, s32[4]{0:T(128)} %get-tuple-element.79.hi_ref, bf16[1024,1024]{1,0:T(8,128)(2,1)} %get-tuple-element.60.refs_0_, bf16[1024,1024]{1,0:T(8,128)(2,1)} %get-tuple-element.61.refs_1_, ...), custom_call_target="tpu_custom_call" | custom-call | flops 1000 | bytes 1000 | tf_op jit(solution)/shard_map/pallas_call | solution.py:274
  377.0 3.5 fusion.12
  380.5 2.0 add_convert_fusion
  382.5 1.9 pad_maximum_fusion.refs_6_
  384.5 1.4 copy-done.20
  386.8 4.3 fusion.3.refs_13_
  392.2 2.0 convert_bitcast_fusion
  394.2 182.0 %shard_map.208 = (bf16[7,256,1024]{2,1,0:T(8,128)(2,1)}, f32[128,128]{1,0:T(8,128)}, f32[64,512]{1,0:T(8,128)}, bf16[7,256,512]{2,1,0:T(8,128)(2,1)}, bf16[7,256,512]{2,1,0:T(8,128)(2,1)}) custom-call(bf16[1024,768]{1,0:T(8,128)(2,1)} %get-tuple-element.65.refs_0_, bf16[1024,768]{1,0:T(8,128)(2,1)} %get-tuple-element.67.refs_1_, ...), custom_call_target="tpu_custom_call" | custom-call | flops 1000 | bytes 1000 | tf_op jit(solution)/shard_map/pallas_call | solution.py:749
  578.8 1.3 slice_bitcast_fusion
  580.1 3.8 fusion.13
  583.9 6.4 %fusion.2 = bf16[1792,1024]{1,0:T(8,128)(2,1)} fusion(bf16[1792,1024]{1,0:T(8,128)(2,1)S(1)} %bitcast.85, f32[1792,1024]{1,0:T(8,128)S(1)} %fusion.13, bf16[1792,1024]{1,0:T(8,128)(2,1)} %collective-permute-done.refs_8_, bf16[1792,1024]{1,0:T(8,128)(2,1)} %get-tuple-element.59, bf16[1792,512]{1,0:T(8,128)(2,1)S(1)} %bitcast.110, f32[1024]{0:T(1024)S(1)} %copy-done.31, ...), kind=kOutput, calls=%fused_computation.3 | convolution fusion | flops 1895563264 | bytes 24907776 | tf_op jit(solution)/shard_map/dot_general | solution.py:20
  592.7 4.5 copy.78
  (104 shorter events, 19.7 us)
Async XLA Ops:
  7.2 229.2 %copy-start = (s32[7,5]{1,0:T(8,128)S(1)}, s32[7,5]{1,0:T(8,128)}, u32[]{:S(2)}) copy-start(s32[7,5]{1,0:T(8,128)} %param.26) | copy-start | bytes 424
  7.2 2.5 copy-start.11
  7.2 2.5 copy-start.12
  11.7 78.8 %copy-start.13 = (bf16[7,256,1024]{2,1,0:T(8,128)(2,1)S(1)}, bf16[7,256,1024]{2,1,0:T(8,128)(2,1)}, u32[]{:S(2)}) copy-start(bf16[7,256,1024]{2,1,0:T(8,128)(2,1)} %refs_12_.1) | copy-start | bytes 11010052
  86.0 4.5 copy-start.2
  98.3 61.3 %all-to-all-start = ((bf16[8,256,256]{2,1,0:T(8,128)(2,1)}), bf16[8,256,256]{2,1,0:T(8,128)(2,1)S(1)}, u32[]{:S(2)}, u32[]{:S(2)}) async-start(bf16[8,256,256]{2,1,0:T(8,128)(2,1)} %concatenate.20), calls=%async_computation | async-start | bytes 2097152 | tf_op jit(solution)/shard_map/all_to_all | solution.py:928
  105.9 204.2 %reduce-scatter.4.cloned.1.call-start = ((), (), s32[]{:S(2)}) async-start(), calls=%async_computation.5 | async-start | bytes 4456448 | tf_op jit(solution)/shard_map/reduce_scatter | solution.py:956
  107.7 51.9 %collective-permute-start.1 = (bf16[1024,512]{1,0:T(8,128)(2,1)S(1)}, bf16[1024,512]{1,0:T(8,128)(2,1)S(1)}, u32[]{:S(2)}, u32[]{:S(2)}) collective-permute-start(bf16[1024,512]{1,0:T(8,128)(2,1)S(1)} %slice.71), channel_id=1, source_target_pairs={{0,1},{1,0},{2,3},{3,2},{4,5},{5,4},{6,7},{7,6},{8,9},{9,8},{10,11... | collective-permute-start | bytes 3145736 | tf_op jit(solution)/shard_map/ppermute | solution.py:893
  159.6 26.3 %copy-start.9 = (bf16[1024,512]{1,0:T(8,128)(2,1)}, bf16[1024,512]{1,0:T(8,128)(2,1)S(1)}, u32[]{:S(2)}) copy-start(bf16[1024,512]{1,0:T(8,128)(2,1)S(1)} %collective-permute-done.1.refs_1_.refs_9_) | copy-start | bytes 3145732
  159.6 26.3 %copy-start.5 = (bf16[8,256,256]{2,1,0:T(8,128)(2,1)}, bf16[8,256,256]{2,1,0:T(8,128)(2,1)S(1)}, u32[]{:S(2)}) copy-start(bf16[8,256,256]{2,1,0:T(8,128)(2,1)S(1)} %all-to-all-done) | copy-start | bytes 3145732
  159.6 2.8 copy-start.4
  185.9 206.2 %reduce-scatter.6.cloned.1.call-start = ((), (), s32[]{:S(2)}) async-start(), calls=%async_computation.6 | async-start | bytes 4456448 | tf_op jit(solution)/shard_map/reduce_scatter | solution.py:956
  187.7 124.2 %all-to-all-start.1 = ((bf16[8,256,256]{2,1,0:T(8,128)(2,1)}), bf16[8,256,256]{2,1,0:T(8,128)(2,1)S(1)}, u32[]{:S(2)}, u32[]{:S(2)}) async-start(bf16[8,256,256]{2,1,0:T(8,128)(2,1)} %concatenate.21), calls=%async_computation.2 | async-start | bytes 2097152 | tf_op jit(solution)/shard_map/all_to_all | solution.py:928
  231.3 5.2 copy-start.28
  231.3 359.1 %reduce-scatter.8.cloned.1.call-start = ((), (), s32[]{:S(2)}) async-start(), calls=%async_computation.7 | async-start | bytes 3342336 | tf_op jit(solution)/shard_map/reduce_scatter | solution.py:956
  234.3 152.5 %collective-permute-start.2 = (bf16[7,128,1024]{2,1,0:T(8,128)(2,1)}, bf16[7,128,1024]{2,1,0:T(8,128)(2,1)}, u32[]{:S(2)}, u32[]{:S(2)}) collective-permute-start(bf16[7,128,1024]{2,1,0:T(8,128)(2,1)} %dynamic-slice_bitcast_fusion), channel_id=1, source_target_pairs={{0,1},{1,0},{2,3},{3,2},{4,5},{5,4},{6,7},{7,6},{8,9},{9,8},{10,11... | collective-permute-start | bytes 5505032 | tf_op jit(solution)/shard_map/ppermute | solution.py:893
  234.9 159.3 %collective-permute-start = (bf16[1792,1024]{1,0:T(8,128)(2,1)}, bf16[1792,1024]{1,0:T(8,128)(2,1)}, u32[]{:S(2)}, u32[]{:S(2)}) collective-permute-start(bf16[1792,1024]{1,0:T(8,128)(2,1)} %get-tuple-element.59), channel_id=1, source_target_pairs={{0,1},{1,0},{2,3},{3,2},{4,5},{5,4},{6,7},{7,6},{8,9},{9,8},{10,11... | collective-permute-start | bytes 11010056 | tf_op jit(solution)/shard_map/ppermute | solution.py:893
  237.1 4.5 copy-start.7
  244.6 59.8 %copy-start.15 = (bf16[1024,1024]{1,0:T(8,128)(2,1)S(1)}, bf16[1024,1024]{1,0:T(8,128)(2,1)}, u32[]{:S(2)}) copy-start(bf16[1024,1024]{1,0:T(8,128)(2,1)} %get-tuple-element.61.refs_1_) | copy-start | bytes 6291460
  304.4 3.6 copy-start.17
  304.4 3.6 copy-start.19
  312.8 64.2 %copy-start.18 = (bf16[1024,1024]{1,0:T(8,128)(2,1)S(1)}, bf16[1024,1024]{1,0:T(8,128)(2,1)}, u32[]{:S(2)}) copy-start(bf16[1024,1024]{1,0:T(8,128)(2,1)} %get-tuple-element.60.refs_0_) | copy-start | bytes 6291460
  377.0 3.5 copy-start.16
  377.0 3.5 copy-start.23
  386.8 4.4 copy-start.22
  386.8 4.4 copy-start.24
  394.2 185.9 %copy-start.10 = (bf16[1024,512]{1,0:T(8,128)(2,1)S(1)}, bf16[1024,512]{1,0:T(8,128)(2,1)}, u32[]{:S(2)}) copy-start(bf16[1024,512]{1,0:T(8,128)(2,1)} %copy-done.9) | copy-start | bytes 3145732
  580.1 3.8 copy-start.8
  580.1 3.8 copy-start.30
  580.1 3.8 copy-start.31
  592.7 5.1 copy-start.1
  592.7 4.5 copy-start.27
  (8 other events, 12.5 us)
Sparse Core Ops, SparseCore 0:
  186.0 107.8 reduce-scatter.3
  298.3 71.6 reduce-scatter.5
  384.6 99.6 reduce-scatter.7

commit v6 on v5

--- a/solution.py
+++ b/solution.py
@@ -513,7 +513,7 @@
 def tail_kernel(groups, waits, *refs):
     g_mine, g_other, heads = refs[:groups], refs[groups:2 * groups], refs[2 * groups:3 * groups]
     (w_ref, tok_ref, cot_ref, add_ref, gain_ref, extra_ref, out_ref, sum_ref, wgrad_ref, mixed_ref, facing_ref,
-     sent, got, home_send, home, grads, mix, total, terms, inbox, norms, small, small_in, small_box, small_out,
+     sent, got, home_send, home, grads, mix, total, terms, paired, merged, inbox, norms, small, small_in, small_box, small_out,
      a_send, a_recv, b_send, b_recv, c_send, c_recv, c_local, d_send, d_recv, e_send, e_recv, e_local,
      f_send, f_recv, g_send, g_recv, h_send, h_recv, i_send, i_recv) = refs[3 * groups + waits:]
     rows, part, model = tok_ref.shape
@@ -556,7 +556,7 @@
         return pltpu.make_async_copy(grads.at[r], own_half(out_ref, r), c_local.at[r])
 
     def heads_of(ref, k, r):
-        wide = heads[k].shape[1]
+        wide = heads[-1].shape[1]
         return ref.at[r, :, k * wide:(k + 1) * wide]
 
     def attended(k, s):
@@ -574,6 +574,9 @@
             own_heads(k).start()
         else:
             heads_home(k, lax.rem(block + n, blocks)).start()
+
+    def landed(r):
+        return pltpu.make_async_copy(heads[0].at[r], heads_of(mix, 0, r), d_send.at[r])
 
     def heads_across(k, r):
         return remote(heads_of(mix, k, r), heads_of(facing_ref, k, r), e_send.at[k * blocks + r],
@@ -585,7 +588,9 @@
             s = lax.rem(block + n, blocks)
             sent[s] = product(g_other, s).astype(BF)
             across(s).start()
-            send_heads(0, n)
+
+    for r in range(rows):
+        landed(r).start()
 
     def keep_heads(r):
         return pltpu.make_async_copy(mix.at[r], mixed_ref.at[r], e_local.at[r])
@@ -620,7 +625,8 @@
 
         @pl.when(r < rows)
         def _():
-            heads_arrive(0, n, r)
+            landed(r).wait()
+            heads_across(0, r).start()
             if n:
                 remote(home_send.at[r], home.at[r], b_send.at[r], b_recv.at[r], facing).wait_recv()
             grad = home[r].astype(F32) + add_ref[r].astype(F32)
@@ -671,17 +677,27 @@
             total[...] += nn(cot_ref[r].T, mix[r])
 
     size = terms.shape[1]
+    core = lax.axis_index("dp")
     for j in range(count):
         terms[j] = total[j * size:(j + 1) * size].astype(BF)
 
-    def term(j):
-        return remote(terms.at[j], inbox.at[me], f_send.at[j], f_recv.at[me], device(j))
-
-    for j in peers():
-        term(j).start()
+    def to_sibling():
+        theirs = terms.at[pl.ds((1 - core) * blocks, blocks)]
+        return remote(theirs, paired, f_send.at[blocks], f_recv.at[blocks], {"dp": 1 - core})
+
+    to_sibling().start()
 
     swapped.wait()
     small[:3 * lines, :] += small_in[...]
+    to_sibling().wait()
+
+    def term(s):
+        return remote(merged.at[s], inbox.at[block], f_send.at[s], f_recv.at[block], {"blk": s})
+
+    for s in range(blocks):
+        merged[s] = (terms[core * blocks + s].astype(F32) + paired[s].astype(F32)).astype(BF)
+    for n in range(1, blocks):
+        term(lax.rem(block + n, blocks)).start()
 
     def line(ref, j):
         return ref.at[pl.ds(pl.multiple_of(j * 8, 8), 8)]
@@ -703,20 +719,22 @@
     small_out[pl.ds(pl.multiple_of(me * 8, 8), 8), :] = added
     for j in peers():
         small_sum(j).start()
-    inbox[me] = terms[me]
-    for j in peers():
-        remote(inbox.at[j], inbox.at[j], f_send.at[j], f_recv.at[j], device(j)).wait_recv()
+    inbox[block] = merged[block]
+    for n in range(1, blocks):
+        s = lax.rem(block + n, blocks)
+        remote(inbox.at[s], inbox.at[s], f_send.at[s], f_recv.at[s], facing).wait_recv()
     added = inbox[0].astype(F32)
-    for j in range(1, count):
-        added = added + inbox[j].astype(F32)
+    for s in range(1, blocks):
+        added = added + inbox[s].astype(F32)
     wgrad_ref[...] = added
     for j in peers():
         remote(line(small_out, j), line(small_out, j), i_send.at[j], i_recv.at[j], device(j)).wait_recv()
     sum_ref[...] = small_out[...]
     for j in peers():
-        term(j).wait_send()
         small_term(j).wait_send()
         small_sum(j).wait_send()
+    for n in range(1, blocks):
+        term(lax.rem(block + n, blocks)).wait_send()
 
     for r in range(rows):
         share(r).wait()
@@ -731,7 +749,7 @@
             across(s).wait_send()
         for n in range(1, blocks):
             homeward(lax.rem(block + n, blocks)).wait_send()
-            for k in range(groups):
+            for k in range(1, groups):
                 heads_home(k, lax.rem(block + n, blocks)).wait_send()
 
 
@@ -742,7 +760,7 @@
     dma = pltpu.SemaphoreType.DMA
     groups, hbm = len(g_mine), pl.BlockSpec(memory_space=pl.ANY)
     count = lax.axis_size("dp") * blocks
-    wide_heads = sum(o.shape[1] for o in attended)
+    wide_heads = sum(o.shape[-1] for o in attended)
     lines = 3 * model // LANES
     heads = jax.ShapeDtypeStruct((rows, 2 * part, wide_heads), BF)
     vmem = pl.BlockSpec(memory_space=pltpu.VMEM)
@@ -756,7 +774,8 @@
         out_specs=[hbm, vmem, vmem, hbm, hbm],
         scratch_shapes=[pltpu.VMEM((blocks, part, model), BF)] * 4 + [pltpu.VMEM((rows, part, model), BF)]
         + [pltpu.VMEM(heads.shape, BF), pltpu.VMEM((model, wide_heads), F32)]
-        + [pltpu.VMEM((count, model // count, wide_heads), BF)] * 2
+        + [pltpu.VMEM((count, model // count, wide_heads), BF)]
+        + [pltpu.VMEM((blocks, model // count, wide_heads), BF)] * 3
         + [pltpu.VMEM((8, model), F32), pltpu.VMEM((8 * count, LANES), F32), pltpu.VMEM((lines, LANES), F32)]
         + [pltpu.VMEM((count, 8, LANES), F32), pltpu.VMEM((8 * count, LANES), F32)]
         + [dma((blocks,))] * 4 + [dma((rows,))] * 3 + [dma((groups * blocks,))] * 4 + [dma((rows,))]
@@ -1035,7 +1054,8 @@
         extra = jnp.zeros((8 * (model // shard.shape[0]), LANES), F32)
         extra = extra.at[2 * lines:3 * lines].set(tensor_sums).at[3 * lines:used].set(bias_sums)
         grad_tokens, sums, grad_out_sum, mixed, other_mixed = go_home(
-            [g[0] for g in grad_packed], [g[1] for g in grad_packed], attended, weights, own_tokens, cotangent,
+            [g[0] for g in grad_packed], [g[1] for g in grad_packed],
+            [to_blocks(attended[0].reshape(blocks, group, wide), rows)] + attended[1:], weights, own_tokens, cotangent,
             mlp_back, ln_gain[None], extra, [grad_qkv, grad_proj_sum, other_mlp, other_out],
         )
         norm_sums, bias_sums = sums[:3 * lines].reshape(3, model), sums[3 * lines:used].reshape(-1)

time: 610 us -> 599 us (0.982)
  Pallas kernels: 452 us -> 433 us
    pallas_call x1, Pallas kernels: 182 us -> 167 us  [go_home(): pl.pallas_call(functools.partial(tail_kernel, groups, len(waits)), grid=(...]
  transfers between devices with their start and end apart: 8 -> 9, of which waited for: 0 -> 0; matrix products, arithmetic and copies ran while one was open for 8% -> 9% of each run, Pallas kernels for 59% -> 57%
where the time goes in v6:
time: 599 us; the launch traced here: 593 us
  Pallas kernels  433 us (72%)
  starting transfers between devices  61.3 us (10%)
  local copies, waits for them, and re-layouts  40.2 us (7%)
  matrix products  24.6 us (4%)
  other arithmetic  18.3 us (3%)
  between operations  14.5 us (2%)
    pallas_call x1, Pallas kernels, go_home(): pl.pallas_call(functools.partial(tail_kernel, groups, len(waits)), grid=(...  167 us
    pallas_call x2, Pallas kernels, attention(): pl.pallas_call(functools.partial(attn_kernel, bq, bk, part, len(waits)),...  120 us
    pallas_call x1, Pallas kernels, gather_weights(): pl.pallas_call(gather_kernel, out_shape=[jax.ShapeDtypeStruct((cores * bl...  72.4 us
    all_to_all x2, starting transfers between devices, to_rows(): lax.all_to_all(jnp.concatenate([value, pad], 0), 'blk', 0, 0, tiled=True)  51.2 us
    pallas_call x1, Pallas kernels, mlp(): pl.pallas_call(functools.partial(mlp_kernel, tile, len(waits), len(moves)...  50.3 us
    pallas_call x1, Pallas kernels, weight_grads(): pl.pallas_call(functools.partial(weight_grad_kernel, half, len(waits)), g...  23.5 us
    unnamed x66, local copies, waits for them, and re-layouts  18.5 us
    dot_general x5, matrix products, dot(): return jnp.dot(a, b, preferred_element_type=F32)  14.4 us
  transfers between devices with their start and end apart: 9, of which 0 were waited for; matrix products, arithmetic and copies ran while one was open for 9% of the time, Pallas kernels for 57%

profile of v6, /device:TPU:28, one launch (start us, length us, event | category | flops | bytes accessed | tf_op | source)
XLA Modules:
  0.0 593.0 jit_solution(14790848141211620599)
XLA Ops:
  9.7 2.0 copy-done.6
  11.7 72.4 %shard_map.203 = (bf16[1024,6144]{1,0:T(8,128)(2,1)S(1)}, bf16[7,256,1024]{2,1,0:T(8,128)(2,1)S(1)}) custom-call(bf16[64,6144]{1,0:T(8,128)(2,1)S(1)} %pad_maximum_fusion.1.x_ref, bf16[7,256,1024]{2,1,0:T(8,128)(2,1)S(1)} %copy-done.6, f32[1,1024]{1,0:T(1,128)S(1)} %bitcast.88, f32[1,1024]{1,0:T(1,128)S(1)} %bitcast.89), custom_call_target="tpu_custom_call" | custom-call | tf_op jit(solution)/shard_map/pallas_call | solution.py:412
  84.2 1.8 copy-done.3
  86.0 4.5 copy-done.2
  90.5 3.4 fusion.4
  93.9 2.8 copy.56
  98.3 7.6 %all-to-all-start = ((bf16[8,256,256]{2,1,0:T(8,128)(2,1)}), bf16[8,256,256]{2,1,0:T(8,128)(2,1)S(1)}, u32[]{:S(2)}, u32[]{:S(2)}) async-start(bf16[8,256,256]{2,1,0:T(8,128)(2,1)} %concatenate.20), calls=%async_computation | async-start | bytes 2097152 | tf_op jit(solution)/shard_map/all_to_all | solution.py:947
  107.7 1.6 collective-permute-start.1
  109.3 50.3 %shard_map.204 = (bf16[1792,2048]{1,0:T(8,128)(2,1)}, bf16[1792,2048]{1,0:T(8,128)(2,1)}, bf16[1792,1024]{1,0:T(8,128)(2,1)}, bf16[1792,1024]{1,0:T(8,128)(2,1)}...) custom-call(bf16[1792,1024]{1,0:T(8,128)(2,1)} %bitcast.81, ...), custom_call_target="tpu_custom_call" | custom-call | flops 1000 | bytes 1000 | tf_op jit(solution)/shard_map/pallas_call | solution.py:892
  159.7 2.8 copy-done.4
  162.5 23.5 %shard_map.205 = (bf16[1024,2048]{1,0:T(8,128)(2,1)}, bf16[1024,2048]{1,0:T(8,128)(2,1)}) custom-call(bf16[1792,1024]{1,0:T(8,128)(2,1)S(1)} %bitcast.82, bf16[1792,1024]{1,0:T(8,128)(2,1)} %bitcast.91, bf16[2048,256]{1,0:T(8,128)(2,1)S(1)} %bitcast.83, bf16[1024,512]{1,0:T(8,128)(2,1)S(1)} %collective-permute-done.1.refs_1_.refs_9_, ...), custom_call_target="tpu_custom_call" | custom-call | flops 1000 | bytes 1000 | tf_op jit(solution)/shard_map/pallas_call | solution.py:817
  187.9 43.6 %all-to-all-start.1 = ((bf16[8,256,256]{2,1,0:T(8,128)(2,1)}), bf16[8,256,256]{2,1,0:T(8,128)(2,1)S(1)}, u32[]{:S(2)}, u32[]{:S(2)}) async-start(bf16[8,256,256]{2,1,0:T(8,128)(2,1)} %concatenate.21), calls=%async_computation.2 | async-start | bytes 2097152 | tf_op jit(solution)/shard_map/all_to_all | solution.py:947
  231.4 3.1 dynamic-slice_bitcast_fusion
  235.1 1.5 collective-permute-start
  237.9 3.9 convert_reduce_fusion
  241.8 1.4 dynamic-slice_bitcast_fusion.2.refs_3_.refs_11_
  244.8 59.8 %shard_map.206 = (bf16[2048,256]{1,0:T(8,128)(2,1)}, bf16[1024,768]{1,0:T(8,128)(2,1)}, bf16[1024,768]{1,0:T(8,128)(2,1)}) custom-call(s32[4]{0:T(128)} %get-tuple-element.80.lo_ref, s32[4]{0:T(128)} %get-tuple-element.79.hi_ref, bf16[1024,1024]{1,0:T(8,128)(2,1)} %get-tuple-element.60.refs_0_, bf16[1024,1024]{1,0:T(8,128)(2,1)} %get-tuple-element.61.refs_1_, ...), custom_call_target="tpu_custom_call" | custom-call | flops 1000 | bytes 1000 | tf_op jit(solution)/shard_map/pallas_call | solution.py:274
  304.6 3.5 fusion.11
  308.1 2.0 add_convert_fusion.1
  310.2 1.8 convert_element_type.92.refs_3_
  312.0 6.0 %all-to-all-start.2 = ((bf16[8,256,256]{2,1,0:T(8,128)(2,1)}), bf16[8,256,256]{2,1,0:T(8,128)(2,1)}, u32[]{:S(2)}, u32[]{:S(2)}) async-start(bf16[8,256,256]{2,1,0:T(8,128)(2,1)} %bitcast.21), calls=%async_computation.3 | async-start | bytes 2097152 | tf_op jit(solution)/shard_map/all_to_all | solution.py:951
  318.0 60.0 %shard_map.207 = (bf16[2048,256]{1,0:T(8,128)(2,1)}, bf16[1024,768]{1,0:T(8,128)(2,1)}, bf16[1024,768]{1,0:T(8,128)(2,1)}) custom-call(s32[4]{0:T(128)} %get-tuple-element.80.lo_ref, s32[4]{0:T(128)} %get-tuple-element.79.hi_ref, bf16[1024,1024]{1,0:T(8,128)(2,1)} %get-tuple-element.60.refs_0_, bf16[1024,1024]{1,0:T(8,128)(2,1)} %get-tuple-element.61.refs_1_, ...), custom_call_target="tpu_custom_call" | custom-call | flops 1000 | bytes 1000 | tf_op jit(solution)/shard_map/pallas_call | solution.py:274
  378.0 3.5 fusion.12
  381.5 2.0 add_convert_fusion
  383.5 1.9 pad_maximum_fusion.refs_6_
  387.8 4.3 fusion.3.refs_13_
  392.1 2.4 slice.86.refs_4_
  395.3 2.0 convert_bitcast_fusion
  397.3 167.4 %shard_map.208 = (bf16[7,256,1024]{2,1,0:T(8,128)(2,1)}, f32[128,128]{1,0:T(8,128)}, f32[64,512]{1,0:T(8,128)}, bf16[7,256,512]{2,1,0:T(8,128)(2,1)}, bf16[7,256,512]{2,1,0:T(8,128)(2,1)}) custom-call(bf16[1024,768]{1,0:T(8,128)(2,1)} %get-tuple-element.65.refs_0_, bf16[1024,768]{1,0:T(8,128)(2,1)} %get-tuple-element.67.refs_1_, ...), custom_call_target="tpu_custom_call" | custom-call | flops 1000 | bytes 1000 | tf_op jit(solution)/shard_map/pallas_call | solution.py:767
  568.6 3.8 fusion.13
  572.4 6.4 %fusion.2 = bf16[1792,1024]{1,0:T(8,128)(2,1)} fusion(bf16[1792,1024]{1,0:T(8,128)(2,1)S(1)} %bitcast.86, f32[1792,1024]{1,0:T(8,128)S(1)} %fusion.13, bf16[1792,1024]{1,0:T(8,128)(2,1)} %collective-permute-done.refs_8_, bf16[1792,1024]{1,0:T(8,128)(2,1)} %get-tuple-element.59, bf16[1792,512]{1,0:T(8,128)(2,1)S(1)} %bitcast.111, f32[1024]{0:T(1024)S(1)} %copy-done.31, ...), kind=kOutput, calls=%fused_computation.3 | convolution fusion | flops 1895563264 | bytes 24907776 | tf_op jit(solution)/shard_map/dot_general | solution.py:20
  581.2 4.5 copy.78
  (107 shorter events, 21.3 us)
Async XLA Ops:
  7.2 229.3 %copy-start = (s32[7,5]{1,0:T(8,128)S(1)}, s32[7,5]{1,0:T(8,128)}, u32[]{:S(2)}) copy-start(s32[7,5]{1,0:T(8,128)} %param.26) | copy-start | bytes 424
  11.7 78.8 %copy-start.13 = (bf16[7,256,1024]{2,1,0:T(8,128)(2,1)S(1)}, bf16[7,256,1024]{2,1,0:T(8,128)(2,1)}, u32[]{:S(2)}) copy-start(bf16[7,256,1024]{2,1,0:T(8,128)(2,1)} %refs_12_.1) | copy-start | bytes 11010052
  86.0 4.5 copy-start.2
  98.3 61.4 %all-to-all-start = ((bf16[8,256,256]{2,1,0:T(8,128)(2,1)}), bf16[8,256,256]{2,1,0:T(8,128)(2,1)S(1)}, u32[]{:S(2)}, u32[]{:S(2)}) async-start(bf16[8,256,256]{2,1,0:T(8,128)(2,1)} %concatenate.20), calls=%async_computation | async-start | bytes 2097152 | tf_op jit(solution)/shard_map/all_to_all | solution.py:947
  105.9 204.3 %reduce-scatter.4.cloned.1.call-start = ((), (), s32[]{:S(2)}) async-start(), calls=%async_computation.6 | async-start | bytes 4456448 | tf_op jit(solution)/shard_map/reduce_scatter | solution.py:975
  107.7 51.9 %collective-permute-start.1 = (bf16[1024,512]{1,0:T(8,128)(2,1)S(1)}, bf16[1024,512]{1,0:T(8,128)(2,1)S(1)}, u32[]{:S(2)}, u32[]{:S(2)}) collective-permute-start(bf16[1024,512]{1,0:T(8,128)(2,1)S(1)} %slice.74), channel_id=1, source_target_pairs={{0,1},{1,0},{2,3},{3,2},{4,5},{5,4},{6,7},{7,6},{8,9},{9,8},{10,11... | collective-permute-start | bytes 3145736 | tf_op jit(solution)/shard_map/ppermute | solution.py:912
  159.7 26.3 %copy-start.9 = (bf16[1024,512]{1,0:T(8,128)(2,1)}, bf16[1024,512]{1,0:T(8,128)(2,1)S(1)}, u32[]{:S(2)}) copy-start(bf16[1024,512]{1,0:T(8,128)(2,1)S(1)} %collective-permute-done.1.refs_1_.refs_9_) | copy-start | bytes 3145732
  159.7 26.3 %copy-start.5 = (bf16[8,256,256]{2,1,0:T(8,128)(2,1)}, bf16[8,256,256]{2,1,0:T(8,128)(2,1)S(1)}, u32[]{:S(2)}) copy-start(bf16[8,256,256]{2,1,0:T(8,128)(2,1)S(1)} %all-to-all-done) | copy-start | bytes 3145732
  159.7 2.8 copy-start.4
  186.0 209.3 %reduce-scatter.6.cloned.1.call-start = ((), (), s32[]{:S(2)}) async-start(), calls=%async_computation.7 | async-start | bytes 4456448 | tf_op jit(solution)/shard_map/reduce_scatter | solution.py:975
  187.9 124.1 %all-to-all-start.1 = ((bf16[8,256,256]{2,1,0:T(8,128)(2,1)}), bf16[8,256,256]{2,1,0:T(8,128)(2,1)S(1)}, u32[]{:S(2)}, u32[]{:S(2)}) async-start(bf16[8,256,256]{2,1,0:T(8,128)(2,1)} %concatenate.21), calls=%async_computation.2 | async-start | bytes 2097152 | tf_op jit(solution)/shard_map/all_to_all | solution.py:947
  231.4 5.2 copy-start.28
  234.5 153.3 %collective-permute-start.2 = (bf16[7,128,1024]{2,1,0:T(8,128)(2,1)}, bf16[7,128,1024]{2,1,0:T(8,128)(2,1)}, u32[]{:S(2)}, u32[]{:S(2)}) collective-permute-start(bf16[7,128,1024]{2,1,0:T(8,128)(2,1)} %dynamic-slice_bitcast_fusion), channel_id=1, source_target_pairs={{0,1},{1,0},{2,3},{3,2},{4,5},{5,4},{6,7},{7,6},{8,9},{9,8},{10,11... | collective-permute-start | bytes 5505032 | tf_op jit(solution)/shard_map/ppermute | solution.py:912
  235.1 162.2 %collective-permute-start = (bf16[1792,1024]{1,0:T(8,128)(2,1)}, bf16[1792,1024]{1,0:T(8,128)(2,1)}, u32[]{:S(2)}, u32[]{:S(2)}) collective-permute-start(bf16[1792,1024]{1,0:T(8,128)(2,1)} %get-tuple-element.59), channel_id=1, source_target_pairs={{0,1},{1,0},{2,3},{3,2},{4,5},{5,4},{6,7},{7,6},{8,9},{9,8},{10,11... | collective-permute-start | bytes 11010056 | tf_op jit(solution)/shard_map/ppermute | solution.py:912
  237.3 4.5 copy-start.7
  244.8 59.8 %copy-start.15 = (bf16[1024,1024]{1,0:T(8,128)(2,1)S(1)}, bf16[1024,1024]{1,0:T(8,128)(2,1)}, u32[]{:S(2)}) copy-start(bf16[1024,1024]{1,0:T(8,128)(2,1)} %get-tuple-element.61.refs_1_) | copy-start | bytes 6291460
  304.5 3.6 copy-start.17
  304.6 3.6 copy-start.19
  312.0 6.0 %copy-start.25 = (bf16[8,256,256]{2,1,0:T(8,128)(2,1)}, bf16[8,256,256]{2,1,0:T(8,128)(2,1)S(1)}, u32[]{:S(2)}) copy-start(bf16[8,256,256]{2,1,0:T(8,128)(2,1)S(1)} %all-to-all-done.1) | copy-start | bytes 3145732
  312.0 80.1 %all-to-all-start.2 = ((bf16[8,256,256]{2,1,0:T(8,128)(2,1)}), bf16[8,256,256]{2,1,0:T(8,128)(2,1)}, u32[]{:S(2)}, u32[]{:S(2)}) async-start(bf16[8,256,256]{2,1,0:T(8,128)(2,1)} %bitcast.21), calls=%async_computation.3 | async-start | bytes 2097152 | tf_op jit(solution)/shard_map/all_to_all | solution.py:951
  318.0 260.9 %reduce-scatter.8.cloned.1.call-start = ((), (), s32[]{:S(2)}) async-start(), calls=%async_computation.8 | async-start | bytes 3342336 | tf_op jit(solution)/shard_map/reduce_scatter | solution.py:975
  318.0 60.0 %copy-start.18 = (bf16[1024,1024]{1,0:T(8,128)(2,1)S(1)}, bf16[1024,1024]{1,0:T(8,128)(2,1)}, u32[]{:S(2)}) copy-start(bf16[1024,1024]{1,0:T(8,128)(2,1)} %get-tuple-element.60.refs_0_) | copy-start | bytes 6291460
  378.0 3.5 copy-start.16
  378.0 3.5 copy-start.23
  387.8 6.7 %copy-start.24 = (bf16[1024,768]{1,0:T(8,128)(2,1)S(1)}, bf16[1024,768]{1,0:T(8,128)(2,1)}, u32[]{:S(2)}) copy-start(bf16[1024,768]{1,0:T(8,128)(2,1)} %get-tuple-element.69.refs_3_) | copy-start | bytes 4718596
  392.1 2.9 copy-start.29
  397.3 171.3 %copy-start.10 = (bf16[1024,512]{1,0:T(8,128)(2,1)S(1)}, bf16[1024,512]{1,0:T(8,128)(2,1)}, u32[]{:S(2)}) copy-start(bf16[1024,512]{1,0:T(8,128)(2,1)} %copy-done.9) | copy-start | bytes 3145732
  568.6 3.8 copy-start.8
  568.6 3.8 copy-start.30
  568.6 3.8 copy-start.31
  581.2 5.1 copy-start.1
  581.2 4.5 copy-start.27
  (9 other events, 18.1 us)
Sparse Core Ops, SparseCore 0:
  186.1 107.8 reduce-scatter.3
  298.3 77.2 reduce-scatter.5
  385.5 96.7 reduce-scatter.7

commit v7 on v6

--- a/solution.py
+++ b/solution.py
@@ -516,7 +516,7 @@
      sent, got, home_send, home, grads, mix, total, terms, paired, merged, inbox, norms, small, small_in, small_box, small_out,
      a_send, a_recv, b_send, b_recv, c_send, c_recv, c_local, d_send, d_recv, e_send, e_recv, e_local,
      f_send, f_recv, g_send, g_recv, h_send, h_recv, i_send, i_recv) = refs[3 * groups + waits:]
-    rows, part, model = tok_ref.shape
+    rows, part, model = tok_ref.shape[0], tok_ref.shape[1] // 2, tok_ref.shape[2]
     block, half = lax.axis_index("blk"), lax.axis_index("tensor")
     blocks = lax.axis_size("blk")
     facing = {"tensor": 1 - half}
@@ -630,7 +630,8 @@
             if n:
                 remote(home_send.at[r], home.at[r], b_send.at[r], b_recv.at[r], facing).wait_recv()
             grad = home[r].astype(F32) + add_ref[r].astype(F32)
-            x = tok_ref[r].astype(F32)
+            here = pl.ds(pl.multiple_of(half * part, part), part)
+            x = tok_ref[r, here, :].astype(F32)
             x = x - jnp.mean(x, -1, keepdims=True)
             scale = lax.rsqrt(jnp.mean(x * x, -1, keepdims=True) + EPSILON)
             x = x * scale
@@ -638,8 +639,9 @@
             norms[1:2, :] += jnp.sum(grad, 0, keepdims=True)
             grad = grad * gain_ref[...]
             grad = grad - jnp.mean(grad, -1, keepdims=True) - x * jnp.mean(grad * x, -1, keepdims=True)
-            own = cot_ref[r, pl.ds(pl.multiple_of(half * part, part), part), :]
-            grads[r] = (own.astype(F32) + scale * grad).astype(BF)
+            own = cot_ref[r, here, :].astype(F32)
+            norms[2:3, :] += jnp.sum(own, 0, keepdims=True)
+            grads[r] = (own + scale * grad).astype(BF)
             keep(r).start()
 
     lag = 2
@@ -657,7 +659,7 @@
 
     small[...] = extra_ref[...]
     lines = norms.shape[1] // LANES
-    for n in range(2):
+    for n in range(3):
         for k in range(lines):
             small[n * lines + k:n * lines + k + 1, :] = norms[n:n + 1, k * LANES:(k + 1) * LANES]
     shared = small.at[pl.ds(0, 3 * lines)]
@@ -754,7 +756,7 @@
 
 
 def go_home(g_mine, g_other, attended, weights, tokens, cot, add, gain, extra, waits=()):
-    rows, part, model = tokens.shape
+    rows, part, model = tokens.shape[0], tokens.shape[1] // 2, tokens.shape[2]
     blocks = lax.axis_size("blk")
     wide = sum(g.shape[1] for g in g_mine)
     dma = pltpu.SemaphoreType.DMA
@@ -840,8 +842,6 @@
         step, steps = pl.program_id(0), pl.num_programs(0)
         rows = RowTransfer(refs[0], *refs[moves + 5:])
         pl.when(step == 0)(rows.start)
-        for n in range(1, rows.blocks):
-            pl.when(step == jnp.minimum(n, steps - 1))(lambda: rows.onward(n))
     hid, cot = hid_ref[...], cot_ref[...]
 
     @pl.when(pl.program_id(0) == 0)
@@ -870,6 +870,8 @@
     res_ref[...] = res.astype(BF)
     back_ref[...] = back.astype(BF)
     if moves:
+        for n in range(1, rows.blocks):
+            pl.when(step == jnp.minimum(n, steps - 1))(lambda: rows.onward(n))
         pl.when(step == steps - 1)(rows.finish)
 
 
@@ -1032,7 +1034,7 @@
     bias = by_pair(b_qkv[None], width)
     own_tokens, own_cot = part_of(tokens, 1, mine), part_of(cotangent, 1, mine)
     grad_packed, grad_qkv, attended = [], [], []
-    waits = [grad_fc, own_tokens, own_cot]
+    waits = [grad_fc]
     for n, row_grad in enumerate(row_grads):
         out, grads = attention(
             row_hidden, weights, bias, n * (wide // LANES), row_grad, index - start, start,
@@ -1052,10 +1054,10 @@
     if pair:
         used = 3 * lines + bias_sums.shape[0]
         extra = jnp.zeros((8 * (model // shard.shape[0]), LANES), F32)
-        extra = extra.at[2 * lines:3 * lines].set(tensor_sums).at[3 * lines:used].set(bias_sums)
+        extra = extra.at[3 * lines:used].set(bias_sums)
         grad_tokens, sums, grad_out_sum, mixed, other_mixed = go_home(
             [g[0] for g in grad_packed], [g[1] for g in grad_packed],
-            [to_blocks(attended[0].reshape(blocks, group, wide), rows)] + attended[1:], weights, own_tokens, cotangent,
+            [to_blocks(attended[0].reshape(blocks, group, wide), rows)] + attended[1:], weights, tokens, cotangent,
             mlp_back, ln_gain[None], extra, [grad_qkv, grad_proj_sum, other_mlp, other_out],
         )
         norm_sums, bias_sums = sums[:3 * lines].reshape(3, model), sums[3 * lines:used].reshape(-1)

time: 599 us -> 593 us (0.990)
    unnamed x66 -> x62, local copies, waits for them, and re-layouts: 18.5 us -> 18.5 us
  transfers between devices with their start and end apart: 9 -> 9, of which waited for: 0 -> 0; matrix products, arithmetic and copies ran while one was open for 9% -> 8% of each run, Pallas kernels for 57% -> 57%
where the time goes in v7:
time: 593 us; the launch traced here: 587 us
  Pallas kernels  433 us (73%)
  starting transfers between devices  61.2 us (10%)
  local copies, waits for them, and re-layouts  39.1 us (7%)
  matrix products  24.6 us (4%)
  other arithmetic  14.5 us (2%)
  between operations  14.4 us (2%)
    pallas_call x1, Pallas kernels, go_home(): pl.pallas_call(functools.partial(tail_kernel, groups, len(waits)), grid=(...  166 us
    pallas_call x2, Pallas kernels, attention(): pl.pallas_call(functools.partial(attn_kernel, bq, bk, part, len(waits)),...  120 us
    pallas_call x1, Pallas kernels, gather_weights(): pl.pallas_call(gather_kernel, out_shape=[jax.ShapeDtypeStruct((cores * bl...  72.4 us
    all_to_all x2, starting transfers between devices, to_rows(): lax.all_to_all(jnp.concatenate([value, pad], 0), 'blk', 0, 0, tiled=True)  51 us
    pallas_call x1, Pallas kernels, mlp(): pl.pallas_call(functools.partial(mlp_kernel, tile, len(waits), len(moves)...  50.3 us
    pallas_call x1, Pallas kernels, weight_grads(): pl.pallas_call(functools.partial(weight_grad_kernel, half, len(waits)), g...  23.5 us
    unnamed x62, local copies, waits for them, and re-layouts  18.5 us
    dot_general x5, matrix products, dot(): return jnp.dot(a, b, preferred_element_type=F32)  14.4 us
  transfers between devices with their start and end apart: 9, of which 0 were waited for; matrix products, arithmetic and copies ran while one was open for 8% of the time, Pallas kernels for 57%

profile of v7, /device:TPU:28, one launch (start us, length us, event | category | flops | bytes accessed | tf_op | source)
XLA Modules:
  0.0 587.4 jit_solution(9638196001304459905)
XLA Ops:
  9.7 2.0 copy-done.5
  11.7 72.4 %shard_map.203 = (bf16[1024,6144]{1,0:T(8,128)(2,1)S(1)}, bf16[7,256,1024]{2,1,0:T(8,128)(2,1)S(1)}) custom-call(bf16[64,6144]{1,0:T(8,128)(2,1)S(1)} %pad_maximum_fusion.1.x_ref, bf16[7,256,1024]{2,1,0:T(8,128)(2,1)S(1)} %copy-done.5, f32[1,1024]{1,0:T(1,128)S(1)} %bitcast.75, f32[1,1024]{1,0:T(1,128)S(1)} %bitcast.76), custom_call_target="tpu_custom_call" | custom-call | tf_op jit(solution)/shard_map/pallas_call | solution.py:412
  84.2 1.8 copy-done.3
  86.0 4.5 copy-done.2
  90.5 3.4 fusion.4
  93.9 2.8 copy.50
  98.3 7.6 %all-to-all-start = ((bf16[8,256,256]{2,1,0:T(8,128)(2,1)}), bf16[8,256,256]{2,1,0:T(8,128)(2,1)S(1)}, u32[]{:S(2)}, u32[]{:S(2)}) async-start(bf16[8,256,256]{2,1,0:T(8,128)(2,1)} %concatenate.18), calls=%async_computation | async-start | bytes 2097152 | tf_op jit(solution)/shard_map/all_to_all | solution.py:949
  107.7 1.6 collective-permute-start.1
  109.3 50.3 %shard_map.204 = (bf16[1792,2048]{1,0:T(8,128)(2,1)}, bf16[1792,2048]{1,0:T(8,128)(2,1)}, bf16[1792,1024]{1,0:T(8,128)(2,1)}, bf16[1792,1024]{1,0:T(8,128)(2,1)}...) custom-call(bf16[1792,1024]{1,0:T(8,128)(2,1)} %bitcast.69, ...), custom_call_target="tpu_custom_call" | custom-call | flops 1000 | bytes 1000 | tf_op jit(solution)/shard_map/pallas_call | solution.py:894
  159.7 2.8 copy-done.4
  162.5 23.5 %shard_map.205 = (bf16[1024,2048]{1,0:T(8,128)(2,1)}, bf16[1024,2048]{1,0:T(8,128)(2,1)}) custom-call(bf16[1792,1024]{1,0:T(8,128)(2,1)S(1)} %bitcast.70, bf16[1792,1024]{1,0:T(8,128)(2,1)} %bitcast.78, bf16[2048,256]{1,0:T(8,128)(2,1)S(1)} %bitcast.72, bf16[1024,512]{1,0:T(8,128)(2,1)S(1)} %collective-permute-done.1.refs_1_.refs_9_, ...), custom_call_target="tpu_custom_call" | custom-call | flops 1000 | bytes 1000 | tf_op jit(solution)/shard_map/pallas_call | solution.py:819
  187.8 43.4 %all-to-all-start.1 = ((bf16[8,256,256]{2,1,0:T(8,128)(2,1)}), bf16[8,256,256]{2,1,0:T(8,128)(2,1)S(1)}, u32[]{:S(2)}, u32[]{:S(2)}) async-start(bf16[8,256,256]{2,1,0:T(8,128)(2,1)} %concatenate.19), calls=%async_computation.2 | async-start | bytes 2097152 | tf_op jit(solution)/shard_map/all_to_all | solution.py:949
  231.2 3.0 dynamic-slice_bitcast_fusion
  234.8 1.5 collective-permute-start
  239.3 60.1 %shard_map.206 = (bf16[2048,256]{1,0:T(8,128)(2,1)}, bf16[1024,768]{1,0:T(8,128)(2,1)}, bf16[1024,768]{1,0:T(8,128)(2,1)}) custom-call(s32[4]{0:T(128)} %get-tuple-element.68.lo_ref, s32[4]{0:T(128)} %get-tuple-element.67.hi_ref, bf16[1024,1024]{1,0:T(8,128)(2,1)} %get-tuple-element.48.refs_0_, bf16[1024,1024]{1,0:T(8,128)(2,1)} %get-tuple-element.49.refs_1_, ...), custom_call_target="tpu_custom_call" | custom-call | flops 1000 | bytes 1000 | tf_op jit(solution)/shard_map/pallas_call | solution.py:274
  299.4 3.5 fusion.11
  303.0 2.0 add_convert_fusion.1
  305.0 1.8 convert_element_type.89.refs_3_
  306.8 6.0 %all-to-all-start.2 = ((bf16[8,256,256]{2,1,0:T(8,128)(2,1)}), bf16[8,256,256]{2,1,0:T(8,128)(2,1)}, u32[]{:S(2)}, u32[]{:S(2)}) async-start(bf16[8,256,256]{2,1,0:T(8,128)(2,1)} %bitcast.17), calls=%async_computation.3 | async-start | bytes 2097152 | tf_op jit(solution)/shard_map/all_to_all | solution.py:953
  312.8 60.1 %shard_map.207 = (bf16[2048,256]{1,0:T(8,128)(2,1)}, bf16[1024,768]{1,0:T(8,128)(2,1)}, bf16[1024,768]{1,0:T(8,128)(2,1)}) custom-call(s32[4]{0:T(128)} %get-tuple-element.68.lo_ref, s32[4]{0:T(128)} %get-tuple-element.67.hi_ref, bf16[1024,1024]{1,0:T(8,128)(2,1)} %get-tuple-element.48.refs_0_, bf16[1024,1024]{1,0:T(8,128)(2,1)} %get-tuple-element.49.refs_1_, ...), custom_call_target="tpu_custom_call" | custom-call | flops 1000 | bytes 1000 | tf_op jit(solution)/shard_map/pallas_call | solution.py:274
  373.0 3.5 fusion.12
  376.5 2.0 add_convert_fusion
  378.5 1.9 pad_maximum_fusion.refs_6_
  380.4 1.4 copy-done.19
  382.8 4.3 fusion.3.refs_13_
  387.1 2.4 slice.69.refs_4_
  390.6 2.0 convert_bitcast_fusion
  392.7 166.4 %shard_map.208 = (bf16[7,256,1024]{2,1,0:T(8,128)(2,1)}, f32[128,128]{1,0:T(8,128)}, f32[64,512]{1,0:T(8,128)}, bf16[7,256,512]{2,1,0:T(8,128)(2,1)}, bf16[7,256,512]{2,1,0:T(8,128)(2,1)}) custom-call(bf16[1024,768]{1,0:T(8,128)(2,1)} %get-tuple-element.53.refs_0_, bf16[1024,768]{1,0:T(8,128)(2,1)} %get-tuple-element.55.refs_1_, ...), custom_call_target="tpu_custom_call" | custom-call | flops 1000 | bytes 1000 | tf_op jit(solution)/shard_map/pallas_call | solution.py:769
  561.7 1.3 slice_bitcast_fusion
  563.0 3.8 fusion.13
  566.8 6.4 %fusion.2 = bf16[1792,1024]{1,0:T(8,128)(2,1)} fusion(bf16[1792,1024]{1,0:T(8,128)(2,1)S(1)} %bitcast.71, f32[1792,1024]{1,0:T(8,128)S(1)} %fusion.13, bf16[1792,1024]{1,0:T(8,128)(2,1)} %collective-permute-done.refs_8_, bf16[1792,1024]{1,0:T(8,128)(2,1)} %get-tuple-element.47, bf16[1792,512]{1,0:T(8,128)(2,1)S(1)} %bitcast.96, f32[1024]{0:T(1024)S(1)} %copy-done.29, ...), kind=kOutput, calls=%fused_computation.3 | convolution fusion | flops 1895563264 | bytes 24907776 | tf_op jit(solution)/shard_map/dot_general | solution.py:20
  575.5 4.5 copy.67
  (100 shorter events, 18.9 us)
Async XLA Ops:
  7.2 229.1 %copy-start = (s32[7,5]{1,0:T(8,128)S(1)}, s32[7,5]{1,0:T(8,128)}, u32[]{:S(2)}) copy-start(s32[7,5]{1,0:T(8,128)} %param.24) | copy-start | bytes 424
  7.2 2.5 copy-start.10
  11.7 78.8 %copy-start.12 = (bf16[7,256,1024]{2,1,0:T(8,128)(2,1)S(1)}, bf16[7,256,1024]{2,1,0:T(8,128)(2,1)}, u32[]{:S(2)}) copy-start(bf16[7,256,1024]{2,1,0:T(8,128)(2,1)} %refs_12_.1) | copy-start | bytes 11010052
  86.0 4.5 copy-start.2
  98.3 61.4 %all-to-all-start = ((bf16[8,256,256]{2,1,0:T(8,128)(2,1)}), bf16[8,256,256]{2,1,0:T(8,128)(2,1)S(1)}, u32[]{:S(2)}, u32[]{:S(2)}) async-start(bf16[8,256,256]{2,1,0:T(8,128)(2,1)} %concatenate.18), calls=%async_computation | async-start | bytes 2097152 | tf_op jit(solution)/shard_map/all_to_all | solution.py:949
  105.9 199.1 %reduce-scatter.4.cloned.1.call-start = ((), (), s32[]{:S(2)}) async-start(), calls=%async_computation.6 | async-start | bytes 4456448 | tf_op jit(solution)/shard_map/reduce_scatter | solution.py:977
  107.7 51.9 %collective-permute-start.1 = (bf16[1024,512]{1,0:T(8,128)(2,1)S(1)}, bf16[1024,512]{1,0:T(8,128)(2,1)S(1)}, u32[]{:S(2)}, u32[]{:S(2)}) collective-permute-start(bf16[1024,512]{1,0:T(8,128)(2,1)S(1)} %slice.57), channel_id=1, source_target_pairs={{0,1},{1,0},{2,3},{3,2},{4,5},{5,4},{6,7},{7,6},{8,9},{9,8},{10,11... | collective-permute-start | bytes 3145736 | tf_op jit(solution)/shard_map/ppermute | solution.py:914
  159.7 26.3 %copy-start.8 = (bf16[1024,512]{1,0:T(8,128)(2,1)}, bf16[1024,512]{1,0:T(8,128)(2,1)S(1)}, u32[]{:S(2)}) copy-start(bf16[1024,512]{1,0:T(8,128)(2,1)S(1)} %collective-permute-done.1.refs_1_.refs_9_) | copy-start | bytes 3145732
  159.7 26.3 %copy-start.7 = (bf16[8,256,256]{2,1,0:T(8,128)(2,1)}, bf16[8,256,256]{2,1,0:T(8,128)(2,1)S(1)}, u32[]{:S(2)}) copy-start(bf16[8,256,256]{2,1,0:T(8,128)(2,1)S(1)} %all-to-all-done) | copy-start | bytes 3145732
  159.7 2.8 copy-start.4
  186.0 204.6 %reduce-scatter.6.cloned.1.call-start = ((), (), s32[]{:S(2)}) async-start(), calls=%async_computation.7 | async-start | bytes 4456448 | tf_op jit(solution)/shard_map/reduce_scatter | solution.py:977
  187.8 119.0 %all-to-all-start.1 = ((bf16[8,256,256]{2,1,0:T(8,128)(2,1)}), bf16[8,256,256]{2,1,0:T(8,128)(2,1)S(1)}, u32[]{:S(2)}, u32[]{:S(2)}) async-start(bf16[8,256,256]{2,1,0:T(8,128)(2,1)} %concatenate.19), calls=%async_computation.2 | async-start | bytes 2097152 | tf_op jit(solution)/shard_map/all_to_all | solution.py:949
  231.2 5.2 copy-start.26
  234.2 148.5 %collective-permute-start.2 = (bf16[7,128,1024]{2,1,0:T(8,128)(2,1)}, bf16[7,128,1024]{2,1,0:T(8,128)(2,1)}, u32[]{:S(2)}, u32[]{:S(2)}) collective-permute-start(bf16[7,128,1024]{2,1,0:T(8,128)(2,1)} %dynamic-slice_bitcast_fusion), channel_id=1, source_target_pairs={{0,1},{1,0},{2,3},{3,2},{4,5},{5,4},{6,7},{7,6},{8,9},{9,8},{10,11... | collective-permute-start | bytes 5505032 | tf_op jit(solution)/shard_map/ppermute | solution.py:914
  234.8 157.8 %collective-permute-start = (bf16[1792,1024]{1,0:T(8,128)(2,1)}, bf16[1792,1024]{1,0:T(8,128)(2,1)}, u32[]{:S(2)}, u32[]{:S(2)}) collective-permute-start(bf16[1792,1024]{1,0:T(8,128)(2,1)} %get-tuple-element.47), channel_id=1, source_target_pairs={{0,1},{1,0},{2,3},{3,2},{4,5},{5,4},{6,7},{7,6},{8,9},{9,8},{10,11... | collective-permute-start | bytes 11010056 | tf_op jit(solution)/shard_map/ppermute | solution.py:914
  239.3 60.1 %copy-start.14 = (bf16[1024,1024]{1,0:T(8,128)(2,1)S(1)}, bf16[1024,1024]{1,0:T(8,128)(2,1)}, u32[]{:S(2)}) copy-start(bf16[1024,1024]{1,0:T(8,128)(2,1)} %get-tuple-element.49.refs_1_) | copy-start | bytes 6291460
  299.4 3.5 copy-start.16
  299.4 3.5 copy-start.18
  306.8 6.0 %copy-start.24 = (bf16[8,256,256]{2,1,0:T(8,128)(2,1)}, bf16[8,256,256]{2,1,0:T(8,128)(2,1)S(1)}, u32[]{:S(2)}) copy-start(bf16[8,256,256]{2,1,0:T(8,128)(2,1)S(1)} %all-to-all-done.1) | copy-start | bytes 3145732
  306.8 80.3 %all-to-all-start.2 = ((bf16[8,256,256]{2,1,0:T(8,128)(2,1)}), bf16[8,256,256]{2,1,0:T(8,128)(2,1)}, u32[]{:S(2)}, u32[]{:S(2)}) async-start(bf16[8,256,256]{2,1,0:T(8,128)(2,1)} %bitcast.17), calls=%async_computation.3 | async-start | bytes 2097152 | tf_op jit(solution)/shard_map/all_to_all | solution.py:953
  312.8 260.4 %reduce-scatter.8.cloned.1.call-start = ((), (), s32[]{:S(2)}) async-start(), calls=%async_computation.8 | async-start | bytes 3342336 | tf_op jit(solution)/shard_map/reduce_scatter | solution.py:977
  312.8 60.1 %copy-start.17 = (bf16[1024,1024]{1,0:T(8,128)(2,1)S(1)}, bf16[1024,1024]{1,0:T(8,128)(2,1)}, u32[]{:S(2)}) copy-start(bf16[1024,1024]{1,0:T(8,128)(2,1)} %get-tuple-element.48.refs_0_) | copy-start | bytes 6291460
  372.9 3.5 copy-start.15
  373.0 3.5 copy-start.22
  382.8 6.7 %copy-start.23 = (bf16[1024,768]{1,0:T(8,128)(2,1)S(1)}, bf16[1024,768]{1,0:T(8,128)(2,1)}, u32[]{:S(2)}) copy-start(bf16[1024,768]{1,0:T(8,128)(2,1)} %get-tuple-element.57.refs_3_) | copy-start | bytes 4718596
  387.1 2.9 copy-start.27
  392.7 170.3 %copy-start.9 = (bf16[1024,512]{1,0:T(8,128)(2,1)S(1)}, bf16[1024,512]{1,0:T(8,128)(2,1)}, u32[]{:S(2)}) copy-start(bf16[1024,512]{1,0:T(8,128)(2,1)} %copy-done.8) | copy-start | bytes 3145732
  563.0 3.8 copy-start.6
  563.0 3.8 copy-start.28
  563.0 3.8 copy-start.29
  575.5 5.1 copy-start.1
  575.5 4.5 copy-start.25
  (7 other events, 13.6 us)
Sparse Core Ops, SparseCore 0:
  186.1 107.6 reduce-scatter.3
  298.1 72.8 reduce-scatter.5
  380.5 96.2 reduce-scatter.7
